TPU v7x, 32 devices: a whole 2x2x4 slice. The times are simulated.
32 devices in a mesh: ctx: 8 (over y, x, core), head: 4 (over z).
Axes of the slice: x: 2, y: 2, z: 4, core: 2. Of those that a mesh axis runs over, the one named last changes fastest.
Arguments:
- tokens: bfloat16 [8192, 4096], P('ctx', 'head'), may hold values from -23 to 23
- proj_weight: bfloat16 [4096, 32, 384], P(None, 'head'), may hold values from -1 to 1
- partner_shard: int32 [32, 128, 3], P('head'), may hold values from 0 to 7, all different within a row; in each aligned block of 16 rows (0 to 15, 16 to 31, ..., all dimensions but the last counted through in order) at most 12 rows name the same one
- partner_block: int32 [32, 128, 3], P('head'), may hold values from 0 to 15
Outputs:
- attended: bfloat16 [8192, 32, 128], P('ctx', 'head')
Inputs may be any that keep to these rules, and one draw needn't show every extreme that they name: `partner_shard`: the 3 entries of one row differ. For each head, within each aligned run of 16 block rows, no value is named more than 12 times, and some runs name one value exactly 12 times.
All inputs are finite; a program needn't handle non-finite values.
Results may differ from a plain program's by a relative error of at most 0.008.
Values may be sent and summed in bfloat16 or wider, within the bound.
No kernel may reach another device: no remote copies, remote signals or barrier semaphores. Data moves between devices by JAX's collectives and lax.ppermute only.
A program may use at most 192 MiB of HBM per device.

v0:
```python
import jax
import jax.numpy as jnp
from jax import lax
from jax.sharding import PartitionSpec as P

HEAD_DIMENSION = 128
BLK = 64
GLOB = 2
RAND = 3


def padded_2(cells, sides, width):
    for axis, dim in sides:
        count = lax.axis_size(axis)
        head = lax.slice_in_dim(cells, 0, width, axis=dim)
        tail = lax.slice_in_dim(cells, cells.shape[dim] - width, cells.shape[dim], axis=dim)
        cells = jnp.concatenate(
            [
                lax.ppermute(tail, axis, [(i, (i + 1) % count) for i in range(count)]),
                cells,
                lax.ppermute(head, axis, [((i + 1) % count, i) for i in range(count)]),
            ],
            axis=dim,
        )
    return cells


def from_root(block, axis, holder):
    block = jnp.where(lax.axis_index(axis) == holder, block, jnp.zeros_like(block))
    return lax.psum(block, axis)


def combined_all(part, axis, combine):
    gathered = jax.tree.map(lambda a: lax.all_gather(a, axis), part)

    def take(source):
        return jax.tree.map(lambda a: lax.dynamic_index_in_dim(a, source, 0, False), gathered)

    return lax.fori_loop(
        1, lax.axis_size(axis), lambda source, state: combine(state, take(source)), take(0)
    )


def per_device(tokens, proj_weight, partner_shard, partner_block):
    row_count = tokens.shape[0]
    head_count = proj_weight.shape[1]
    blocks = row_count // BLK
    shard_index = lax.axis_index("ctx")
    inverse_root_scale = HEAD_DIMENSION ** (-0.5)
    packed = jnp.einsum(
        "td,dhe->the",
        lax.all_gather(tokens, "head", axis=1, tiled=True),
        proj_weight,
        preferred_element_type=jnp.float32,
    ).astype(jnp.bfloat16)
    queries = packed[..., :HEAD_DIMENSION]
    keyval = packed[..., HEAD_DIMENSION:]
    padded = padded_2(keyval, (("ctx", 0),), BLK)
    window = jnp.concatenate(
        [
            padded[0:row_count].reshape(blocks, BLK, head_count, 2 * HEAD_DIMENSION),
            padded[BLK : row_count + BLK].reshape(blocks, BLK, head_count, 2 * HEAD_DIMENSION),
            padded[2 * BLK : row_count + 2 * BLK].reshape(
                blocks, BLK, head_count, 2 * HEAD_DIMENSION
            ),
        ],
        axis=1,
    )
    global_pack = from_root(packed[: GLOB * BLK], "ctx", 0)
    global_query = global_pack[..., :HEAD_DIMENSION]
    global_keyval = global_pack[..., HEAD_DIMENSION:]
    row_total = blocks * RAND
    owners = lax.dynamic_slice_in_dim(partner_shard, shard_index * blocks, blocks, 1).reshape(
        head_count, row_total
    )
    offsets = lax.dynamic_slice_in_dim(partner_block, shard_index * blocks, blocks, 1).reshape(
        head_count, row_total
    )
    partner_index = owners * blocks + offsets
    block_rows = lax.all_gather(keyval, "ctx", axis=0, tiled=True)
    piece_blocks = block_rows.shape[0] // BLK
    piece_hot = (partner_index[..., None] == jnp.arange(piece_blocks)).astype(jnp.bfloat16)
    blocked = block_rows.reshape(piece_blocks, BLK, head_count, 2 * HEAD_DIMENSION)
    fetched = jnp.einsum(
        "hrb,bthe->hrte", piece_hot, blocked, preferred_element_type=jnp.float32
    ).astype(jnp.bfloat16)
    remote = fetched
    remote = remote.reshape(head_count, blocks, RAND * BLK, 2 * HEAD_DIMENSION)
    blocked_query_rows = queries.reshape(blocks, BLK, head_count, HEAD_DIMENSION)
    window_scores = jnp.einsum(
        "bqhd,bkhd->bhqk",
        blocked_query_rows,
        window[..., :HEAD_DIMENSION],
        preferred_element_type=jnp.float32,
    )
    global_scores = jnp.einsum(
        "bqhd,khd->bhqk",
        blocked_query_rows,
        global_keyval[..., :HEAD_DIMENSION],
        preferred_element_type=jnp.float32,
    )
    remote_scores = jnp.einsum(
        "bqhd,hbkd->bhqk",
        blocked_query_rows,
        remote[..., :HEAD_DIMENSION],
        preferred_element_type=jnp.float32,
    )
    logit_scores = (
        jnp.concatenate([window_scores, global_scores, remote_scores], axis=-1) * inverse_root_scale
    )
    softmax_weight_matrix = jax.nn.softmax(logit_scores, axis=-1).astype(jnp.bfloat16)
    width_window = 3 * BLK
    width_global = GLOB * BLK
    context = jnp.einsum(
        "bhqk,bkhd->bqhd",
        softmax_weight_matrix[..., :width_window],
        window[..., HEAD_DIMENSION:],
        preferred_element_type=jnp.float32,
    )
    context = context + jnp.einsum(
        "bhqk,khd->bqhd",
        softmax_weight_matrix[..., width_window : width_window + width_global],
        global_keyval[..., HEAD_DIMENSION:],
        preferred_element_type=jnp.float32,
    )
    context = context + jnp.einsum(
        "bhqk,hbkd->bqhd",
        softmax_weight_matrix[..., width_window + width_global :],
        remote[..., HEAD_DIMENSION:],
        preferred_element_type=jnp.float32,
    )
    sparse_attention_output = context.astype(jnp.bfloat16).reshape(
        row_count, head_count, HEAD_DIMENSION
    )
    lead_scores = (
        jnp.einsum(
            "qhd,khd->hqk",
            global_query,
            keyval[..., :HEAD_DIMENSION],
            preferred_element_type=jnp.float32,
        )
        * inverse_root_scale
    )
    maxima = jnp.max(lead_scores, axis=-1)
    exp_terms = jnp.exp(lead_scores - maxima[..., None])
    totals = jnp.sum(exp_terms, axis=-1)
    summed = jnp.einsum(
        "hqk,khd->hqd",
        exp_terms,
        keyval[..., HEAD_DIMENSION:].astype(jnp.float32),
        precision=lax.Precision.HIGHEST,
    )

    def combine(first, second):
        max_first, total_first, sum_first = first
        max_second, total_second, sum_second = second
        larger = jnp.maximum(max_first, max_second)
        factor_first = jnp.exp(max_first - larger)
        factor_second = jnp.exp(max_second - larger)
        return (
            larger,
            total_first * factor_first + total_second * factor_second,
            sum_first * factor_first[..., None] + sum_second * factor_second[..., None],
        )

    maxima, totals, summed = combined_all((maxima, totals, summed), "ctx", combine)
    global_out = jnp.transpose((summed / totals[..., None]).astype(jnp.bfloat16), (1, 0, 2))
    head_rows = jnp.where(shard_index == 0, global_out, sparse_attention_output[: GLOB * BLK])
    return jnp.concatenate([head_rows, sparse_attention_output[GLOB * BLK :]], axis=0)


def solution(mesh):
    in_specs = (
        P("ctx", "head"),
        P(None, "head", None),
        P("head", None, None),
        P("head", None, None),
    )
    out_specs = P("ctx", "head", None)
    return jax.shard_map(
        per_device, mesh=mesh, in_specs=in_specs, out_specs=out_specs, check_vma=False
    )
```

profile of v0, /device:TPU:1, one launch (start us, length us, event | category | flops | bytes accessed | tf_op | source)
XLA Modules:
  0.0 605.0 jit_solution(16496929446723531965)
XLA Ops:
  6.5 0.7 all-gather.7.cloned.1.call-update
  7.3 0.0 all-reduce.2.cloned.1.call-start
  7.3 153.6 %all-gather.7.cloned.1.call-done = bf16[1024,4096]{1,0:T(8,128)(2,1)} async-done(((bf16[1024,1024]{1,0:T(8,128)(2,1)}), bf16[1024,4096]{1,0:T(8,128)(2,1)}) %all-gather.7.cloned.1.call-update) | async-done | bytes 8388624 | tf_op jit(solution)/shard_map/all_gather | solution.py:52
  160.9 32.4 %fusion.25 = bf16[1024,8,384]{2,0,1:T(8,128)(2,1)S(1)} fusion(bf16[4096,8,384]{2,1,0:T(8,128)(2,1)} %param.7, bf16[1024,4096]{1,0:T(8,128)(2,1)} %all-gather.7.cloned.1.call-done), kind=kOutput, calls=%fused_computation.38 | convolution fusion | flops 25772949504 | bytes 39845888 | tf_op jit(solution)/shard_map/td,dhe->the/dot_general | solution.py:50
  193.3 0.0 copy-start.4
  193.3 2.6 copy-done.4
  195.9 1.0 slice_select_fusion
  196.8 0.0 all-reduce.2.cloned.1.call-update
  196.8 0.0 all-gather.11.cloned.1.call-start
  196.9 52.6 %all-reduce.2.cloned.1.call-done = bf16[128,8,384]{2,0,1:T(8,128)(2,1)} async-done(((bf16[128,8,384]{2,0,1:T(8,128)(2,1)}), bf16[128,8,384]{2,0,1:T(8,128)(2,1)}) %all-reduce.2.cloned.1.call-update) | async-done | bytes 786448 | tf_op jit(solution)/shard_map/psum | solution.py:30
  249.5 2.5 multiply_reduce_fusion
  252.0 2.0 copy-done.1
  254.0 5.0 fusion.30
  259.0 0.0 all-gather.11.cloned.1.call-update
  259.0 0.0 copy-start.7
  259.0 0.0 copy-start.8
  259.1 0.0 all-gather.9.cloned.1.call-start
  259.1 4.4 slice.116
  263.5 0.0 all-gather.9.cloned.1.call-update
  263.5 1.1 fusion.57
  264.6 2.1 collective-permute-start
  266.7 0.2 collective-permute-start.1
  266.9 0.1 dynamic-slice_add_fusion
  267.0 0.1 copy.44
  267.1 0.1 copy.45
  267.1 2.0 slice.114
  269.2 6.9 %collective-permute-done = bf16[64,8,256]{2,0,1:T(8,128)(2,1)S(1)} collective-permute-done((bf16[64,8,256]{2,0,1:T(8,128)(2,1)S(1)}, bf16[64,8,256]{2,0,1:T(8,128)(2,1)S(1)}, u32[]{:S(2)}, u32[]{:S(2)}) %collective-permute-start) | collective-permute-done | bytes 262176 | tf_op jit(solution)/shard_map/ppermute | solution.py:19
  276.1 4.3 collective-permute-done.1
  280.4 0.6 pad_maximum_fusion.2
  281.0 10.0 %pad_maximum_fusion = bf16[16,192,8,256]{3,1,0,2:T(8,128)(2,1)S(1)} fusion(bf16[16,64,8,256]{3,1,0,2:T(8,128)(2,1)S(1)} %bitcast.70, bf16[16,64,8,256]{3,1,0,2:T(8,128)(2,1)S(1)} %bitcast.63, bf16[16,64,8,256]{3,1,0,2:T(8,128)(2,1)S(1)} %bitcast.69), kind=kLoop, calls=%fused_computation.16 | loop fusion | flops 37748736 | bytes 25165824 | tf_op jit(solution)/shard_map/concatenate | solution.py:59
  291.0 4.8 fusion.55
  295.8 7.3 %fusion.20 = f32[16,8,64,192]{3,2,1,0:T(8,128)} fusion(bf16[16,192,8,128]{3,1,0,2:T(8,128)(2,1)S(1)} %get-tuple-element.203, bf16[16,64,8,128]{3,1,0,2:T(8,128)(2,1)S(1)} %bitcast.66), kind=kOutput, calls=%fused_computation.27 | convolution fusion | flops 402653184 | bytes 14680064 | tf_op jit(solution)/shard_map/bqhd,bkhd->bhqk/dot_general | solution.py:90
  303.1 7.5 %all-gather = f32[64,128]{1,0:T(8,128)S(1)} all-gather(f32[8,128]{1,0:T(8,128)S(1)} %get-tuple-element.212), channel_id=2, replica_groups=mesh['ctx'=8,'head'=4] {'ctx'}, dimensions={0}, use_global_device_ids=true | all-gather | bytes 36864 | tf_op jit(solution)/shard_map/all_gather | solution.py:34
  310.6 0.9 fusion.31
  311.5 9.6 %all-gather.1 = f32[64,128]{1,0:T(8,128)S(1)} all-gather(f32[8,128]{1,0:T(8,128)S(1)} %fusion.31), channel_id=3, replica_groups=mesh['ctx'=8,'head'=4] {'ctx'}, dimensions={0}, use_global_device_ids=true | all-gather | bytes 36864 | tf_op jit(solution)/shard_map/all_gather | solution.py:34
  321.2 0.0 copy-done.6
  321.2 2.7 convolution_bitcast_fusion
  323.9 1.1 slice.113
  325.0 11.0 %while.19 = (s32[]{:T(128)}, f32[8,128]{1,0:T(8,128)S(1)}, f32[8,128]{1,0:T(8,128)S(1)}, f32[8,128,128]{2,1,0:T(8,128)S(1)}, f32[8,8,128]{2,1,0:T(8,128)S(1)}, /...) while((s32[]{:T(128)}, f32[8,128]{1,0:T(8,128)S(1)}, ...), condition=%wide.region_4.5_spmd, body=%wide.region_3.4_spmd.sunk | while | flops 399365 | bytes 1613975 | solution.py:39
  325.0 1.5 fusion.62
  326.6 1.5 fusion.62
  328.1 1.5 fusion.62
  329.7 1.5 fusion.62
  331.3 1.5 fusion.62
  332.8 1.5 fusion.62
  334.4 1.5 fusion.62
  335.9 0.1 copy.37
  336.0 127.4 %all-gather.9.cloned.1.call-done = bf16[8192,8,256]{2,0,1:T(8,128)(2,1)} async-done(((bf16[1024,8,256]{2,0,1:T(8,128)(2,1)}), bf16[8192,8,256]{2,0,1:T(8,128)(2,1)}) %all-gather.9.cloned.1.call-update) | async-done | bytes 33554448 | tf_op jit(solution)/shard_map/all_gather | solution.py:80
  463.4 32.8 %fusion.11 = bf16[8,48,64,256]{3,1,2,0:T(8,128)(2,1)S(1)} fusion(bf16[128,64,8,256]{3,1,0,2:T(8,128)(2,1)} %bitcast.65, s32[8,48]{1,0:T(8,128)S(1)} %copy.45), kind=kOutput, calls=%fused_computation.20 | convolution fusion | flops 1616953344 | bytes 46138880 | tf_op jit(solution)/shard_map/hrb,bthe->hrte/dot_general | solution.py:84
  496.2 10.8 %copy.47 = bf16[8,48,64,256]{3,2,1,0:T(8,128)(2,1)S(1)} copy(bf16[8,48,64,256]{3,1,2,0:T(8,128)(2,1)S(1)} %fusion.11) | data formatting | bytes 25165824 | tf_op jit(solution)/shard_map/convert_element_type | solution.py:86
  507.0 4.8 fusion.56
  511.8 7.3 %fusion.18 = f32[16,8,64,192]{3,2,1,0:T(8,128)} fusion(bf16[8,16,192,128]{3,2,1,0:T(8,128)(2,1)S(1)} %get-tuple-element.204, bf16[16,64,8,128]{3,1,0,2:T(8,128)(2,1)S(1)} %bitcast.68), kind=kOutput, calls=%fused_computation.25 | convolution fusion | flops 402653184 | bytes 14680064 | tf_op jit(solution)/shard_map/bqhd,hbkd->bhqk/dot_general | solution.py:102
  519.1 53.3 %fusion.58 = (f32[16,8,64]{2,1,0:T(8,128)S(1)}, f32[16,8,64,512]{3,2,1,0:T(8,128)}) fusion(f32[16,8,64,192]{3,2,1,0:T(8,128)} %fusion.18, f32[16,8,64,128]{3,2,1,0:T(8,128)} %convolution_bitcast_fusion, f32[16,8,64,192]{3,2,1,0:T(8,128)} %fusion.20), kind=kOutput, calls=%fused_computation.70 | output fusion | flops 20972032 | bytes 33587200 | tf_op jit(solution)/shard_map/sub | solution.py:111
  572.4 7.1 %divide_convert_fusion = bf16[16,8,64,512]{3,2,1,0:T(8,128)(2,1)S(1)} fusion(f32[16,8,64,512]{3,2,1,0:T(8,128)} %get-tuple-element.211, f32[16,8,64]{2,1,0:T(8,128)S(1)} %get-tuple-element.210), kind=kLoop, calls=%fused_computation.14 | loop fusion | flops 8388608 | bytes 25198592 | tf_op jit(solution)/shard_map/convert_element_type | solution.py:111
  579.5 0.6 copy-done.3
  580.0 4.4 fusion.14
  584.4 2.8 fusion.36
  587.2 0.4 copy-done.5
  587.6 6.7 %fusion.24 = bf16[16,64,8,128]{3,1,2,0:T(8,128)(2,1)S(1)} fusion(f32[16,8,128,64]{2,3,1,0:T(8,128)S(1)} %copy-done.5, f32[8,128,16,64]{1,3,0,2:T(8,128)} %fusion.36, bf16[16,192,8,128]{3,1,0,2:T(8,128)(2,1)} %get-tuple-element.202, bf16[16,8,64,512]{3,2,1,0:T(8,128)(2,1)S(1)} %divide_convert_fusion), kind=kOutput, calls=%fused_computation.34 | convolution fusion | flops 405798912 | bytes 20971520 | tf_op jit(solution)/shard_map/bhqk,bkhd->bqhd/dot_general | solution.py:114
  594.4 0.2 slice.128
  594.6 1.5 copy.52
  596.1 0.2 copy.51
  596.3 0.4 bitcast_select_fusion
  596.7 1.5 pad_maximum_fusion.3
  (23 shorter events, 0.2 us)
Async XLA Ops:
  6.5 154.4 %all-gather.7.cloned.1.call-start = ((), (), s32[]{:S(2)}) async-start(), calls=%async_computation | async-start | bytes 10485760 | tf_op jit(solution)/shard_map/all_gather | solution.py:52
  7.3 242.2 %all-reduce.2.cloned.1.call-start = ((), (), s32[]{:S(2)}) async-start(), calls=%async_computation.1 | async-start | bytes 1572864 | tf_op jit(solution)/shard_map/psum | solution.py:30
  193.3 2.6 copy-start.4
  196.8 127.0 %all-gather.11.cloned.1.call-start = ((), (), s32[]{:S(2)}) async-start(), calls=%async_computation.3 | async-start | bytes 4718592 | tf_op jit(solution)/shard_map/all_gather | solution.py:34
  252.0 2.0 copy-start.1
  259.0 7.8 %copy-start.7 = (s32[8,128,3]{1,0,2:T(8,128)S(1)}, s32[8,128,3]{1,0,2:T(8,128)}, u32[]{:S(2)}) copy-start(s32[8,128,3]{1,0,2:T(8,128)} %param.9) | copy-start | bytes 36868
  259.0 7.8 %copy-start.8 = (s32[8,128,3]{1,0,2:T(8,128)S(1)}, s32[8,128,3]{1,0,2:T(8,128)}, u32[]{:S(2)}) copy-start(s32[8,128,3]{1,0,2:T(8,128)} %param.8) | copy-start | bytes 36868
  259.1 204.3 %all-gather.9.cloned.1.call-start = ((), (), s32[]{:S(2)}) async-start(), calls=%async_computation.2 | async-start | bytes 37748736 | tf_op jit(solution)/shard_map/all_gather | solution.py:80
  264.6 11.5 %collective-permute-start = (bf16[64,8,256]{2,0,1:T(8,128)(2,1)S(1)}, bf16[64,8,256]{2,0,1:T(8,128)(2,1)S(1)}, u32[]{:S(2)}, u32[]{:S(2)}) collective-permute-start(bf16[64,8,256]{2,0,1:T(8,128)(2,1)S(1)} %get-tuple-element.206), channel_id=1, source_target_pairs={{0,4},{4,8},{8,12},{12,16},{16,20},{20,24},{24,28},{28,0},{1,5},{5... | collective-permute-start | bytes 786440 | tf_op jit(solution)/shard_map/ppermute | solution.py:19
  266.7 13.8 %collective-permute-start.1 = (bf16[64,8,256]{2,0,1:T(8,128)(2,1)S(1)}, bf16[64,8,256]{2,0,1:T(8,128)(2,1)S(1)}, u32[]{:S(2)}, u32[]{:S(2)}) collective-permute-start(bf16[64,8,256]{2,0,1:T(8,128)(2,1)S(1)} %get-tuple-element.207), channel_id=1, source_target_pairs={{4,0},{8,4},{12,8},{16,12},{20,16},{24,20},{28,24},{0,28},{5,1},{9... | collective-permute-start | bytes 786440 | tf_op jit(solution)/shard_map/ppermute | solution.py:21
  267.1 13.3 %copy-start = (bf16[1024,8,256]{2,0,1:T(8,128)(2,1)S(1)}, bf16[1024,8,256]{2,0,1:T(8,128)(2,1)}, u32[]{:S(2)}) copy-start(bf16[1024,8,256]{2,0,1:T(8,128)(2,1)} %slice.116) | copy-start | bytes 12582916
  295.8 14.8 %copy-start.2 = (f32[8,128,1024]{2,1,0:T(8,128)S(1)}, f32[8,128,1024]{2,1,0:T(8,128)}, u32[]{:S(2)}) copy-start(f32[8,128,1024]{2,1,0:T(8,128)} %copy-done.1) | copy-start | bytes 12582916
  295.8 25.4 %copy-start.6 = (bf16[128,8,384]{2,0,1:T(8,128)(2,1)S(1)}, bf16[128,8,384]{2,0,1:T(8,128)(2,1)}, u32[]{:S(2)}) copy-start(bf16[128,8,384]{2,0,1:T(8,128)(2,1)} %all-reduce.2.cloned.1.call-done) | copy-start | bytes 2359300
  572.4 7.6 %copy-start.3 = (bf16[8,16,192,128]{3,2,1,0:T(8,128)(2,1)S(1)}, bf16[8,16,192,128]{3,2,1,0:T(8,128)(2,1)}, u32[]{:S(2)}) copy-start(bf16[8,16,192,128]{3,2,1,0:T(8,128)(2,1)} %get-tuple-element.205) | copy-start | bytes 18874372
  584.4 3.2 copy-start.5
Sparse Core Ops, SparseCore 0:
  8.9 151.9 all-gather.6
  197.0 52.4 all-reduce.1
  259.2 41.6 all-gather.10
  302.6 160.7 all-gather.8
where the time goes:
time: 614 us; the launch traced here: 605 us
  waiting for transfers between devices  346 us (56%)
  matrix products  104 us (17%)
  other arithmetic  85.5 us (14%)
  local copies, waits for them, and re-layouts  36.8 us (6%)
  blocking collectives  17.1 us (3%)
  between operations  13.6 us (2%)
    all_gather x1, waiting for transfers between devices, per_device(): lax.all_gather(tokens, 'head', axis=1, tiled=True)  154 us
    all_gather x1, waiting for transfers between devices, per_device(): block_rows = lax.all_gather(keyval, 'ctx', axis=0, tiled=True)  127 us
    sub x1, other arithmetic, per_device(): jax.nn.softmax(logit_scores, axis=-1).astype(jnp.bfloat16)  53.3 us
    psum x1, waiting for transfers between devices, from_root(): return lax.psum(block, axis)  52.6 us
    dot_general x1, matrix products, per_device(): jnp.einsum('hrb,bthe->hrte', piece_hot, blocked, preferred_element_type=j...  32.8 us
    dot_general x1, matrix products, per_device(): jnp.einsum('td,dhe->the', lax.all_gather(tokens, 'head', axis=1, tiled=Tr...  32.4 us
    all_gather x2, blocking collectives, combined_all(): gathered = jax.tree.map(lambda a: lax.all_gather(a, axis), part)  17.1 us
  transfers between devices with their start and end apart: 6, of which 5 were waited for; matrix products, arithmetic and copies ran while one was open for 8% of the time, Pallas kernels for 0%

commit v1 on v0

v1 whole, which is shorter than its diff:
```python
import functools

import jax
import jax.numpy as jnp
from jax import lax
from jax.experimental import pallas as pl
from jax.experimental.pallas import tpu as pltpu
from jax.sharding import PartitionSpec as P

HEAD_DIMENSION = 128
BLK = 64
GLOB = 2
RAND = 3
KEY_SET = 3 + GLOB + RAND
LEAD = GLOB * BLK
EXPONENT = HEAD_DIMENSION ** (-0.5) * 1.4426950408889634
PARTS = (4, 4, 4, 4)
TOGETHER = 8
TRANSPOSED = (((1,), (1,)), ((), ()))


def project_kernel(x_ref, w_ref, *refs):
    q_ref, kv_ref = refs[-2:]
    out = jnp.dot(x_ref[...], w_ref[...], preferred_element_type=jnp.float32).astype(jnp.bfloat16)
    for i in range(out.shape[1] // (3 * HEAD_DIMENSION)):
        at = i * 3 * HEAD_DIMENSION
        q_ref[:, i * HEAD_DIMENSION : (i + 1) * HEAD_DIMENSION] = out[:, at : at + HEAD_DIMENSION]
        kv_ref[:, 2 * i * HEAD_DIMENSION : 2 * (i + 1) * HEAD_DIMENSION] = out[
            :, at + HEAD_DIMENSION : at + 3 * HEAD_DIMENSION
        ]


def project(x, weight, queries, start, total, after):
    rows, depth = x.shape
    heads = weight.shape[1] // (3 * HEAD_DIMENSION)
    per = 2
    at = start // rows
    assert at * rows == start
    given = () if queries is None else (queries,)
    return pl.pallas_call(
        project_kernel,
        grid=(heads // per,),
        in_specs=[
            pl.BlockSpec((rows, depth), lambda i: (0, 0)),
            pl.BlockSpec((depth, per * 3 * HEAD_DIMENSION), lambda i: (0, i)),
        ]
        + [pl.BlockSpec(memory_space=pltpu.HBM)] * (len(given) + len(after)),
        out_specs=[
            pl.BlockSpec((rows, per * HEAD_DIMENSION), lambda i: (at, i)),
            pl.BlockSpec((rows, per * 2 * HEAD_DIMENSION), lambda i: (0, i)),
        ],
        out_shape=[
            jax.ShapeDtypeStruct((total, heads * HEAD_DIMENSION), jnp.bfloat16),
            jax.ShapeDtypeStruct((rows, heads * 2 * HEAD_DIMENSION), jnp.bfloat16),
        ],
        input_output_aliases={2: 0} if given else {},
        compiler_params=pltpu.CompilerParams(vmem_limit_bytes=40 << 20),
    )(x, weight, *given, *after)


def column_copies(sources, places, head, target, sem):
    at = pl.multiple_of(head * 2 * HEAD_DIMENSION, 2 * HEAD_DIMENSION)
    return [
        pltpu.make_async_copy(
            ref.at[:, pl.ds(at, 2 * HEAD_DIMENSION)], target.at[pl.ds(place, ref.shape[0]), :], sem
        )
        for ref, place in zip(sources, places)
    ]


def sparse_kernel(places, heads, blocks, at_ref, q_ref, *refs):
    sources, (o_ref, held, sem) = refs[: len(places)], refs[len(places) :]
    head = pl.program_id(0)
    slot = lax.rem(head, 2)

    def copies(which, into):
        return column_copies(sources, places, which, held.at[into], sem.at[into])

    @pl.when(head == 0)
    def _():
        for copy in copies(head, slot):
            copy.start()

    @pl.when(head + 1 < heads)
    def _():
        for copy in copies(head + 1, 1 - slot):
            copy.start()

    for copy in copies(head, slot):
        copy.wait()

    def step(group, carry):
        rows, keys, scores, weights, totals = [], [], [], [], []
        for i in range(TOGETHER):
            block = group * TOGETHER + i
            rows.append(pl.ds(pl.multiple_of(block * BLK, BLK), BLK))
            keys.append(
                jnp.concatenate(
                    [
                        held[
                            slot,
                            pl.ds(
                                pl.multiple_of(
                                    at_ref[(head * blocks + block) * KEY_SET + j], BLK
                                ),
                                BLK,
                            ),
                            :,
                        ]
                        for j in range(KEY_SET)
                    ],
                    axis=0,
                )
            )
        for i in range(TOGETHER):
            scores.append(
                lax.dot_general(
                    q_ref[rows[i], :],
                    keys[i][:, :HEAD_DIMENSION],
                    TRANSPOSED,
                    preferred_element_type=jnp.float32,
                )
            )
        for i in range(TOGETHER):
            largest = jnp.max(scores[i], axis=-1, keepdims=True)
            weight = jnp.exp2((scores[i] - largest) * EXPONENT)
            totals.append(jnp.sum(weight, axis=-1, keepdims=True))
            weights.append(weight.astype(jnp.bfloat16))
        for i in range(TOGETHER):
            out = jnp.dot(
                weights[i], keys[i][:, HEAD_DIMENSION:], preferred_element_type=jnp.float32
            )
            o_ref[rows[i], :] = (out / totals[i]).astype(jnp.bfloat16)
        return carry

    lax.fori_loop(0, blocks // TOGETHER, step, 0)


def sparse(at, queries, sources, places, span):
    rows, width = queries.shape
    heads = width // HEAD_DIMENSION
    return pl.pallas_call(
        functools.partial(sparse_kernel, places, heads, rows // BLK),
        grid_spec=pltpu.PrefetchScalarGridSpec(
            num_scalar_prefetch=1,
            grid=(heads,),
            in_specs=[pl.BlockSpec((rows, HEAD_DIMENSION), lambda i, s: (0, i))]
            + [pl.BlockSpec(memory_space=pltpu.HBM)] * len(sources),
            out_specs=pl.BlockSpec((rows, HEAD_DIMENSION), lambda i, s: (0, i)),
            scratch_shapes=[
                pltpu.VMEM((2, span, 2 * HEAD_DIMENSION), jnp.bfloat16),
                pltpu.SemaphoreType.DMA((2,)),
            ],
        ),
        out_shape=jax.ShapeDtypeStruct(queries.shape, jnp.bfloat16),
        compiler_params=pltpu.CompilerParams(vmem_limit_bytes=48 << 20),
    )(at, queries, *sources)


def lead_kernel(places, step, head_ref, q_ref, *refs):
    sources, (o_ref, held, scores, sem) = refs[: len(places)], refs[len(places) :]
    copies = column_copies(sources, places, head_ref[0], held, sem.at[0])
    for copy in copies:
        copy.start()
    for copy in copies:
        copy.wait()
    q = q_ref[...]
    spans = [pl.ds(i, step) for i in range(0, held.shape[0], step)]
    for span in spans:
        scores[:, span] = lax.dot_general(
            q, held[span, :HEAD_DIMENSION], TRANSPOSED, preferred_element_type=jnp.float32
        )
    largest = jnp.max(scores[...], axis=-1, keepdims=True)
    total = jnp.zeros_like(largest)
    out = jnp.zeros(o_ref.shape, jnp.float32)
    for span in spans:
        weight = jnp.exp2((scores[:, span] - largest) * EXPONENT)
        total += jnp.sum(weight, axis=-1, keepdims=True)
        out += jnp.dot(
            weight.astype(jnp.bfloat16),
            held[span, HEAD_DIMENSION:],
            preferred_element_type=jnp.float32,
        )
    o_ref[...] = (out / total).astype(jnp.bfloat16)


def lead(head, queries, sources, places, span):
    return pl.pallas_call(
        functools.partial(lead_kernel, places, 1024),
        grid_spec=pltpu.PrefetchScalarGridSpec(
            num_scalar_prefetch=1,
            grid=(1,),
            in_specs=[pl.BlockSpec(queries.shape, lambda i, s: (0, 0))]
            + [pl.BlockSpec(memory_space=pltpu.HBM)] * len(sources),
            out_specs=pl.BlockSpec(queries.shape, lambda i, s: (0, 0)),
            scratch_shapes=[
                pltpu.VMEM((span, 2 * HEAD_DIMENSION), jnp.bfloat16),
                pltpu.VMEM((queries.shape[0], span), jnp.float32),
                pltpu.SemaphoreType.DMA((1,)),
            ],
        ),
        out_shape=jax.ShapeDtypeStruct(queries.shape, jnp.bfloat16),
        compiler_params=pltpu.CompilerParams(vmem_limit_bytes=48 << 20),
    )(head, queries, *sources)


def crossed(cells, bit, count):
    return lax.ppermute(cells, "ctx", [(i, i ^ bit) for i in range(count)])


def spread(own, count, turned):
    bits = [1 << i for i in range(1, count.bit_length() - 1)]
    held = {0: own}
    for bit in (bits[::-1] if turned else bits) + [1]:
        held.update({run ^ bit: crossed(cells, bit, count) for run, cells in list(held.items())})
    return held


def awaited(parts):
    near = [parts[-1][run] for run in (2, 4) if run in parts[-1]] if parts else []
    return near + ([cells for run, cells in parts[-2].items() if run] if len(parts) > 1 else [])


def from_first(cells, count):
    me = lax.axis_index("ctx")
    knows = [0]
    for bit in [1 << i for i in range(1, count.bit_length() - 1)] + [1]:
        got = lax.ppermute(cells, "ctx", [(i, i ^ bit) for i in knows])
        cells = jnp.where((me & bit) != 0, got, cells)
        knows = knows + [i ^ bit for i in knows]
    return cells


def per_device(tokens, proj_weight, partner_shard, partner_block):
    rows = tokens.shape[0]
    depth, heads, _ = proj_weight.shape
    blocks = rows // BLK
    count = lax.axis_size("ctx")
    me = lax.axis_index("ctx")
    span = rows * count
    weight = proj_weight.reshape(depth, heads * 3 * HEAD_DIMENSION)

    mine = me * blocks + jnp.arange(blocks)
    near = (mine[:, None] + jnp.array([-1, 0, 1])) % (count * blocks)
    fixed = jnp.concatenate(
        [near, jnp.broadcast_to(jnp.arange(GLOB)[None], (blocks, GLOB))], axis=1
    )
    partners = lax.dynamic_slice_in_dim(partner_shard * blocks + partner_block, me * blocks, blocks, 1)
    key_set = jnp.concatenate(
        [jnp.broadcast_to(fixed[None], (heads, blocks, 3 + GLOB)), partners], axis=2
    ).astype(jnp.int32)
    at = (((key_set // blocks) ^ me) * rows + (key_set % blocks) * BLK).astype(jnp.int32)

    sources, places = [], []
    queries, start = None, 0
    parts = []
    for part, share in enumerate(PARTS):
        size = rows * share // sum(PARTS)
        x = lax.all_gather(
            lax.slice_in_dim(tokens, start, start + size), "head", axis=1, tiled=True
        )
        queries, keyval = project(
            x, weight, queries, start, rows, awaited(parts)
        )
        if part == 0:
            lead_queries = from_first(queries[:LEAD], count)
        parts.append(spread(keyval, count, part % 2 == 1))
        for run, cells in parts[-1].items():
            sources.append(cells)
            places.append(run * rows + start)
        start += size

    share = heads * LEAD // count
    head = (me * share) // LEAD
    mine = lax.dynamic_slice(
        lead_queries, ((me * share) % LEAD, head * HEAD_DIMENSION), (share, HEAD_DIMENSION)
    )
    lead_out = lead(head.astype(jnp.int32).reshape(1), mine, sources, places, span)
    lead_out = lax.all_gather(lead_out, "ctx", axis=0, tiled=True)
    lead_out = jnp.transpose(lead_out.reshape(heads, LEAD, HEAD_DIMENSION), (1, 0, 2))
    out = sparse(at.reshape(-1), queries, sources, places, span)
    out = out.reshape(rows, heads, HEAD_DIMENSION)
    first = jnp.where(me == 0, lead_out, out[:LEAD])
    return jnp.concatenate([first, out[LEAD:]], axis=0)


def solution(mesh):
    in_specs = (
        P("ctx", "head"),
        P(None, "head", None),
        P("head", None, None),
        P("head", None, None),
    )
    out_specs = P("ctx", "head", None)
    return jax.shard_map(
        per_device, mesh=mesh, in_specs=in_specs, out_specs=out_specs, check_vma=False
    )
```

time: 614 us -> 327 us (0.53); the launches traced: 605 us -> 325 us
  waiting for transfers between devices: 346 us -> 103 us
  matrix products: 104 us -> 0 us
  other arithmetic: 85.5 us -> 2.86 us
  starting transfers between devices: 2.38 us -> 82.2 us
  Pallas kernels: 0 us -> 74.9 us
  blocking collectives: 17.1 us -> 10.5 us
    all_gather x3 -> x4, waiting for transfers between devices: 281 us -> 55.7 us  [per_device(): lax.all_gather(lax.slice_in_dim(tokens, start, start + size), 'head', axi...]
    dot_general x10 -> x0, matrix products: 104 us -> none  [the longest x1 32.8 us: per_device(): jnp.einsum('hrb,bthe->hrte', piece_hot, blocked, preferred_element_type=j...]
    ppermute x2 -> x31, starting transfers between devices: 2.25 us -> 82 us  [the longest x28 78.5 us: crossed(): return lax.ppermute(cells, 'ctx', [(i, i ^ bit) for i in range(count)])]
    pallas_call x0 -> x6, Pallas kernels: none -> 74.9 us  [the longest x4 51.1 us: project(): pl.pallas_call(project_kernel, grid=(heads // per,), in_specs=[pl.BlockSp...]
    sub x1 -> x0, other arithmetic: 53.3 us -> none  [per_device(): jax.nn.softmax(logit_scores, axis=-1).astype(jnp.bfloat16)]
    psum x1 -> x0, waiting for transfers between devices: 52.6 us -> none  [from_root(): return lax.psum(block, axis)]
    ppermute x2 -> x31, waiting for transfers between devices: 11.2 us -> 46 us  [the longest x28 46 us: crossed(): return lax.ppermute(cells, 'ctx', [(i, i ^ bit) for i in range(count)])]
    unnamed x18 -> x35, local copies, waits for them, and re-layouts: 5.61 us -> 35.5 us
  transfers between devices with their start and end apart: 6 -> 35, of which waited for: 5 -> 10; matrix products, arithmetic and copies ran while one was open for 8% -> 8% of each run, Pallas kernels for 0% -> 16%
where the time goes in v1:
time: 327 us; the launch traced here: 325 us
  waiting for transfers between devices  103 us (31%)
  starting transfers between devices  82.2 us (25%)
  Pallas kernels  74.9 us (23%)
  local copies, waits for them, and re-layouts  38.6 us (12%)
  between operations  13.4 us (4%)
  blocking collectives  10.5 us (3%)
    ppermute x28, starting transfers between devices, crossed(): return lax.ppermute(cells, 'ctx', [(i, i ^ bit) for i in range(count)])  78.5 us
    all_gather x4, waiting for transfers between devices, per_device(): lax.all_gather(lax.slice_in_dim(tokens, start, start + size), 'head', axi...  55.7 us
    pallas_call x4, Pallas kernels, project(): pl.pallas_call(project_kernel, grid=(heads // per,), in_specs=[pl.BlockSp...  51.1 us
    ppermute x28, waiting for transfers between devices, crossed(): return lax.ppermute(cells, 'ctx', [(i, i ^ bit) for i in range(count)])  46 us
    unnamed x35, local copies, waits for them, and re-layouts  35.5 us
    pallas_call x1, Pallas kernels, sparse(): pl.pallas_call(functools.partial(sparse_kernel, places, heads, rows // BL...  19.5 us
    all_gather x1, blocking collectives, per_device(): lead_out = lax.all_gather(lead_out, 'ctx', axis=0, tiled=True)  10.5 us
  transfers between devices with their start and end apart: 35, of which 10 were waited for; matrix products, arithmetic and copies ran while one was open for 8% of the time, Pallas kernels for 16%

profile of v1, /device:TPU:1, one launch (start us, length us, event | category | flops | bytes accessed | tf_op | source)
XLA Modules:
  0.0 325.5 jit_solution(12783938145526225932)
XLA Ops:
  6.5 2.9 fusion.9
  9.5 0.7 all-gather.7.cloned.1.call-update
  10.2 0.7 all-gather.9.cloned.1.call-update
  11.0 23.4 %copy.13 = bf16[512,8,8,384]{3,1,2,0:T(8,128)(2,1)} copy(bf16[512,8,8,384]{3,2,1,0:T(8,128)(2,1)} %bitcast.17) | data formatting | bytes 50331648
  34.4 23.2 %all-gather.5.cloned.1.call-done.x_ref = bf16[256,4096]{1,0:T(8,128)(2,1)} async-done(((bf16[256,1024]{1,0:T(8,128)(2,1)}), bf16[256,4096]{1,0:T(8,128)(2,1)}) %all-gather.5.cloned.1.call-update) | async-done | bytes 2097168 | tf_op jit(solution)/shard_map/all_gather | solution.py:259
  57.6 1.6 copy-done.5
  59.2 12.6 %shard_map.55 = (bf16[1024,1024]{1,0:T(8,128)(2,1)S(1)}, bf16[256,2048]{1,0:T(8,128)(2,1)}) custom-call(bf16[256,4096]{1,0:T(8,128)(2,1)S(1)} %copy-done.5, bf16[4096,3072]{1,0:T(8,128)(2,1)} %bitcast.13), custom_call_target="tpu_custom_call" | custom-call | tf_op jit(solution)/shard_map/pallas_call | solution.py:40
  71.8 1.2 collective-permute-start.3
  73.0 1.2 collective-permute-start.4
  74.2 1.4 collective-permute-start
  75.6 3.1 collective-permute-start.6
  78.8 17.4 %collective-permute-done.3.refs_1_.refs_3_ = bf16[256,2048]{1,0:T(8,128)(2,1)S(1)} collective-permute-done((bf16[256,2048]{1,0:T(8,128)(2,1)}, bf16[256,2048]{1,0:T(8,128)(2,1)S(1)}, u32[]{:S(2)}, u32[]{:S(2)}) %collective-permute-start.3) | collective-permute-done | bytes 1048608 | tf_op jit(solution)/shard_map/ppermute | solution.py:208
  96.2 1.1 collective-permute-start.5
  97.3 6.5 %all-gather.7.cloned.1.call-done.x_ref = bf16[256,4096]{1,0:T(8,128)(2,1)} async-done(((bf16[256,1024]{1,0:T(8,128)(2,1)}), bf16[256,4096]{1,0:T(8,128)(2,1)}) %all-gather.7.cloned.1.call-update) | async-done | bytes 2097168 | tf_op jit(solution)/shard_map/all_gather | solution.py:259
  103.8 1.6 copy-done.6
  105.4 12.6 %shard_map.56 = (bf16[1024,1024]{1,0:T(8,128)(2,1)S(1)}, bf16[256,2048]{1,0:T(8,128)(2,1)}) custom-call(bf16[256,4096]{1,0:T(8,128)(2,1)S(1)} %copy-done.6, bf16[4096,3072]{1,0:T(8,128)(2,1)} %bitcast.14, bf16[1024,1024]{1,0:T(8,128)(2,1)S(1)} %get-tuple-element.13.refs_0_, ...), custom_call_target="tpu_custom_call", output_to_operand_aliasing={{0}: (2, {})} | custom-call | tf_op jit(solution)/shard_map/pallas_call | solution.py:40
  118.0 1.2 collective-permute-start.10
  119.3 1.2 collective-permute-start.11
  120.5 1.2 collective-permute-start.7
  121.7 0.5 collective-permute-start.9
  122.2 21.0 %collective-permute-done.10.refs_2_.refs_3_.refs_9_ = bf16[256,2048]{1,0:T(8,128)(2,1)} collective-permute-done((bf16[256,2048]{1,0:T(8,128)(2,1)}, bf16[256,2048]{1,0:T(8,128)(2,1)}, u32[]{:S(2)}, u32[]{:S(2)}) %collective-permute-start.10) | collective-permute-done | bytes 1048608 | tf_op jit(solution)/shard_map/ppermute | solution.py:208
  143.3 1.1 collective-permute-start.13
  144.3 1.1 collective-permute-start.12
  145.5 1.0 copy-done.1
  146.4 1.1 collective-permute-start.14
  147.6 1.0 copy-done.3
  148.6 1.4 all-gather.9.cloned.1.call-done.x_ref
  150.0 1.2 copy-done.2
  151.2 1.2 copy-done.4
  152.4 13.0 %shard_map.57 = (bf16[1024,1024]{1,0:T(8,128)(2,1)S(1)}, bf16[256,2048]{1,0:T(8,128)(2,1)}) custom-call(bf16[256,4096]{1,0:T(8,128)(2,1)} %all-gather.9.cloned.1.call-done.x_ref, bf16[4096,3072]{1,0:T(8,128)(2,1)} %bitcast.15, bf16[1024,1024]{1,0:T(8,128)(2,1)S(1)} %get-tuple-element.16.refs_0_, ...), custom_call_target="tpu_custom_call", output_to_operand_aliasing={{0}: (2, {})} | custom-call | tf_op jit(solution)/shard_map/pallas_call | solution.py:40
  165.5 1.2 collective-permute-start.17
  166.7 1.2 collective-permute-start.18
  167.9 0.6 collective-permute-done.12.refs_5_.refs_11_
  168.5 3.0 collective-permute-start.16
  171.5 24.6 %all-gather.11.cloned.1.call-done.x_ref = bf16[256,4096]{1,0:T(8,128)(2,1)} async-done(((bf16[256,1024]{1,0:T(8,128)(2,1)}), bf16[256,4096]{1,0:T(8,128)(2,1)}) %all-gather.11.cloned.1.call-update) | async-done | bytes 2097168 | tf_op jit(solution)/shard_map/all_gather | solution.py:259
  196.2 12.8 %shard_map.58 = (bf16[1024,1024]{1,0:T(8,128)(2,1)S(1)}, bf16[256,2048]{1,0:T(8,128)(2,1)}) custom-call(bf16[256,4096]{1,0:T(8,128)(2,1)} %all-gather.11.cloned.1.call-done.x_ref, bf16[4096,3072]{1,0:T(8,128)(2,1)} %bitcast.16, bf16[1024,1024]{1,0:T(8,128)(2,1)S(1)} %get-tuple-element.18.refs_0_, ...), custom_call_target="tpu_custom_call", output_to_operand_aliasing={{0}: (2, {})} | custom-call | tf_op jit(solution)/shard_map/pallas_call | solution.py:40
  209.0 1.3 copy-done
  210.3 1.2 collective-permute-start.24
  211.5 0.7 collective-permute-start.1
  212.2 1.5 collective-permute-start.2
  213.7 1.2 collective-permute-start.25
  214.9 26.0 %collective-permute-start.27 = (bf16[256,2048]{1,0:T(8,128)(2,1)}, bf16[256,2048]{1,0:T(8,128)(2,1)S(1)}, u32[]{:S(2)}, u32[]{:S(2)}) collective-permute-start(bf16[256,2048]{1,0:T(8,128)(2,1)} %get-tuple-element.19.refs_24_), channel_id=1, source_target_pairs={{0,4},{4,0},{8,12},{12,8},{16,20},{20,16},{24,28},{28,24},{1,5},{5... | collective-permute-start | bytes 3145736 | tf_op jit(solution)/shard_map/ppermute | solution.py:208
  240.9 2.2 collective-permute-start.19
  243.1 0.3 collective-permute-start.21
  243.4 0.6 collective-permute-start.26
  244.1 18.3 %collective-permute-start.22 = (bf16[256,2048]{1,0:T(8,128)(2,1)}, bf16[256,2048]{1,0:T(8,128)(2,1)}, u32[]{:S(2)}, u32[]{:S(2)}) collective-permute-start(bf16[256,2048]{1,0:T(8,128)(2,1)} %collective-permute-done.18.refs_2_.refs_18_), channel_id=1, source_target_pairs={{0,4},{4,0},{8,12},{12,8},{16,20},{20,16},{24,28},{28,24},{1,5},{5... | collective-permute-start | bytes 3145736 | tf_op jit(solution)/shard_map/ppermute | solution.py:208
  262.5 4.5 %collective-permute-done.19.refs_19_ = bf16[256,2048]{1,0:T(8,128)(2,1)} collective-permute-done((bf16[256,2048]{1,0:T(8,128)(2,1)}, bf16[256,2048]{1,0:T(8,128)(2,1)}, u32[]{:S(2)}, u32[]{:S(2)}) %collective-permute-start.19) | collective-permute-done | bytes 1048608 | tf_op jit(solution)/shard_map/ppermute | solution.py:208
  267.0 0.6 collective-permute-start.29
  267.6 1.1 collective-permute-done.26.refs_27_
  268.8 8.4 %collective-permute-start.30 = (bf16[256,2048]{1,0:T(8,128)(2,1)}, bf16[256,2048]{1,0:T(8,128)(2,1)}, u32[]{:S(2)}, u32[]{:S(2)}) collective-permute-start(bf16[256,2048]{1,0:T(8,128)(2,1)} %collective-permute-done.26.refs_27_), channel_id=1, source_target_pairs={{0,4},{4,0},{8,12},{12,8},{16,20},{20,16},{24,28},{28,24},{1,5},{5... | collective-permute-start | bytes 3145736 | tf_op jit(solution)/shard_map/ppermute | solution.py:208
  277.2 0.1 copy.12
  277.4 0.1 add_select_fusion.1
  277.5 0.1 pad_add_fusion
  277.6 0.1 concatenate.13
  277.8 0.8 dynamic-slice_select_fusion.q_ref
  278.6 1.2 collective-permute-done.30.refs_31_
  279.8 19.5 %shard_map.60 = bf16[1024,1024]{1,0:T(8,128)(2,1)} custom-call(s32[1024]{0:T(1024)S(1)} %fusion.3.at_ref, bf16[1024,1024]{1,0:T(8,128)(2,1)} %copy-done, bf16[256,2048]{1,0:T(8,128)(2,1)} %get-tuple-element.14.refs_0_, bf16[256,2048]{1,0:T(8,128)(2,1)S(1)} %collective-permute-done.3.refs_1_.refs_3_, ...), custom_call_target="tpu_custom_call" | custom-call | tf_op jit(solution)/shard_map/pallas_call | solution.py:142
  299.3 1.0 slice_bitcast_fusion.1
  300.3 1.6 slice_bitcast_fusion
  301.9 4.2 %shard_map.59 = bf16[128,128]{1,0:T(8,128)(2,1)S(1)} custom-call(s32[1]{0:T(128)} %bitcast.head_ref, bf16[128,128]{1,0:T(8,128)(2,1)S(1)} %dynamic-slice_select_fusion.q_ref, bf16[256,2048]{1,0:T(8,128)(2,1)} %get-tuple-element.14.refs_0_, bf16[256,2048]{1,0:T(8,128)(2,1)S(1)} %collective-permute-done.3.refs_1_.refs_3_, ...), custom_call_target="tpu_custom_call" | custom-call | tf_op jit(solution)/shard_map/pallas_call | solution.py:188
  306.2 10.5 %all_gather.19 = bf16[1024,128]{1,0:T(8,128)(2,1)S(1)} all-gather(bf16[128,128]{1,0:T(8,128)(2,1)S(1)} %shard_map.59), channel_id=1, replica_groups=mesh['ctx'=8,'head'=4] {'ctx'}, dimensions={0}, use_global_device_ids=true | all-gather | bytes 294912 | tf_op jit(solution)/shard_map/all_gather | solution.py:279
  316.7 0.5 copy.15
  317.3 0.2 bitcast_select_fusion
  317.5 1.5 pad_maximum_fusion
  (69 shorter events, 0.7 us)
Async XLA Ops:
  6.5 51.0 %all-gather.5.cloned.1.call-start = ((), (), s32[]{:S(2)}) async-start(), calls=%async_computation | async-start | bytes 2621440 | tf_op jit(solution)/shard_map/all_gather | solution.py:259
  9.4 94.4 %all-gather.7.cloned.1.call-start = ((), (), s32[]{:S(2)}) async-start(), calls=%async_computation.1 | async-start | bytes 2621440 | tf_op jit(solution)/shard_map/all_gather | solution.py:259
  10.2 139.8 %all-gather.9.cloned.1.call-start = ((), (), s32[]{:S(2)}) async-start(), calls=%async_computation.2 | async-start | bytes 2621440 | tf_op jit(solution)/shard_map/all_gather | solution.py:259
  10.9 185.2 %all-gather.11.cloned.1.call-start = ((), (), s32[]{:S(2)}) async-start(), calls=%async_computation.3 | async-start | bytes 2621440 | tf_op jit(solution)/shard_map/all_gather | solution.py:259
  57.6 1.6 copy-start.5
  71.8 24.4 %collective-permute-start.3 = (bf16[256,2048]{1,0:T(8,128)(2,1)}, bf16[256,2048]{1,0:T(8,128)(2,1)S(1)}, u32[]{:S(2)}, u32[]{:S(2)}) collective-permute-start(bf16[256,2048]{1,0:T(8,128)(2,1)} %get-tuple-element.14.refs_0_), channel_id=1, source_target_pairs={{0,8},{4,12},{8,0},{12,4},{16,24},{20,28},{24,16},{28,20},{1,9},{5... | collective-permute-start | bytes 3145736 | tf_op jit(solution)/shard_map/ppermute | solution.py:208
  73.0 30.8 %collective-permute-start.4 = (bf16[256,2048]{1,0:T(8,128)(2,1)}, bf16[256,2048]{1,0:T(8,128)(2,1)}, u32[]{:S(2)}, u32[]{:S(2)}) collective-permute-start(bf16[256,2048]{1,0:T(8,128)(2,1)} %get-tuple-element.14.refs_0_), channel_id=1, source_target_pairs={{0,16},{4,20},{8,24},{12,28},{16,0},{20,4},{24,8},{28,12},{1,17},{... | collective-permute-start | bytes 3145736 | tf_op jit(solution)/shard_map/ppermute | solution.py:208
  74.2 4.5 %collective-permute-start = (bf16[128,1024]{1,0:T(8,128)(2,1)S(1)}, bf16[128,1024]{1,0:T(8,128)(2,1)}, u32[]{:S(2)}, u32[]{:S(2)}) collective-permute-start(bf16[128,1024]{1,0:T(8,128)(2,1)S(1)} %slice.28), channel_id=1, source_target_pairs={{0,8},{1,9},{2,10},{3,11}} | collective-permute-start | bytes 786440 | tf_op jit(solution)/shard_map/ppermute | solution.py:228
  75.6 46.1 %collective-permute-start.6 = (bf16[256,2048]{1,0:T(8,128)(2,1)}, bf16[256,2048]{1,0:T(8,128)(2,1)}, u32[]{:S(2)}, u32[]{:S(2)}) collective-permute-start(bf16[256,2048]{1,0:T(8,128)(2,1)} %get-tuple-element.14.refs_0_), channel_id=1, source_target_pairs={{0,4},{4,0},{8,12},{12,8},{16,20},{20,16},{24,28},{28,24},{1,5},{5... | collective-permute-start | bytes 3145736 | tf_op jit(solution)/shard_map/ppermute | solution.py:208
  96.2 25.5 %collective-permute-start.5 = (bf16[256,2048]{1,0:T(8,128)(2,1)S(1)}, bf16[256,2048]{1,0:T(8,128)(2,1)}, u32[]{:S(2)}, u32[]{:S(2)}) collective-permute-start(bf16[256,2048]{1,0:T(8,128)(2,1)S(1)} %collective-permute-done.3.refs_1_.refs_3_), channel_id=1, source_target_pairs={{0,16},{4,20},{8,24},{12,28},{16,0},{20,4},{24,8},{28,12},{1,17},{... | collective-permute-start | bytes 3145736 | tf_op jit(solution)/shard_map/ppermute | solution.py:208
  103.8 1.6 copy-start.6
  118.0 25.2 %collective-permute-start.10 = (bf16[256,2048]{1,0:T(8,128)(2,1)}, bf16[256,2048]{1,0:T(8,128)(2,1)}, u32[]{:S(2)}, u32[]{:S(2)}) collective-permute-start(bf16[256,2048]{1,0:T(8,128)(2,1)} %get-tuple-element.15.refs_8_), channel_id=1, source_target_pairs={{0,16},{4,20},{8,24},{12,28},{16,0},{20,4},{24,8},{28,12},{1,17},{... | collective-permute-start | bytes 3145736 | tf_op jit(solution)/shard_map/ppermute | solution.py:208
  119.3 25.1 %collective-permute-start.11 = (bf16[256,2048]{1,0:T(8,128)(2,1)}, bf16[256,2048]{1,0:T(8,128)(2,1)}, u32[]{:S(2)}, u32[]{:S(2)}) collective-permute-start(bf16[256,2048]{1,0:T(8,128)(2,1)} %get-tuple-element.15.refs_8_), channel_id=1, source_target_pairs={{0,8},{4,12},{8,0},{12,4},{16,24},{20,28},{24,16},{28,20},{1,9},{5... | collective-permute-start | bytes 3145736 | tf_op jit(solution)/shard_map/ppermute | solution.py:208
  120.5 25.0 %collective-permute-start.7 = (bf16[256,2048]{1,0:T(8,128)(2,1)S(1)}, bf16[256,2048]{1,0:T(8,128)(2,1)S(1)}, u32[]{:S(2)}, u32[]{:S(2)}) collective-permute-start(bf16[256,2048]{1,0:T(8,128)(2,1)S(1)} %collective-permute-done.3.refs_1_.refs_3_), channel_id=1, source_target_pairs={{0,4},{4,0},{8,12},{12,8},{16,20},{20,16},{24,28},{28,24},{1,5},{5... | collective-permute-start | bytes 3145736 | tf_op jit(solution)/shard_map/ppermute | solution.py:208
  121.7 25.9 %collective-permute-start.8 = (bf16[256,2048]{1,0:T(8,128)(2,1)}, bf16[256,2048]{1,0:T(8,128)(2,1)S(1)}, u32[]{:S(2)}, u32[]{:S(2)}) collective-permute-start(bf16[256,2048]{1,0:T(8,128)(2,1)} %collective-permute-done.4.refs_2_.refs_4_), channel_id=1, source_target_pairs={{0,4},{4,0},{8,12},{12,8},{16,20},{20,16},{24,28},{28,24},{1,5},{5... | collective-permute-start | bytes 3145736 | tf_op jit(solution)/shard_map/ppermute | solution.py:208
  121.7 28.3 %collective-permute-start.9 = (bf16[256,2048]{1,0:T(8,128)(2,1)}, bf16[256,2048]{1,0:T(8,128)(2,1)}, u32[]{:S(2)}, u32[]{:S(2)}) collective-permute-start(bf16[256,2048]{1,0:T(8,128)(2,1)} %collective-permute-done.5.refs_5_.refs_3_), channel_id=1, source_target_pairs={{0,4},{4,0},{8,12},{12,8},{16,20},{20,16},{24,28},{28,24},{1,5},{5... | collective-permute-start | bytes 3145736 | tf_op jit(solution)/shard_map/ppermute | solution.py:208
  143.3 23.5 %collective-permute-start.13 = (bf16[256,2048]{1,0:T(8,128)(2,1)}, bf16[256,2048]{1,0:T(8,128)(2,1)}, u32[]{:S(2)}, u32[]{:S(2)}) collective-permute-start(bf16[256,2048]{1,0:T(8,128)(2,1)} %get-tuple-element.15.refs_8_), channel_id=1, source_target_pairs={{0,4},{4,0},{8,12},{12,8},{16,20},{20,16},{24,28},{28,24},{1,5},{5... | collective-permute-start | bytes 3145736 | tf_op jit(solution)/shard_map/ppermute | solution.py:208
  144.3 24.2 %collective-permute-start.12 = (bf16[256,2048]{1,0:T(8,128)(2,1)}, bf16[256,2048]{1,0:T(8,128)(2,1)}, u32[]{:S(2)}, u32[]{:S(2)}) collective-permute-start(bf16[256,2048]{1,0:T(8,128)(2,1)} %collective-permute-done.10.refs_2_.refs_3_.refs_9_), channel_id=1, source_target_pairs={{0,8},{4,12},{8,0},{12,4},{16,24},{20,28},{24,16},{28,20},{1,9},{5... | collective-permute-start | bytes 3145736 | tf_op jit(solution)/shard_map/ppermute | solution.py:208
  145.5 1.0 copy-start.1
  146.4 25.1 %collective-permute-start.14 = (bf16[256,2048]{1,0:T(8,128)(2,1)}, bf16[256,2048]{1,0:T(8,128)(2,1)}, u32[]{:S(2)}, u32[]{:S(2)}) collective-permute-start(bf16[256,2048]{1,0:T(8,128)(2,1)} %collective-permute-done.10.refs_2_.refs_3_.refs_9_), channel_id=1, source_target_pairs={{0,4},{4,0},{8,12},{12,8},{16,20},{20,16},{24,28},{28,24},{1,5},{5... | collective-permute-start | bytes 3145736 | tf_op jit(solution)/shard_map/ppermute | solution.py:208
  147.6 1.0 copy-start.3
  148.6 47.5 %collective-permute-start.15 = (bf16[256,2048]{1,0:T(8,128)(2,1)}, bf16[256,2048]{1,0:T(8,128)(2,1)}, u32[]{:S(2)}, u32[]{:S(2)}) collective-permute-start(bf16[256,2048]{1,0:T(8,128)(2,1)} %collective-permute-done.11.refs_1_.refs_4_.refs_10_), channel_id=1, source_target_pairs={{0,4},{4,0},{8,12},{12,8},{16,20},{20,16},{24,28},{28,24},{1,5},{5... | collective-permute-start | bytes 3145736 | tf_op jit(solution)/shard_map/ppermute | solution.py:208
  150.0 1.2 copy-start.2
  151.2 1.2 copy-start.4
  165.5 30.6 %collective-permute-start.17 = (bf16[256,2048]{1,0:T(8,128)(2,1)}, bf16[256,2048]{1,0:T(8,128)(2,1)}, u32[]{:S(2)}, u32[]{:S(2)}) collective-permute-start(bf16[256,2048]{1,0:T(8,128)(2,1)} %get-tuple-element.17.refs_16_), channel_id=1, source_target_pairs={{0,8},{4,12},{8,0},{12,4},{16,24},{20,28},{24,16},{28,20},{1,9},{5... | collective-permute-start | bytes 3145736 | tf_op jit(solution)/shard_map/ppermute | solution.py:208
  166.7 29.4 %collective-permute-start.18 = (bf16[256,2048]{1,0:T(8,128)(2,1)}, bf16[256,2048]{1,0:T(8,128)(2,1)}, u32[]{:S(2)}, u32[]{:S(2)}) collective-permute-start(bf16[256,2048]{1,0:T(8,128)(2,1)} %get-tuple-element.17.refs_16_), channel_id=1, source_target_pairs={{0,16},{4,20},{8,24},{12,28},{16,0},{20,4},{24,8},{28,12},{1,17},{... | collective-permute-start | bytes 3145736 | tf_op jit(solution)/shard_map/ppermute | solution.py:208
  168.5 27.6 %collective-permute-start.16 = (bf16[256,2048]{1,0:T(8,128)(2,1)}, bf16[256,2048]{1,0:T(8,128)(2,1)}, u32[]{:S(2)}, u32[]{:S(2)}) collective-permute-start(bf16[256,2048]{1,0:T(8,128)(2,1)} %collective-permute-done.12.refs_5_.refs_11_), channel_id=1, source_target_pairs={{0,4},{4,0},{8,12},{12,8},{16,20},{20,16},{24,28},{28,24},{1,5},{5... | collective-permute-start | bytes 3145736 | tf_op jit(solution)/shard_map/ppermute | solution.py:208
  171.5 71.6 %collective-permute-start.20 = (bf16[256,2048]{1,0:T(8,128)(2,1)}, bf16[256,2048]{1,0:T(8,128)(2,1)}, u32[]{:S(2)}, u32[]{:S(2)}) collective-permute-start(bf16[256,2048]{1,0:T(8,128)(2,1)} %get-tuple-element.17.refs_16_), channel_id=1, source_target_pairs={{0,4},{4,0},{8,12},{12,8},{16,20},{20,16},{24,28},{28,24},{1,5},{5... | collective-permute-start | bytes 3145736 | tf_op jit(solution)/shard_map/ppermute | solution.py:208
  196.1 81.0 %copy-start.12 = (s32[8,128,3]{1,0,2:T(8,128)S(1)}, s32[8,128,3]{1,0,2:T(8,128)}, u32[]{:S(2)}) copy-start(s32[8,128,3]{1,0,2:T(8,128)} %param.8) | copy-start | bytes 36868
  196.1 81.0 %copy-start.13 = (s32[8,128,3]{1,0,2:T(8,128)S(1)}, s32[8,128,3]{1,0,2:T(8,128)}, u32[]{:S(2)}) copy-start(s32[8,128,3]{1,0,2:T(8,128)} %param.7) | copy-start | bytes 36868
  196.2 81.2 %copy-start.14 = (s32[3]{0:T(128)S(1)}, s32[3]{0:T(128)}, u32[]{:S(2)}) copy-start(s32[3]{0:T(128)} %constant.77.clone) | copy-start | bytes 40
  209.0 1.3 copy-start
  210.3 33.1 %collective-permute-start.24 = (bf16[256,2048]{1,0:T(8,128)(2,1)}, bf16[256,2048]{1,0:T(8,128)(2,1)S(1)}, u32[]{:S(2)}, u32[]{:S(2)}) collective-permute-start(bf16[256,2048]{1,0:T(8,128)(2,1)} %get-tuple-element.19.refs_24_), channel_id=1, source_target_pairs={{0,16},{4,20},{8,24},{12,28},{16,0},{20,4},{24,8},{28,12},{1,17},{... | collective-permute-start | bytes 3145736 | tf_op jit(solution)/shard_map/ppermute | solution.py:208
  211.5 0.7 collective-permute-start.1
  212.2 56.6 %copy-start.11 = (bf16[128,1024]{1,0:T(8,128)(2,1)}, bf16[128,1024]{1,0:T(8,128)(2,1)S(1)}, u32[]{:S(2)}) copy-start(bf16[128,1024]{1,0:T(8,128)(2,1)S(1)} %broadcast_select_fusion.1) | copy-start | bytes 786436
  212.2 28.7 %collective-permute-start.2 = (bf16[128,1024]{1,0:T(8,128)(2,1)S(1)}, bf16[128,1024]{1,0:T(8,128)(2,1)S(1)}, u32[]{:S(2)}, u32[]{:S(2)}) collective-permute-start(bf16[128,1024]{1,0:T(8,128)(2,1)S(1)} %broadcast_select_fusion.1), channel_id=1, source_target_pairs={{0,4},{8,12},{16,20},{24,28},{1,5},{9,13},{17,21},{25,29},{2,6},{1... | collective-permute-start | bytes 786440 | tf_op jit(solution)/shard_map/ppermute | solution.py:228
  213.7 30.4 %collective-permute-start.25 = (bf16[256,2048]{1,0:T(8,128)(2,1)}, bf16[256,2048]{1,0:T(8,128)(2,1)S(1)}, u32[]{:S(2)}, u32[]{:S(2)}) collective-permute-start(bf16[256,2048]{1,0:T(8,128)(2,1)} %get-tuple-element.19.refs_24_), channel_id=1, source_target_pairs={{0,8},{4,12},{8,0},{12,4},{16,24},{20,28},{24,16},{28,20},{1,9},{5... | collective-permute-start | bytes 3145736 | tf_op jit(solution)/shard_map/ppermute | solution.py:208
  214.9 47.5 %collective-permute-start.27 = (bf16[256,2048]{1,0:T(8,128)(2,1)}, bf16[256,2048]{1,0:T(8,128)(2,1)S(1)}, u32[]{:S(2)}, u32[]{:S(2)}) collective-permute-start(bf16[256,2048]{1,0:T(8,128)(2,1)} %get-tuple-element.19.refs_24_), channel_id=1, source_target_pairs={{0,4},{4,0},{8,12},{12,8},{16,20},{20,16},{24,28},{28,24},{1,5},{5... | collective-permute-start | bytes 3145736 | tf_op jit(solution)/shard_map/ppermute | solution.py:208
  240.9 26.0 %collective-permute-start.19 = (bf16[256,2048]{1,0:T(8,128)(2,1)}, bf16[256,2048]{1,0:T(8,128)(2,1)}, u32[]{:S(2)}, u32[]{:S(2)}) collective-permute-start(bf16[256,2048]{1,0:T(8,128)(2,1)} %collective-permute-done.17.refs_1_.refs_17_), channel_id=1, source_target_pairs={{0,16},{4,20},{8,24},{12,28},{16,0},{20,4},{24,8},{28,12},{1,17},{... | collective-permute-start | bytes 3145736 | tf_op jit(solution)/shard_map/ppermute | solution.py:208
  243.1 24.4 %collective-permute-start.21 = (bf16[256,2048]{1,0:T(8,128)(2,1)}, bf16[256,2048]{1,0:T(8,128)(2,1)S(1)}, u32[]{:S(2)}, u32[]{:S(2)}) collective-permute-start(bf16[256,2048]{1,0:T(8,128)(2,1)} %collective-permute-done.17.refs_1_.refs_17_), channel_id=1, source_target_pairs={{0,4},{4,0},{8,12},{12,8},{16,20},{20,16},{24,28},{28,24},{1,5},{5... | collective-permute-start | bytes 3145736 | tf_op jit(solution)/shard_map/ppermute | solution.py:208
  243.4 36.4 %copy-start.7 = (bf16[256,2048]{1,0:T(8,128)(2,1)}, bf16[256,2048]{1,0:T(8,128)(2,1)S(1)}, u32[]{:S(2)}) copy-start(bf16[256,2048]{1,0:T(8,128)(2,1)S(1)} %collective-permute-done.24.refs_25_) | copy-start | bytes 3145732
  243.4 25.4 %collective-permute-start.26 = (bf16[256,2048]{1,0:T(8,128)(2,1)S(1)}, bf16[256,2048]{1,0:T(8,128)(2,1)}, u32[]{:S(2)}, u32[]{:S(2)}) collective-permute-start(bf16[256,2048]{1,0:T(8,128)(2,1)S(1)} %collective-permute-done.24.refs_25_), channel_id=1, source_target_pairs={{0,8},{4,12},{8,0},{12,4},{16,24},{20,28},{24,16},{28,20},{1,9},{5... | collective-permute-start | bytes 3145736 | tf_op jit(solution)/shard_map/ppermute | solution.py:208
  244.1 35.7 %copy-start.8 = (bf16[256,2048]{1,0:T(8,128)(2,1)}, bf16[256,2048]{1,0:T(8,128)(2,1)S(1)}, u32[]{:S(2)}) copy-start(bf16[256,2048]{1,0:T(8,128)(2,1)S(1)} %collective-permute-done.25.refs_26_) | copy-start | bytes 3145732
  244.1 34.5 %collective-permute-start.22 = (bf16[256,2048]{1,0:T(8,128)(2,1)}, bf16[256,2048]{1,0:T(8,128)(2,1)}, u32[]{:S(2)}, u32[]{:S(2)}) collective-permute-start(bf16[256,2048]{1,0:T(8,128)(2,1)} %collective-permute-done.18.refs_2_.refs_18_), channel_id=1, source_target_pairs={{0,4},{4,0},{8,12},{12,8},{16,20},{20,16},{24,28},{28,24},{1,5},{5... | collective-permute-start | bytes 3145736 | tf_op jit(solution)/shard_map/ppermute | solution.py:208
  262.4 6.4 %copy-start.9 = (bf16[256,2048]{1,0:T(8,128)(2,1)}, bf16[256,2048]{1,0:T(8,128)(2,1)S(1)}, u32[]{:S(2)}) copy-start(bf16[256,2048]{1,0:T(8,128)(2,1)S(1)} %collective-permute-done.27.refs_28_) | copy-start | bytes 3145732
  262.4 16.2 %collective-permute-start.28 = (bf16[256,2048]{1,0:T(8,128)(2,1)S(1)}, bf16[256,2048]{1,0:T(8,128)(2,1)}, u32[]{:S(2)}, u32[]{:S(2)}) collective-permute-start(bf16[256,2048]{1,0:T(8,128)(2,1)S(1)} %collective-permute-done.24.refs_25_), channel_id=1, source_target_pairs={{0,4},{4,0},{8,12},{12,8},{16,20},{20,16},{24,28},{28,24},{1,5},{5... | collective-permute-start | bytes 3145736 | tf_op jit(solution)/shard_map/ppermute | solution.py:208
  267.0 11.6 %collective-permute-start.29 = (bf16[256,2048]{1,0:T(8,128)(2,1)S(1)}, bf16[256,2048]{1,0:T(8,128)(2,1)}, u32[]{:S(2)}, u32[]{:S(2)}) collective-permute-start(bf16[256,2048]{1,0:T(8,128)(2,1)S(1)} %collective-permute-done.25.refs_26_), channel_id=1, source_target_pairs={{0,4},{4,0},{8,12},{12,8},{16,20},{20,16},{24,28},{28,24},{1,5},{5... | collective-permute-start | bytes 3145736 | tf_op jit(solution)/shard_map/ppermute | solution.py:208
  267.6 1.2 copy-start.10
  267.6 11.0 %collective-permute-start.23 = (bf16[256,2048]{1,0:T(8,128)(2,1)}, bf16[256,2048]{1,0:T(8,128)(2,1)}, u32[]{:S(2)}, u32[]{:S(2)}) collective-permute-start(bf16[256,2048]{1,0:T(8,128)(2,1)} %collective-permute-done.19.refs_19_), channel_id=1, source_target_pairs={{0,4},{4,0},{8,12},{12,8},{16,20},{20,16},{24,28},{28,24},{1,5},{5... | collective-permute-start | bytes 3145736 | tf_op jit(solution)/shard_map/ppermute | solution.py:208
  268.8 11.0 %collective-permute-start.30 = (bf16[256,2048]{1,0:T(8,128)(2,1)}, bf16[256,2048]{1,0:T(8,128)(2,1)}, u32[]{:S(2)}, u32[]{:S(2)}) collective-permute-start(bf16[256,2048]{1,0:T(8,128)(2,1)} %collective-permute-done.26.refs_27_), channel_id=1, source_target_pairs={{0,4},{4,0},{8,12},{12,8},{16,20},{20,16},{24,28},{28,24},{1,5},{5... | collective-permute-start | bytes 3145736 | tf_op jit(solution)/shard_map/ppermute | solution.py:208
Sparse Core Ops, SparseCore 0:
  9.5 47.9 all-gather.4
  59.1 44.6 all-gather.6
  105.4 44.5 all-gather.8
  151.4 44.6 all-gather.10

commit v2 on v1

v2 whole, which is shorter than its diff:
```python
import functools

import jax
import jax.numpy as jnp
from jax import lax
from jax.experimental import pallas as pl
from jax.experimental.pallas import tpu as pltpu
from jax.sharding import PartitionSpec as P

HEAD_DIMENSION = 128
BLK = 64
GLOB = 2
RAND = 3
KEY_SET = 3 + GLOB + RAND
LEAD = GLOB * BLK
EXPONENT = HEAD_DIMENSION ** (-0.5) * 1.4426950408889634
PARTS = (4, 4, 4, 4)
PERMUTED = (False, False, False, False)
TOGETHER = 8
PER = 2
VMEM = 60 << 20
TRANSPOSED = (((1,), (1,)), ((), ()))


def project_kernel(line, count, start, *refs):
    pieces, refs = refs[:count], refs[count:]
    w_ref, (q_ref, kv_ref, x_ref, hold_ref, sem) = refs[0], refs[-5:]
    step = pl.program_id(0)
    rows = x_ref.shape[0]

    @pl.when(step == 0)
    def _():
        def fetch(piece, column):
            width = piece.shape[1]
            at = pl.multiple_of(column * width, 128)
            return pltpu.make_async_copy(piece, x_ref.at[:, pl.ds(at, width)], sem)

        if not line:
            copies = [(True, fetch(pieces[0], 0))]
        else:
            z = lax.axis_index("head")
            own, below, above, two, far = pieces
            copies = [
                (True, fetch(own, z)),
                (True, fetch(two, lax.rem(z + 2, 4))),
                (z < 3, fetch(above, lax.min(z + 1, 3))),
                (z > 0, fetch(below, lax.max(z - 1, 0))),
                (jnp.logical_or(z == 0, z == 3), fetch(far, jnp.where(z == 0, 3, 0))),
            ]
        for here, copy in copies:
            pl.when(here)(copy.start)
        for here, copy in copies:
            pl.when(here)(copy.wait)

    out = jnp.dot(x_ref[...], w_ref[...], preferred_element_type=jnp.float32).astype(jnp.bfloat16)
    per = out.shape[1] // (3 * HEAD_DIMENSION)
    for i in range(per):
        at = i * 3 * HEAD_DIMENSION
        hold_ref[step, :, i * HEAD_DIMENSION : (i + 1) * HEAD_DIMENSION] = out[
            :, at : at + HEAD_DIMENSION
        ]
        kv_ref[:, 2 * i * HEAD_DIMENSION : 2 * (i + 1) * HEAD_DIMENSION] = out[
            :, at + HEAD_DIMENSION : at + 3 * HEAD_DIMENSION
        ]
    width = per * HEAD_DIMENSION
    copies = [
        pltpu.make_async_copy(
            hold_ref.at[i], q_ref.at[pl.ds(start, rows), pl.ds(i * width, width)], sem
        )
        for i in range(hold_ref.shape[0])
    ]
    for i, copy in enumerate(copies):
        pl.when(step == i)(copy.start)

    @pl.when(step == len(copies) - 1)
    def _():
        for copy in copies:
            copy.wait()


def project(pieces, weight, queries, start, total, after):
    rows = pieces[0].shape[0]
    depth = weight.shape[0]
    heads = weight.shape[1] // (3 * HEAD_DIMENSION)
    per = PER
    given = () if queries is None else (queries,)
    anywhere = pl.BlockSpec(memory_space=pl.ANY)
    return pl.pallas_call(
        functools.partial(project_kernel, len(pieces) > 1, len(pieces), start),
        grid=(heads // per,),
        in_specs=[anywhere] * len(pieces)
        + [pl.BlockSpec((depth, per * 3 * HEAD_DIMENSION), lambda i: (0, i))]
        + [anywhere] * (len(given) + len(after)),
        out_specs=[anywhere, pl.BlockSpec((rows, per * 2 * HEAD_DIMENSION), lambda i: (0, i))],
        out_shape=[
            jax.ShapeDtypeStruct((total, heads * HEAD_DIMENSION), jnp.bfloat16),
            jax.ShapeDtypeStruct((rows, heads * 2 * HEAD_DIMENSION), jnp.bfloat16),
        ],
        scratch_shapes=[
            pltpu.VMEM((rows, depth), jnp.bfloat16),
            pltpu.VMEM((heads // per, rows, per * HEAD_DIMENSION), jnp.bfloat16),
            pltpu.SemaphoreType.DMA(()),
        ],
        input_output_aliases={len(pieces) + 1: 0} if given else {},
        compiler_params=pltpu.CompilerParams(vmem_limit_bytes=VMEM),
    )(*pieces, weight, *given, *after)


def column_copies(sources, places, head, target, sem):
    at = pl.multiple_of(head * 2 * HEAD_DIMENSION, 2 * HEAD_DIMENSION)
    return [
        pltpu.make_async_copy(
            ref.at[:, pl.ds(at, 2 * HEAD_DIMENSION)], target.at[pl.ds(place, ref.shape[0]), :], sem
        )
        for ref, place in zip(sources, places)
    ]


def sparse_kernel(places, heads, blocks, at_ref, q_ref, *refs):
    sources, (o_ref, held, sem) = refs[: len(places)], refs[-3:]
    head = pl.program_id(0)
    slot = lax.rem(head, 2)

    def copies(which, into):
        return column_copies(sources, places, which, held.at[into], sem.at[into])

    @pl.when(head == 0)
    def _():
        for copy in copies(head, slot):
            copy.start()

    @pl.when(head + 1 < heads)
    def _():
        for copy in copies(head + 1, 1 - slot):
            copy.start()

    for copy in copies(head, slot):
        copy.wait()

    def step(group, carry):
        rows, keys, scores, weights, totals = [], [], [], [], []
        for i in range(TOGETHER):
            block = group * TOGETHER + i
            rows.append(pl.ds(pl.multiple_of(block * BLK, BLK), BLK))
            keys.append(
                jnp.concatenate(
                    [
                        held[
                            slot,
                            pl.ds(
                                pl.multiple_of(
                                    at_ref[(head * blocks + block) * KEY_SET + j], BLK
                                ),
                                BLK,
                            ),
                            :,
                        ]
                        for j in range(KEY_SET)
                    ],
                    axis=0,
                )
            )
        for i in range(TOGETHER):
            scores.append(
                lax.dot_general(
                    q_ref[rows[i], :],
                    keys[i][:, :HEAD_DIMENSION],
                    TRANSPOSED,
                    preferred_element_type=jnp.float32,
                )
            )
        for i in range(TOGETHER):
            largest = jnp.max(scores[i], axis=-1, keepdims=True)
            weight = jnp.exp2((scores[i] - largest) * EXPONENT)
            totals.append(jnp.sum(weight, axis=-1, keepdims=True))
            weights.append(weight.astype(jnp.bfloat16))
        for i in range(TOGETHER):
            out = jnp.dot(
                weights[i], keys[i][:, HEAD_DIMENSION:], preferred_element_type=jnp.float32
            )
            o_ref[rows[i], :] = (out / totals[i]).astype(jnp.bfloat16)
        return carry

    lax.fori_loop(0, blocks // TOGETHER, step, 0)


def sparse(at, queries, sources, places, span, after):
    rows, width = queries.shape
    heads = width // HEAD_DIMENSION
    return pl.pallas_call(
        functools.partial(sparse_kernel, places, heads, rows // BLK),
        grid_spec=pltpu.PrefetchScalarGridSpec(
            num_scalar_prefetch=1,
            grid=(heads,),
            in_specs=[pl.BlockSpec((rows, HEAD_DIMENSION), lambda i, s: (0, i))]
            + [pl.BlockSpec(memory_space=pl.ANY)] * (len(sources) + len(after)),
            out_specs=pl.BlockSpec((rows, HEAD_DIMENSION), lambda i, s: (0, i)),
            scratch_shapes=[
                pltpu.VMEM((2, span, 2 * HEAD_DIMENSION), jnp.bfloat16),
                pltpu.SemaphoreType.DMA((2,)),
            ],
        ),
        out_shape=jax.ShapeDtypeStruct(queries.shape, jnp.bfloat16),
        compiler_params=pltpu.CompilerParams(vmem_limit_bytes=VMEM),
    )(at, queries, *sources, *after)


def lead_kernel(places, step, heads, fresh, last, first_ref, q_ref, *refs):
    sources, refs = refs[: len(places)], refs[len(places) :]
    if not fresh:
        given, refs = refs[:3], refs[3:]
    outs, (held, sem) = refs[:-2], refs[-2:]
    head = pl.program_id(0)
    slot = lax.rem(head, 2)

    def copies(which, into):
        return column_copies(sources, places, first_ref[0] + which, held.at[into], sem.at[into])

    @pl.when(head == 0)
    def _():
        for copy in copies(head, slot):
            copy.start()

    @pl.when(head + 1 < heads)
    def _():
        for copy in copies(head + 1, 1 - slot):
            copy.start()

    for copy in copies(head, slot):
        copy.wait()
    q = q_ref[...]
    spans = [pl.ds(i, step) for i in range(0, held.shape[1], step)]
    scores = [
        lax.dot_general(
            q, held[slot, span, :HEAD_DIMENSION], TRANSPOSED, preferred_element_type=jnp.float32
        )
        for span in spans
    ]
    largest = functools.reduce(
        jnp.maximum, [jnp.max(part, axis=-1, keepdims=True) for part in scores]
    )
    if fresh:
        total, out = 0.0, 0.0
    else:
        largest = jnp.maximum(largest, given[0][:, :1])
        factor = jnp.exp2((given[0][:, :1] - largest) * EXPONENT)
        total, out = given[1][:, :1] * factor, given[2][...] * factor
    for span, part in zip(spans, scores):
        weight = jnp.exp2((part - largest) * EXPONENT)
        total += jnp.sum(weight, axis=-1, keepdims=True)
        out += jnp.dot(
            weight.astype(jnp.bfloat16),
            held[slot, span, HEAD_DIMENSION:],
            preferred_element_type=jnp.float32,
        )
    if last:
        outs[0][...] = (out / total).astype(jnp.bfloat16)
    else:
        outs[0][...] = jnp.broadcast_to(largest, outs[0].shape)
        outs[1][...] = jnp.broadcast_to(total, outs[1].shape)
        outs[2][...] = out


def lead(first, queries, sources, places, span, given, last):
    rows, width = queries.shape
    heads = width // HEAD_DIMENSION
    step = min(span, 1024)
    assert span % step == 0
    block = pl.BlockSpec((rows, HEAD_DIMENSION), lambda i, s: (0, i))
    state = [jax.ShapeDtypeStruct(queries.shape, jnp.float32)] * 3
    return pl.pallas_call(
        functools.partial(lead_kernel, places, step, heads, not given, last),
        grid_spec=pltpu.PrefetchScalarGridSpec(
            num_scalar_prefetch=1,
            grid=(heads,),
            in_specs=[block]
            + [pl.BlockSpec(memory_space=pl.ANY)] * len(sources)
            + [block] * len(given),
            out_specs=block if last else [block] * 3,
            scratch_shapes=[
                pltpu.VMEM((2, span, 2 * HEAD_DIMENSION), jnp.bfloat16),
                pltpu.SemaphoreType.DMA((2,)),
            ],
        ),
        out_shape=jax.ShapeDtypeStruct(queries.shape, jnp.bfloat16) if last else state,
        compiler_params=pltpu.CompilerParams(vmem_limit_bytes=VMEM),
    )(first, queries, *sources, *given)


def crossed(cells, bit, count):
    return lax.ppermute(cells, "ctx", [(i, i ^ bit) for i in range(count)])


def halves(cells):
    half = cells.shape[0] // 2
    return cells[:half], cells[half:]


def spread(own, count, ready=(), before=()):
    own = after(own, *ready) if ready else own
    bits = [1 << i for i in range(1, count.bit_length() - 1)]
    last, other = bits[-1], bits[-2]
    held = [(0, 0, own)]
    for bit in bits[:-2]:
        held += [(run ^ bit, at, crossed(cells, bit, count)) for run, at, cells in held]
    by_other = [(run ^ other, at, crossed(cells, other, count)) for run, at, cells in held]
    by_last = [(run ^ last, at, crossed(cells, last, count)) for run, at, cells in held]
    both = []
    for (run, at, cells), (run_too, _, cells_too) in zip(by_other, by_last):
        one, two = halves(cells)[0], halves(cells_too)[1]
        if before:
            one, two = after(one, *before), after(two, *before)
        both.append((run ^ last, at, crossed(one, last, count)))
        both.append((run_too ^ other, at + cells.shape[0] // 2, crossed(two, other, count)))
    held = held + by_other + by_last + both
    near = [cells for _, _, cells in by_other + by_last]
    far = [cells for _, _, cells in both]
    held += [(run ^ 1, at, crossed(cells, 1, count)) for run, at, cells in held]
    return held, near, far


def awaited(parts):
    near = parts[-1][1] if parts else []
    return near + ([cells for run, _, cells in parts[-2][0] if run] if len(parts) > 1 else [])


def after(cells, *others):
    in_hbm = pl.BlockSpec(memory_space=pl.ANY)
    return pl.pallas_call(
        lambda *refs: None,
        in_specs=[in_hbm] * (1 + len(others)),
        out_specs=in_hbm,
        out_shape=jax.ShapeDtypeStruct(cells.shape, cells.dtype),
        input_output_aliases={0: 0},
    )(cells, *others)


def gather_features(tokens, weight, sizes):
    found, start, two = [], 0, None
    for part, size in enumerate(sizes):
        own = lax.slice_in_dim(tokens, start, start + size)
        if PERMUTED[part] and lax.axis_size("head") == 4:
            two = lax.ppermute(own, "head", [(2, 0), (3, 1), (0, 2), (1, 3)])
            above = lax.ppermute(own, "head", [(1, 0), (2, 1), (3, 2)])
            below = lax.ppermute(own, "head", [(0, 1), (1, 2), (2, 3)])
            two = after(two, weight)
            far = lax.ppermute(two, "head", [(1, 0), (2, 3)])
            found.append((own, below, above, two, far))
        else:
            own = own if two is None else after(own, two)
            found.append((lax.all_gather(own, "head", axis=1, tiled=True),))
        start += size
    return found


def per_device(tokens, proj_weight, partner_shard, partner_block):
    rows = tokens.shape[0]
    depth, heads, _ = proj_weight.shape
    blocks = rows // BLK
    count = lax.axis_size("ctx")
    me = lax.axis_index("ctx")
    span = rows * count
    weight = proj_weight.reshape(depth, heads * 3 * HEAD_DIMENSION)

    mine = me * blocks + jnp.arange(blocks)
    near = (mine[:, None] + jnp.array([-1, 0, 1])) % (count * blocks)
    fixed = jnp.concatenate(
        [near, jnp.broadcast_to(jnp.arange(GLOB)[None], (blocks, GLOB))], axis=1
    )
    partners = lax.dynamic_slice_in_dim(partner_shard * blocks + partner_block, me * blocks, blocks, 1)
    key_set = jnp.concatenate(
        [jnp.broadcast_to(fixed[None], (heads, blocks, 3 + GLOB)), partners], axis=2
    ).astype(jnp.int32)
    at = (((key_set // blocks) ^ me) * rows + (key_set % blocks) * BLK).astype(jnp.int32)

    parts, held, given, lead_queries = [], [], (), None
    queries, start = None, 0
    sizes = [rows * share // sum(PARTS) for share in PARTS]
    half = heads // 2 * HEAD_DIMENSION
    first = jnp.where(me == 1, heads // 2, 0).astype(jnp.int32).reshape(1)

    def placed(which):
        sources, places, start = [], [], 0
        for part in which:
            for run, at_row, cells in parts[part][0]:
                sources.append(cells)
                places.append(start + run * sizes[part] + at_row)
            start += sizes[part] * count
        return sources, places, start

    def at_home():
        sources, places, start = [], [], 0
        for size, part in zip(sizes, parts):
            for run, at_row, cells in part[0]:
                sources.append(cells)
                places.append(run * rows + start + at_row)
            start += size
        return sources, places, span

    at = at.reshape(-1)
    for part, pieces in enumerate(gather_features(tokens, weight, sizes)):
        queries, keyval = project(pieces, weight, queries, start, rows, awaited(parts))
        before = []
        if part == len(sizes) - 1:
            got = lax.ppermute(queries[:LEAD, half:], "ctx", [(0, 1)])
            lead_queries = jnp.where(me == 1, got, queries[:LEAD, :half])
            given = lead(first, lead_queries, *placed(range(part)), (), False)
            before = given[:1]
        parts.append(spread(keyval, count, parts[-1][2] if parts else [], before))
        start += sizes[part]

    lead_own = lead(first, lead_queries, *placed([len(sizes) - 1]), given, True)
    lead_out = jnp.concatenate([lead_own, lax.ppermute(lead_own, "ctx", [(1, 0)])], axis=1)
    out = sparse(at, queries, *at_home(), [lead_own])
    out = out.reshape(rows, heads, HEAD_DIMENSION)
    lead_out = lead_out.reshape(LEAD, heads, HEAD_DIMENSION)
    return jnp.concatenate([jnp.where(me == 0, lead_out, out[:LEAD]), out[LEAD:]], axis=0)


def solution(mesh):
    in_specs = (
        P("ctx", "head"),
        P(None, "head", None),
        P("head", None, None),
        P("head", None, None),
    )
    out_specs = P("ctx", "head", None)
    return jax.shard_map(
        per_device, mesh=mesh, in_specs=in_specs, out_specs=out_specs, check_vma=False
    )
```

time: 327 us -> 303 us (0.927)
  starting transfers between devices: 82.2 us -> 33.3 us
  Pallas kernels: 74.9 us -> 99.9 us
  blocking collectives: 10.5 us -> 0 us
  local copies, waits for them, and re-layouts: 38.6 us -> 43.4 us
  waiting for transfers between devices: 103 us -> 107 us
    ppermute x28 -> x36, starting transfers between devices: 78.5 us -> 29.6 us  [crossed(): return lax.ppermute(cells, 'ctx', [(i, i ^ bit) for i in range(count)])]
    ppermute x28 -> x36, waiting for transfers between devices: 46 us -> 78.7 us  [crossed(): return lax.ppermute(cells, 'ctx', [(i, i ^ bit) for i in range(count)])]
    all_gather x4, waiting for transfers between devices: 55.7 us -> 24.9 us  [gather_features(): found.append((lax.all_gather(own, 'head', axis=1, tiled=True),))]
    pallas_call x5 -> x11, Pallas kernels: 55.3 us -> 80.1 us  [the longest x4 63.1 us: project(): pl.pallas_call(functools.partial(project_kernel, len(pieces) > 1, len(pie...]
    all_gather x1 -> x0, blocking collectives: 10.5 us -> none  [per_device(): lead_out = lax.all_gather(lead_out, 'ctx', axis=0, tiled=True)]
    slice x2 -> x10, local copies, waits for them, and re-layouts: 2.88 us -> 12.9 us  [the longest x8 9.13 us: halves(): return (cells[:half], cells[half:])]
    unnamed x35 -> x50, local copies, waits for them, and re-layouts: 35.5 us -> 30.3 us
  transfers between devices with their start and end apart: 35 -> 42, of which waited for: 10 -> 12; matrix products, arithmetic and copies ran while one was open for 8% -> 13% of each run, Pallas kernels for 16% -> 31%
where the time goes in v2:
time: 303 us; the launch traced here: 302 us
  waiting for transfers between devices  107 us (35%)
  Pallas kernels  99.9 us (33%)
  local copies, waits for them, and re-layouts  43.4 us (14%)
  starting transfers between devices  33.3 us (11%)
  between operations  13.5 us (4%)
  other arithmetic  5.04 us (2%)
    ppermute x36, waiting for transfers between devices, crossed(): return lax.ppermute(cells, 'ctx', [(i, i ^ bit) for i in range(count)])  78.7 us
    pallas_call x4, Pallas kernels, project(): pl.pallas_call(functools.partial(project_kernel, len(pieces) > 1, len(pie...  63.1 us
    unnamed x50, local copies, waits for them, and re-layouts  30.3 us
    ppermute x36, starting transfers between devices, crossed(): return lax.ppermute(cells, 'ctx', [(i, i ^ bit) for i in range(count)])  29.6 us
    all_gather x4, waiting for transfers between devices, gather_features(): found.append((lax.all_gather(own, 'head', axis=1, tiled=True),))  24.9 us
    pallas_call x1, Pallas kernels, sparse(): pl.pallas_call(functools.partial(sparse_kernel, places, heads, rows // BL...  19.8 us
    pallas_call x2, Pallas kernels, lead(): pl.pallas_call(functools.partial(lead_kernel, places, step, heads, not gi...  17 us
    slice x8, local copies, waits for them, and re-layouts, halves(): return (cells[:half], cells[half:])  9.13 us
  transfers between devices with their start and end apart: 42, of which 12 were waited for; matrix products, arithmetic and copies ran while one was open for 13% of the time, Pallas kernels for 31%

profile of v2, /device:TPU:1, one launch (start us, length us, event | category | flops | bytes accessed | tf_op | source)
XLA Modules:
  0.0 301.9 jit_solution(3408256302308908660)
XLA Ops:
  6.5 2.9 fusion.10
  9.5 0.7 all-gather.9.cloned.1.call-update
  10.2 0.7 all-gather.7.cloned.1.call-update
  11.0 23.4 %copy.16 = bf16[512,8,8,384]{3,1,2,0:T(8,128)(2,1)} copy(bf16[512,8,8,384]{3,2,1,0:T(8,128)(2,1)} %bitcast.13) | data formatting | bytes 50331648
  34.4 23.2 %all-gather.11.cloned.1.call-done.refs_0_ = bf16[256,4096]{1,0:T(8,128)(2,1)} async-done(((bf16[256,1024]{1,0:T(8,128)(2,1)}), bf16[256,4096]{1,0:T(8,128)(2,1)}) %all-gather.11.cloned.1.call-update) | async-done | bytes 2097168 | tf_op jit(solution)/shard_map/all_gather | solution.py:351
  57.6 15.9 %shard_map.55 = (bf16[1024,1024]{1,0:T(8,128)(2,1)}, bf16[256,2048]{1,0:T(8,128)(2,1)}) custom-call(bf16[256,4096]{1,0:T(8,128)(2,1)} %all-gather.11.cloned.1.call-done.refs_0_, bf16[4096,3072]{1,0:T(8,128)(2,1)} %bitcast.9), custom_call_target="tpu_custom_call" | custom-call | tf_op jit(solution)/shard_map/pallas_call | solution.py:88
  73.5 1.3 collective-permute-start
  74.7 1.2 collective-permute-start.1
  75.9 22.0 %collective-permute-done.refs_3_.refs_5_.refs_1_ = bf16[256,2048]{1,0:T(8,128)(2,1)S(1)} collective-permute-done((bf16[256,2048]{1,0:T(8,128)(2,1)}, bf16[256,2048]{1,0:T(8,128)(2,1)S(1)}, u32[]{:S(2)}, u32[]{:S(2)}) %collective-permute-start) | collective-permute-done | bytes 1048608 | tf_op jit(solution)/shard_map/ppermute | solution.py:291
  97.9 0.9 slice.69
  98.8 1.2 collective-permute-start.2
  100.0 0.9 slice.70
  101.0 1.2 collective-permute-start.3
  102.1 1.8 all-gather.9.cloned.1.call-done.refs_0_
  103.9 15.9 %shard_map.56 = (bf16[1024,1024]{1,0:T(8,128)(2,1)}, bf16[256,2048]{1,0:T(8,128)(2,1)}) custom-call(bf16[256,4096]{1,0:T(8,128)(2,1)} %all-gather.9.cloned.1.call-done.refs_0_, bf16[4096,3072]{1,0:T(8,128)(2,1)} %bitcast.10, bf16[1024,1024]{1,0:T(8,128)(2,1)} %get-tuple-element.16.refs_2_, ...), custom_call_target="tpu_custom_call", output_to_operand_aliasing={{0}: (2, {})} | custom-call | tf_op jit(solution)/shard_map/pallas_call | solution.py:88
  119.8 0.8 copy-done.11
  120.8 1.2 collective-permute-start.4
  121.9 1.2 collective-permute-start.5
  123.1 1.2 collective-permute-start.6
  124.9 20.3 %collective-permute-done.4.refs_3_.refs_5_.refs_11_ = bf16[256,2048]{1,0:T(8,128)(2,1)S(1)} collective-permute-done((bf16[256,2048]{1,0:T(8,128)(2,1)}, bf16[256,2048]{1,0:T(8,128)(2,1)S(1)}, u32[]{:S(2)}, u32[]{:S(2)}) %collective-permute-start.4) | collective-permute-done | bytes 1048608 | tf_op jit(solution)/shard_map/ppermute | solution.py:291
  145.2 1.4 collective-permute-start.10
  146.6 1.2 collective-permute-start.9
  147.8 0.9 slice.71
  148.7 1.9 slice.72
  150.6 1.2 collective-permute-start.11
  152.1 0.8 collective-permute-start.15
  152.9 15.8 %shard_map.58 = (bf16[1024,1024]{1,0:T(8,128)(2,1)}, bf16[256,2048]{1,0:T(8,128)(2,1)}) custom-call(bf16[256,4096]{1,0:T(8,128)(2,1)} %all-gather.7.cloned.1.call-done.refs_0_, bf16[4096,3072]{1,0:T(8,128)(2,1)} %bitcast.11, bf16[1024,1024]{1,0:T(8,128)(2,1)} %get-tuple-element.18.refs_2_, ...), custom_call_target="tpu_custom_call", output_to_operand_aliasing={{0}: (2, {})} | custom-call | tf_op jit(solution)/shard_map/pallas_call | solution.py:88
  168.7 0.9 collective-permute-start.13
  169.9 0.6 collective-permute-start.16
  171.1 22.8 %collective-permute-done.13.refs_3_.refs_21_ = bf16[256,2048]{1,0:T(8,128)(2,1)S(1)} collective-permute-done((bf16[256,2048]{1,0:T(8,128)(2,1)}, bf16[256,2048]{1,0:T(8,128)(2,1)S(1)}, u32[]{:S(2)}, u32[]{:S(2)}) %collective-permute-start.13) | collective-permute-done | bytes 1048608 | tf_op jit(solution)/shard_map/ppermute | solution.py:291
  193.9 0.6 collective-permute-start.19
  194.6 0.9 collective-permute-start.25
  195.5 0.8 slice.73
  196.3 0.9 slice.74
  198.8 1.0 copy-done.9
  200.0 15.6 %shard_map.60 = (bf16[1024,1024]{1,0:T(8,128)(2,1)}, bf16[256,2048]{1,0:T(8,128)(2,1)}) custom-call(bf16[256,4096]{1,0:T(8,128)(2,1)} %all-gather.5.cloned.1.call-done.refs_0_, bf16[4096,3072]{1,0:T(8,128)(2,1)} %bitcast.12, bf16[1024,1024]{1,0:T(8,128)(2,1)} %get-tuple-element.20.refs_2_, ...), custom_call_target="tpu_custom_call", output_to_operand_aliasing={{0}: (2, {})} | custom-call | tf_op jit(solution)/shard_map/pallas_call | solution.py:88
  215.6 0.8 copy-done.16
  216.4 1.2 collective-permute-start.24
  217.6 0.7 collective-permute-start.23
  218.3 0.9 slice.60
  219.2 1.5 collective-permute-start.20
  220.7 1.8 collective-permute-done.20
  223.0 1.6 slice_select_fusion.1.q_ref
  224.7 0.6 collective-permute-done.29.refs_29_
  225.3 0.8 copy-done.18
  226.1 10.3 %shard_map.62 = (f32[128,512]{1,0:T(8,128)}, f32[128,512]{1,0:T(8,128)}, f32[128,512]{1,0:T(8,128)}) custom-call(s32[1]{0:T(128)} %bitcast.first_ref, bf16[128,512]{1,0:T(8,128)(2,1)} %slice_select_fusion.1.q_ref, bf16[256,2048]{1,0:T(8,128)(2,1)} %get-tuple-element.17.refs_0_, bf16[256,2048]{1,0:T(8,128)(2,1)} %copy-done, bf16[256,2048]{1,0:T(8,128)(2,1)} %copy-done.2, ...), custom_call_target="tpu_custom_call" | custom-call | tf_op jit(solution)/shard_map/pallas_call | solution.py:271
  236.5 4.6 %collective-permute-done.24.refs_2_.refs_32_ = bf16[256,2048]{1,0:T(8,128)(2,1)S(1)} collective-permute-done((bf16[256,2048]{1,0:T(8,128)(2,1)}, bf16[256,2048]{1,0:T(8,128)(2,1)S(1)}, u32[]{:S(2)}, u32[]{:S(2)}) %collective-permute-start.24) | collective-permute-done | bytes 1048608 | tf_op jit(solution)/shard_map/ppermute | solution.py:291
  241.1 0.9 slice.76.refs_0_
  242.0 1.0 collective-permute-start.31
  243.0 1.9 slice.75.refs_0_
  244.9 1.1 collective-permute-start.30
  246.1 1.5 collective-permute-start.32
  248.2 6.5 %collective-permute-done.31.refs_4_.refs_34_ = bf16[128,2048]{1,0:T(8,128)(2,1)} collective-permute-done((bf16[128,2048]{1,0:T(8,128)(2,1)}, bf16[128,2048]{1,0:T(8,128)(2,1)}, u32[]{:S(2)}, u32[]{:S(2)}) %collective-permute-start.31) | collective-permute-done | bytes 524320 | tf_op jit(solution)/shard_map/ppermute | solution.py:291
  254.7 2.0 collective-permute-start.36
  256.7 0.8 collective-permute-done.30.refs_3_.refs_33_
  257.5 2.1 collective-permute-start.35
  260.1 0.6 fusion.4.at_ref
  260.7 0.8 collective-permute-done.35.refs_8_.refs_38_
  261.7 6.7 %shard_map.65.refs_40_ = bf16[128,512]{1,0:T(8,128)(2,1)} custom-call(s32[1]{0:T(128)} %bitcast.first_ref, bf16[128,512]{1,0:T(8,128)(2,1)} %slice_select_fusion.1.q_ref, bf16[256,2048]{1,0:T(8,128)(2,1)} %shard_map.61.refs_0_.refs_30_, bf16[256,2048]{1,0:T(8,128)(2,1)} %collective-permute-done.23.refs_1_.refs_31_, bf16[256,2048]{1,0:T(8,128)(2,1)} %copy-done.13, ...), custom_call_target="tpu_custom_call" | custom-call | tf_op jit(solution)/shard_map/pallas_call | solution.py:271
  268.4 2.1 collective-permute-start.37
  270.5 19.8 %shard_map.66 = bf16[1024,1024]{1,0:T(8,128)(2,1)} custom-call(s32[1024]{0:T(1024)} %fusion.4.at_ref, bf16[1024,1024]{1,0:T(8,128)(2,1)} %get-tuple-element.22.q_ref, bf16[256,2048]{1,0:T(8,128)(2,1)} %get-tuple-element.17.refs_0_, bf16[256,2048]{1,0:T(8,128)(2,1)} %copy-done, bf16[256,2048]{1,0:T(8,128)(2,1)} %copy-done.2, bf16[128,2048]{1,0:T(8,128)(2,1)} %copy-done.11, ...), custom_call_target="tpu_custom_call" | custom-call | tf_op jit(solution)/shard_map/pallas_call | solution.py:190
  290.2 1.6 slice_bitcast_fusion
  292.8 1.0 fusion
  293.9 1.5 pad_maximum_fusion
  (109 shorter events, 6.7 us)
Async XLA Ops:
  6.5 51.0 %all-gather.11.cloned.1.call-start = ((), (), s32[]{:S(2)}) async-start(), calls=%async_computation.3 | async-start | bytes 2621440 | tf_op jit(solution)/shard_map/all_gather | solution.py:351
  9.4 94.4 %all-gather.9.cloned.1.call-start = ((), (), s32[]{:S(2)}) async-start(), calls=%async_computation.2 | async-start | bytes 2621440 | tf_op jit(solution)/shard_map/all_gather | solution.py:351
  10.2 142.7 %all-gather.7.cloned.1.call-start = ((), (), s32[]{:S(2)}) async-start(), calls=%async_computation.1 | async-start | bytes 2621440 | tf_op jit(solution)/shard_map/all_gather | solution.py:351
  10.9 189.1 %all-gather.5.cloned.1.call-start = ((), (), s32[]{:S(2)}) async-start(), calls=%async_computation | async-start | bytes 2621440 | tf_op jit(solution)/shard_map/all_gather | solution.py:351
  73.5 24.4 %collective-permute-start = (bf16[256,2048]{1,0:T(8,128)(2,1)}, bf16[256,2048]{1,0:T(8,128)(2,1)S(1)}, u32[]{:S(2)}, u32[]{:S(2)}) collective-permute-start(bf16[256,2048]{1,0:T(8,128)(2,1)} %get-tuple-element.17.refs_0_), channel_id=1, source_target_pairs={{0,8},{4,12},{8,0},{12,4},{16,24},{20,28},{24,16},{28,20},{1,9},{5... | collective-permute-start | bytes 3145736 | tf_op jit(solution)/shard_map/ppermute | solution.py:291
  74.7 25.3 %collective-permute-start.1 = (bf16[256,2048]{1,0:T(8,128)(2,1)}, bf16[256,2048]{1,0:T(8,128)(2,1)S(1)}, u32[]{:S(2)}, u32[]{:S(2)}) collective-permute-start(bf16[256,2048]{1,0:T(8,128)(2,1)} %get-tuple-element.17.refs_0_), channel_id=1, source_target_pairs={{0,16},{4,20},{8,24},{12,28},{16,0},{20,4},{24,8},{28,12},{1,17},{... | collective-permute-start | bytes 3145736 | tf_op jit(solution)/shard_map/ppermute | solution.py:291
  97.9 6.0 %copy-start = (bf16[256,2048]{1,0:T(8,128)(2,1)}, bf16[256,2048]{1,0:T(8,128)(2,1)S(1)}, u32[]{:S(2)}) copy-start(bf16[256,2048]{1,0:T(8,128)(2,1)S(1)} %collective-permute-done.refs_3_.refs_5_.refs_1_) | copy-start | bytes 3145732
  98.8 20.9 %collective-permute-start.2 = (bf16[128,2048]{1,0:T(8,128)(2,1)}, bf16[128,2048]{1,0:T(8,128)(2,1)S(1)}, u32[]{:S(2)}, u32[]{:S(2)}) collective-permute-start(bf16[128,2048]{1,0:T(8,128)(2,1)} %slice.69), channel_id=1, source_target_pairs={{0,16},{4,20},{8,24},{12,28},{16,0},{20,4},{24,8},{28,12},{1,17},{... | collective-permute-start | bytes 1572872 | tf_op jit(solution)/shard_map/ppermute | solution.py:291
  100.0 3.8 %copy-start.2 = (bf16[256,2048]{1,0:T(8,128)(2,1)}, bf16[256,2048]{1,0:T(8,128)(2,1)S(1)}, u32[]{:S(2)}) copy-start(bf16[256,2048]{1,0:T(8,128)(2,1)S(1)} %collective-permute-done.1.refs_4_.refs_6_.refs_2_) | copy-start | bytes 3145732
  101.0 18.8 %collective-permute-start.3 = (bf16[128,2048]{1,0:T(8,128)(2,1)}, bf16[128,2048]{1,0:T(8,128)(2,1)S(1)}, u32[]{:S(2)}, u32[]{:S(2)}) collective-permute-start(bf16[128,2048]{1,0:T(8,128)(2,1)} %slice.70), channel_id=1, source_target_pairs={{0,8},{4,12},{8,0},{12,4},{16,24},{20,28},{24,16},{28,20},{1,9},{5... | collective-permute-start | bytes 1572872 | tf_op jit(solution)/shard_map/ppermute | solution.py:291
  119.8 4.6 %copy-start.1 = (bf16[256,2048]{1,0:T(8,128)(2,1)S(1)}, bf16[256,2048]{1,0:T(8,128)(2,1)}, u32[]{:S(2)}) copy-start(bf16[256,2048]{1,0:T(8,128)(2,1)} %copy-done) | copy-start | bytes 3145732
  119.8 4.6 %copy-start.3 = (bf16[256,2048]{1,0:T(8,128)(2,1)S(1)}, bf16[256,2048]{1,0:T(8,128)(2,1)}, u32[]{:S(2)}) copy-start(bf16[256,2048]{1,0:T(8,128)(2,1)} %copy-done.2) | copy-start | bytes 3145732
  119.8 1.0 copy-start.12
  120.8 24.4 %collective-permute-start.4 = (bf16[256,2048]{1,0:T(8,128)(2,1)}, bf16[256,2048]{1,0:T(8,128)(2,1)S(1)}, u32[]{:S(2)}, u32[]{:S(2)}) collective-permute-start(bf16[256,2048]{1,0:T(8,128)(2,1)} %shard_map.57.refs_10_), channel_id=1, source_target_pairs={{0,8},{4,12},{8,0},{12,4},{16,24},{20,28},{24,16},{28,20},{1,9},{5... | collective-permute-start | bytes 3145736 | tf_op jit(solution)/shard_map/ppermute | solution.py:291
  121.9 24.6 %collective-permute-start.5 = (bf16[256,2048]{1,0:T(8,128)(2,1)}, bf16[256,2048]{1,0:T(8,128)(2,1)}, u32[]{:S(2)}, u32[]{:S(2)}) collective-permute-start(bf16[256,2048]{1,0:T(8,128)(2,1)} %shard_map.57.refs_10_), channel_id=1, source_target_pairs={{0,16},{4,20},{8,24},{12,28},{16,0},{20,4},{24,8},{28,12},{1,17},{... | collective-permute-start | bytes 3145736 | tf_op jit(solution)/shard_map/ppermute | solution.py:291
  123.1 27.5 %collective-permute-start.6 = (bf16[256,2048]{1,0:T(8,128)(2,1)}, bf16[256,2048]{1,0:T(8,128)(2,1)}, u32[]{:S(2)}, u32[]{:S(2)}) collective-permute-start(bf16[256,2048]{1,0:T(8,128)(2,1)} %get-tuple-element.17.refs_0_), channel_id=1, source_target_pairs={{0,4},{4,0},{8,12},{12,8},{16,20},{20,16},{24,28},{28,24},{1,5},{5... | collective-permute-start | bytes 3145736 | tf_op jit(solution)/shard_map/ppermute | solution.py:291
  124.3 28.5 %collective-permute-start.7 = (bf16[256,2048]{1,0:T(8,128)(2,1)S(1)}, bf16[256,2048]{1,0:T(8,128)(2,1)}, u32[]{:S(2)}, u32[]{:S(2)}) collective-permute-start(bf16[256,2048]{1,0:T(8,128)(2,1)S(1)} %copy-done.1), channel_id=1, source_target_pairs={{0,4},{4,0},{8,12},{12,8},{16,20},{20,16},{24,28},{28,24},{1,5},{5... | collective-permute-start | bytes 3145736 | tf_op jit(solution)/shard_map/ppermute | solution.py:291
  124.3 28.5 %collective-permute-start.8 = (bf16[256,2048]{1,0:T(8,128)(2,1)S(1)}, bf16[256,2048]{1,0:T(8,128)(2,1)}, u32[]{:S(2)}, u32[]{:S(2)}) collective-permute-start(bf16[256,2048]{1,0:T(8,128)(2,1)S(1)} %copy-done.3), channel_id=1, source_target_pairs={{0,4},{4,0},{8,12},{12,8},{16,20},{20,16},{24,28},{28,24},{1,5},{5... | collective-permute-start | bytes 3145736 | tf_op jit(solution)/shard_map/ppermute | solution.py:291
  145.2 7.7 %copy-start.4 = (bf16[256,2048]{1,0:T(8,128)(2,1)}, bf16[256,2048]{1,0:T(8,128)(2,1)S(1)}, u32[]{:S(2)}) copy-start(bf16[256,2048]{1,0:T(8,128)(2,1)S(1)} %collective-permute-done.4.refs_3_.refs_5_.refs_11_) | copy-start | bytes 3145732
  145.2 6.6 %collective-permute-start.10 = (bf16[128,2048]{1,0:T(8,128)(2,1)}, bf16[128,2048]{1,0:T(8,128)(2,1)}, u32[]{:S(2)}, u32[]{:S(2)}) collective-permute-start(bf16[128,2048]{1,0:T(8,128)(2,1)} %copy-done.12), channel_id=1, source_target_pairs={{0,4},{4,0},{8,12},{12,8},{16,20},{20,16},{24,28},{28,24},{1,5},{5... | collective-permute-start | bytes 1572872 | tf_op jit(solution)/shard_map/ppermute | solution.py:291
  146.6 5.5 %collective-permute-start.9 = (bf16[128,2048]{1,0:T(8,128)(2,1)}, bf16[128,2048]{1,0:T(8,128)(2,1)}, u32[]{:S(2)}, u32[]{:S(2)}) collective-permute-start(bf16[128,2048]{1,0:T(8,128)(2,1)} %copy-done.11), channel_id=1, source_target_pairs={{0,4},{4,0},{8,12},{12,8},{16,20},{20,16},{24,28},{28,24},{1,5},{5... | collective-permute-start | bytes 1572872 | tf_op jit(solution)/shard_map/ppermute | solution.py:291
  150.6 18.1 %collective-permute-start.11 = (bf16[128,2048]{1,0:T(8,128)(2,1)}, bf16[128,2048]{1,0:T(8,128)(2,1)}, u32[]{:S(2)}, u32[]{:S(2)}) collective-permute-start(bf16[128,2048]{1,0:T(8,128)(2,1)} %slice.71), channel_id=1, source_target_pairs={{0,16},{4,20},{8,24},{12,28},{16,0},{20,4},{24,8},{28,12},{1,17},{... | collective-permute-start | bytes 1572872 | tf_op jit(solution)/shard_map/ppermute | solution.py:291
  151.8 16.9 %collective-permute-start.12 = (bf16[128,2048]{1,0:T(8,128)(2,1)}, bf16[128,2048]{1,0:T(8,128)(2,1)}, u32[]{:S(2)}, u32[]{:S(2)}) collective-permute-start(bf16[128,2048]{1,0:T(8,128)(2,1)} %slice.72), channel_id=1, source_target_pairs={{0,8},{4,12},{8,0},{12,4},{16,24},{20,28},{24,16},{28,20},{1,9},{5... | collective-permute-start | bytes 1572872 | tf_op jit(solution)/shard_map/ppermute | solution.py:291
  152.1 18.5 %collective-permute-start.15 = (bf16[256,2048]{1,0:T(8,128)(2,1)}, bf16[256,2048]{1,0:T(8,128)(2,1)}, u32[]{:S(2)}, u32[]{:S(2)}) collective-permute-start(bf16[256,2048]{1,0:T(8,128)(2,1)} %shard_map.57.refs_10_), channel_id=1, source_target_pairs={{0,4},{4,0},{8,12},{12,8},{16,20},{20,16},{24,28},{28,24},{1,5},{5... | collective-permute-start | bytes 3145736 | tf_op jit(solution)/shard_map/ppermute | solution.py:291
  168.7 1.3 copy-start.5
  168.7 25.2 %collective-permute-start.13 = (bf16[256,2048]{1,0:T(8,128)(2,1)}, bf16[256,2048]{1,0:T(8,128)(2,1)S(1)}, u32[]{:S(2)}, u32[]{:S(2)}) collective-permute-start(bf16[256,2048]{1,0:T(8,128)(2,1)} %shard_map.59.refs_20_), channel_id=1, source_target_pairs={{0,8},{4,12},{8,0},{12,4},{16,24},{20,28},{24,16},{28,20},{1,9},{5... | collective-permute-start | bytes 3145736 | tf_op jit(solution)/shard_map/ppermute | solution.py:291
  169.7 24.9 %collective-permute-start.14 = (bf16[256,2048]{1,0:T(8,128)(2,1)}, bf16[256,2048]{1,0:T(8,128)(2,1)S(1)}, u32[]{:S(2)}, u32[]{:S(2)}) collective-permute-start(bf16[256,2048]{1,0:T(8,128)(2,1)} %shard_map.59.refs_20_), channel_id=1, source_target_pairs={{0,16},{4,20},{8,24},{12,28},{16,0},{20,4},{24,8},{28,12},{1,17},{... | collective-permute-start | bytes 3145736 | tf_op jit(solution)/shard_map/ppermute | solution.py:291
  169.9 27.8 %collective-permute-start.16 = (bf16[256,2048]{1,0:T(8,128)(2,1)S(1)}, bf16[256,2048]{1,0:T(8,128)(2,1)S(1)}, u32[]{:S(2)}, u32[]{:S(2)}) collective-permute-start(bf16[256,2048]{1,0:T(8,128)(2,1)S(1)} %copy-done.5), channel_id=1, source_target_pairs={{0,4},{4,0},{8,12},{12,8},{16,20},{20,16},{24,28},{28,24},{1,5},{5... | collective-permute-start | bytes 3145736 | tf_op jit(solution)/shard_map/ppermute | solution.py:291
  170.6 28.2 %collective-permute-start.17 = (bf16[256,2048]{1,0:T(8,128)(2,1)}, bf16[256,2048]{1,0:T(8,128)(2,1)S(1)}, u32[]{:S(2)}, u32[]{:S(2)}) collective-permute-start(bf16[256,2048]{1,0:T(8,128)(2,1)} %collective-permute-done.5.refs_4_.refs_6_.refs_12_), channel_id=1, source_target_pairs={{0,4},{4,0},{8,12},{12,8},{16,20},{20,16},{24,28},{28,24},{1,5},{5... | collective-permute-start | bytes 3145736 | tf_op jit(solution)/shard_map/ppermute | solution.py:291
  170.6 26.6 %collective-permute-start.18 = (bf16[128,2048]{1,0:T(8,128)(2,1)}, bf16[128,2048]{1,0:T(8,128)(2,1)S(1)}, u32[]{:S(2)}, u32[]{:S(2)}) collective-permute-start(bf16[128,2048]{1,0:T(8,128)(2,1)} %collective-permute-done.11.refs_1_.refs_7_.refs_13_), channel_id=1, source_target_pairs={{0,4},{4,0},{8,12},{12,8},{16,20},{20,16},{24,28},{28,24},{1,5},{5... | collective-permute-start | bytes 1572872 | tf_op jit(solution)/shard_map/ppermute | solution.py:291
  193.9 6.0 %copy-start.6 = (bf16[256,2048]{1,0:T(8,128)(2,1)}, bf16[256,2048]{1,0:T(8,128)(2,1)S(1)}, u32[]{:S(2)}) copy-start(bf16[256,2048]{1,0:T(8,128)(2,1)S(1)} %collective-permute-done.13.refs_3_.refs_21_) | copy-start | bytes 3145732
  193.9 3.5 %collective-permute-start.19 = (bf16[128,2048]{1,0:T(8,128)(2,1)}, bf16[128,2048]{1,0:T(8,128)(2,1)S(1)}, u32[]{:S(2)}, u32[]{:S(2)}) collective-permute-start(bf16[128,2048]{1,0:T(8,128)(2,1)} %collective-permute-done.12.refs_2_.refs_8_.refs_14_), channel_id=1, source_target_pairs={{0,4},{4,0},{8,12},{12,8},{16,20},{20,16},{24,28},{28,24},{1,5},{5... | collective-permute-start | bytes 1572872 | tf_op jit(solution)/shard_map/ppermute | solution.py:291
  194.6 5.4 %copy-start.7 = (bf16[256,2048]{1,0:T(8,128)(2,1)}, bf16[256,2048]{1,0:T(8,128)(2,1)S(1)}, u32[]{:S(2)}) copy-start(bf16[256,2048]{1,0:T(8,128)(2,1)S(1)} %collective-permute-done.14.refs_4_.refs_22_) | copy-start | bytes 3145732
  194.6 24.6 %collective-permute-start.25 = (bf16[256,2048]{1,0:T(8,128)(2,1)}, bf16[256,2048]{1,0:T(8,128)(2,1)}, u32[]{:S(2)}, u32[]{:S(2)}) collective-permute-start(bf16[256,2048]{1,0:T(8,128)(2,1)} %shard_map.59.refs_20_), channel_id=1, source_target_pairs={{0,4},{4,0},{8,12},{12,8},{16,20},{20,16},{24,28},{28,24},{1,5},{5... | collective-permute-start | bytes 3145736 | tf_op jit(solution)/shard_map/ppermute | solution.py:291
  197.2 1.7 copy-start.14
  197.2 18.4 %collective-permute-start.21 = (bf16[128,2048]{1,0:T(8,128)(2,1)}, bf16[128,2048]{1,0:T(8,128)(2,1)}, u32[]{:S(2)}, u32[]{:S(2)}) collective-permute-start(bf16[128,2048]{1,0:T(8,128)(2,1)} %slice.73), channel_id=1, source_target_pairs={{0,16},{4,20},{8,24},{12,28},{16,0},{20,4},{24,8},{28,12},{1,17},{... | collective-permute-start | bytes 1572872 | tf_op jit(solution)/shard_map/ppermute | solution.py:291
  197.4 1.4 copy-start.15
  197.4 25.2 %collective-permute-start.26 = (bf16[256,2048]{1,0:T(8,128)(2,1)S(1)}, bf16[256,2048]{1,0:T(8,128)(2,1)}, u32[]{:S(2)}, u32[]{:S(2)}) collective-permute-start(bf16[256,2048]{1,0:T(8,128)(2,1)S(1)} %collective-permute-done.13.refs_3_.refs_21_), channel_id=1, source_target_pairs={{0,4},{4,0},{8,12},{12,8},{16,20},{20,16},{24,28},{28,24},{1,5},{5... | collective-permute-start | bytes 3145736 | tf_op jit(solution)/shard_map/ppermute | solution.py:291
  197.8 1.0 copy-start.8
  197.8 17.8 %collective-permute-start.22 = (bf16[128,2048]{1,0:T(8,128)(2,1)}, bf16[128,2048]{1,0:T(8,128)(2,1)S(1)}, u32[]{:S(2)}, u32[]{:S(2)}) collective-permute-start(bf16[128,2048]{1,0:T(8,128)(2,1)} %slice.74), channel_id=1, source_target_pairs={{0,8},{4,12},{8,0},{12,4},{16,24},{20,28},{24,16},{28,20},{1,9},{5... | collective-permute-start | bytes 1572872 | tf_op jit(solution)/shard_map/ppermute | solution.py:291
  198.8 1.0 copy-start.9
  199.8 24.8 %collective-permute-start.27 = (bf16[256,2048]{1,0:T(8,128)(2,1)S(1)}, bf16[256,2048]{1,0:T(8,128)(2,1)}, u32[]{:S(2)}, u32[]{:S(2)}) collective-permute-start(bf16[256,2048]{1,0:T(8,128)(2,1)S(1)} %collective-permute-done.14.refs_4_.refs_22_), channel_id=1, source_target_pairs={{0,4},{4,0},{8,12},{12,8},{16,20},{20,16},{24,28},{28,24},{1,5},{5... | collective-permute-start | bytes 3145736 | tf_op jit(solution)/shard_map/ppermute | solution.py:291
  215.6 0.8 copy-start.16
  216.4 24.7 %collective-permute-start.24 = (bf16[256,2048]{1,0:T(8,128)(2,1)}, bf16[256,2048]{1,0:T(8,128)(2,1)S(1)}, u32[]{:S(2)}, u32[]{:S(2)}) collective-permute-start(bf16[256,2048]{1,0:T(8,128)(2,1)} %shard_map.61.refs_0_.refs_30_), channel_id=1, source_target_pairs={{0,16},{4,20},{8,24},{12,28},{16,0},{20,4},{24,8},{28,12},{1,17},{... | collective-permute-start | bytes 3145736 | tf_op jit(solution)/shard_map/ppermute | solution.py:291
  217.6 25.5 %collective-permute-start.23 = (bf16[256,2048]{1,0:T(8,128)(2,1)}, bf16[256,2048]{1,0:T(8,128)(2,1)}, u32[]{:S(2)}, u32[]{:S(2)}) collective-permute-start(bf16[256,2048]{1,0:T(8,128)(2,1)} %shard_map.61.refs_0_.refs_30_), channel_id=1, source_target_pairs={{0,8},{4,12},{8,0},{12,4},{16,24},{20,28},{24,16},{28,20},{1,9},{5... | collective-permute-start | bytes 3145736 | tf_op jit(solution)/shard_map/ppermute | solution.py:291
  219.2 3.2 %collective-permute-start.20 = (bf16[128,512]{1,0:T(8,128)(2,1)S(1)}, bf16[128,512]{1,0:T(8,128)(2,1)S(1)}, u32[]{:S(2)}, u32[]{:S(2)}) collective-permute-start(bf16[128,512]{1,0:T(8,128)(2,1)S(1)} %slice.60), channel_id=1, source_target_pairs={{0,4},{1,5},{2,6},{3,7}} | collective-permute-start | bytes 393224 | tf_op jit(solution)/shard_map/ppermute | solution.py:405
  222.5 2.3 collective-permute-start.28
  222.6 2.7 collective-permute-start.29
  225.3 0.8 copy-start.18
  241.1 6.5 %copy-start.13 = (bf16[256,2048]{1,0:T(8,128)(2,1)}, bf16[256,2048]{1,0:T(8,128)(2,1)S(1)}, u32[]{:S(2)}) copy-start(bf16[256,2048]{1,0:T(8,128)(2,1)S(1)} %collective-permute-done.24.refs_2_.refs_32_) | copy-start | bytes 3145732
  242.0 4.1 %copy-start.10 = (bf16[256,2048]{1,0:T(8,128)(2,1)S(1)}, bf16[256,2048]{1,0:T(8,128)(2,1)}, u32[]{:S(2)}) copy-start(bf16[256,2048]{1,0:T(8,128)(2,1)} %shard_map.61.refs_0_.refs_30_) | copy-start | bytes 3145732
  242.0 6.1 %copy-start.22 = (s32[3]{0:T(128)S(1)}, s32[3]{0:T(128)}, u32[]{:S(2)}) copy-start(s32[3]{0:T(128)} %constant.58.clone) | copy-start | bytes 40
  242.0 17.6 %copy-start.20 = (s32[8,128,3]{1,0,2:T(8,128)S(1)}, s32[8,128,3]{1,0,2:T(8,128)}, u32[]{:S(2)}) copy-start(s32[8,128,3]{1,0,2:T(8,128)} %param.8) | copy-start | bytes 36868
  242.0 17.6 %copy-start.21 = (s32[8,128,3]{1,0,2:T(8,128)S(1)}, s32[8,128,3]{1,0,2:T(8,128)}, u32[]{:S(2)}) copy-start(s32[8,128,3]{1,0,2:T(8,128)} %param.7) | copy-start | bytes 36868
  242.0 12.7 %collective-permute-start.31 = (bf16[128,2048]{1,0:T(8,128)(2,1)}, bf16[128,2048]{1,0:T(8,128)(2,1)}, u32[]{:S(2)}, u32[]{:S(2)}) collective-permute-start(bf16[128,2048]{1,0:T(8,128)(2,1)} %shard_map.64), channel_id=1, source_target_pairs={{0,8},{4,12},{8,0},{12,4},{16,24},{20,28},{24,16},{28,20},{1,9},{5... | collective-permute-start | bytes 1572872 | tf_op jit(solution)/shard_map/ppermute | solution.py:291
  244.9 12.6 %collective-permute-start.30 = (bf16[128,2048]{1,0:T(8,128)(2,1)}, bf16[128,2048]{1,0:T(8,128)(2,1)}, u32[]{:S(2)}, u32[]{:S(2)}) collective-permute-start(bf16[128,2048]{1,0:T(8,128)(2,1)} %shard_map.63), channel_id=1, source_target_pairs={{0,16},{4,20},{8,24},{12,28},{16,0},{20,4},{24,8},{28,12},{1,17},{... | collective-permute-start | bytes 1572872 | tf_op jit(solution)/shard_map/ppermute | solution.py:291
  246.1 14.6 %collective-permute-start.32 = (bf16[256,2048]{1,0:T(8,128)(2,1)S(1)}, bf16[256,2048]{1,0:T(8,128)(2,1)S(1)}, u32[]{:S(2)}, u32[]{:S(2)}) collective-permute-start(bf16[256,2048]{1,0:T(8,128)(2,1)S(1)} %copy-done.10), channel_id=1, source_target_pairs={{0,4},{4,0},{8,12},{12,8},{16,20},{20,16},{24,28},{28,24},{1,5},{5... | collective-permute-start | bytes 3145736 | tf_op jit(solution)/shard_map/ppermute | solution.py:291
  247.6 13.1 %collective-permute-start.33 = (bf16[256,2048]{1,0:T(8,128)(2,1)}, bf16[256,2048]{1,0:T(8,128)(2,1)}, u32[]{:S(2)}, u32[]{:S(2)}) collective-permute-start(bf16[256,2048]{1,0:T(8,128)(2,1)} %collective-permute-done.23.refs_1_.refs_31_), channel_id=1, source_target_pairs={{0,4},{4,0},{8,12},{12,8},{16,20},{20,16},{24,28},{28,24},{1,5},{5... | collective-permute-start | bytes 3145736 | tf_op jit(solution)/shard_map/ppermute | solution.py:291
  247.6 13.1 %collective-permute-start.34 = (bf16[256,2048]{1,0:T(8,128)(2,1)S(1)}, bf16[256,2048]{1,0:T(8,128)(2,1)}, u32[]{:S(2)}, u32[]{:S(2)}) collective-permute-start(bf16[256,2048]{1,0:T(8,128)(2,1)S(1)} %collective-permute-done.24.refs_2_.refs_32_), channel_id=1, source_target_pairs={{0,4},{4,0},{8,12},{12,8},{16,20},{20,16},{24,28},{28,24},{1,5},{5... | collective-permute-start | bytes 3145736 | tf_op jit(solution)/shard_map/ppermute | solution.py:291
  254.7 6.0 %collective-permute-start.36 = (bf16[128,2048]{1,0:T(8,128)(2,1)}, bf16[128,2048]{1,0:T(8,128)(2,1)}, u32[]{:S(2)}, u32[]{:S(2)}) collective-permute-start(bf16[128,2048]{1,0:T(8,128)(2,1)} %collective-permute-done.31.refs_4_.refs_34_), channel_id=1, source_target_pairs={{0,4},{4,0},{8,12},{12,8},{16,20},{20,16},{24,28},{28,24},{1,5},{5... | collective-permute-start | bytes 1572872 | tf_op jit(solution)/shard_map/ppermute | solution.py:291
  257.5 3.9 %collective-permute-start.35 = (bf16[128,2048]{1,0:T(8,128)(2,1)}, bf16[128,2048]{1,0:T(8,128)(2,1)}, u32[]{:S(2)}, u32[]{:S(2)}) collective-permute-start(bf16[128,2048]{1,0:T(8,128)(2,1)} %collective-permute-done.30.refs_3_.refs_33_), channel_id=1, source_target_pairs={{0,4},{4,0},{8,12},{12,8},{16,20},{20,16},{24,28},{28,24},{1,5},{5... | collective-permute-start | bytes 1572872 | tf_op jit(solution)/shard_map/ppermute | solution.py:291
  260.7 1.0 copy-start.17
  268.4 24.1 %collective-permute-start.37 = (bf16[128,512]{1,0:T(8,128)(2,1)}, bf16[128,512]{1,0:T(8,128)(2,1)S(1)}, u32[]{:S(2)}, u32[]{:S(2)}) collective-permute-start(bf16[128,512]{1,0:T(8,128)(2,1)} %shard_map.65.refs_40_), channel_id=1, source_target_pairs={{4,0},{5,1},{6,2},{7,3}} | collective-permute-start | bytes 393224 | tf_op jit(solution)/shard_map/ppermute | solution.py:413
  291.9 0.9 copy-start.19
  (1 other events, 0.8 us)
Sparse Core Ops, SparseCore 0:
  9.5 47.9 all-gather.10
  59.1 44.6 all-gather.8
  105.5 44.5 all-gather.6
  151.5 44.7 all-gather.4

commit v3 on v2

--- a/solution.py
+++ b/solution.py
@@ -1,4 +1,5 @@
 import functools
+import math
 
 import jax
 import jax.numpy as jnp
@@ -15,43 +16,17 @@
 LEAD = GLOB * BLK
 EXPONENT = HEAD_DIMENSION ** (-0.5) * 1.4426950408889634
 PARTS = (4, 4, 4, 4)
-PERMUTED = (False, False, False, False)
-TOGETHER = 8
+GROUPS = (0, 1, 2, 3)
+TOGETHER = 16
 PER = 2
 VMEM = 60 << 20
 TRANSPOSED = (((1,), (1,)), ((), ()))
 
 
-def project_kernel(line, count, start, *refs):
-    pieces, refs = refs[:count], refs[count:]
-    w_ref, (q_ref, kv_ref, x_ref, hold_ref, sem) = refs[0], refs[-5:]
+def project_kernel(start, x_ref, w_ref, *refs):
+    q_ref, kv_ref, hold_ref, sem = refs[-4:]
     step = pl.program_id(0)
     rows = x_ref.shape[0]
-
-    @pl.when(step == 0)
-    def _():
-        def fetch(piece, column):
-            width = piece.shape[1]
-            at = pl.multiple_of(column * width, 128)
-            return pltpu.make_async_copy(piece, x_ref.at[:, pl.ds(at, width)], sem)
-
-        if not line:
-            copies = [(True, fetch(pieces[0], 0))]
-        else:
-            z = lax.axis_index("head")
-            own, below, above, two, far = pieces
-            copies = [
-                (True, fetch(own, z)),
-                (True, fetch(two, lax.rem(z + 2, 4))),
-                (z < 3, fetch(above, lax.min(z + 1, 3))),
-                (z > 0, fetch(below, lax.max(z - 1, 0))),
-                (jnp.logical_or(z == 0, z == 3), fetch(far, jnp.where(z == 0, 3, 0))),
-            ]
-        for here, copy in copies:
-            pl.when(here)(copy.start)
-        for here, copy in copies:
-            pl.when(here)(copy.wait)
-
     out = jnp.dot(x_ref[...], w_ref[...], preferred_element_type=jnp.float32).astype(jnp.bfloat16)
     per = out.shape[1] // (3 * HEAD_DIMENSION)
     for i in range(per):
@@ -78,18 +53,20 @@
             copy.wait()
 
 
-def project(pieces, weight, queries, start, total, after):
-    rows = pieces[0].shape[0]
-    depth = weight.shape[0]
+def project(x, begin, rows, weight, queries, start, total, after):
+    depth = x.shape[1]
+    assert begin % rows == 0
     heads = weight.shape[1] // (3 * HEAD_DIMENSION)
     per = PER
     given = () if queries is None else (queries,)
     anywhere = pl.BlockSpec(memory_space=pl.ANY)
     return pl.pallas_call(
-        functools.partial(project_kernel, len(pieces) > 1, len(pieces), start),
+        functools.partial(project_kernel, start),
         grid=(heads // per,),
-        in_specs=[anywhere] * len(pieces)
-        + [pl.BlockSpec((depth, per * 3 * HEAD_DIMENSION), lambda i: (0, i))]
+        in_specs=[
+            pl.BlockSpec((rows, depth), lambda i: (begin // rows, 0)),
+            pl.BlockSpec((depth, per * 3 * HEAD_DIMENSION), lambda i: (0, i)),
+        ]
         + [anywhere] * (len(given) + len(after)),
         out_specs=[anywhere, pl.BlockSpec((rows, per * 2 * HEAD_DIMENSION), lambda i: (0, i))],
         out_shape=[
@@ -97,13 +74,17 @@
             jax.ShapeDtypeStruct((rows, heads * 2 * HEAD_DIMENSION), jnp.bfloat16),
         ],
         scratch_shapes=[
-            pltpu.VMEM((rows, depth), jnp.bfloat16),
             pltpu.VMEM((heads // per, rows, per * HEAD_DIMENSION), jnp.bfloat16),
             pltpu.SemaphoreType.DMA(()),
         ],
-        input_output_aliases={len(pieces) + 1: 0} if given else {},
+        input_output_aliases={2: 0} if given else {},
+        cost_estimate=pl.CostEstimate(
+            flops=2 * rows * depth * weight.shape[1],
+            bytes_accessed=2 * (rows * depth + (depth + rows) * weight.shape[1]),
+            transcendentals=0,
+        ),
         compiler_params=pltpu.CompilerParams(vmem_limit_bytes=VMEM),
-    )(*pieces, weight, *given, *after)
+    )(x, weight, *given, *after)
 
 
 def column_copies(sources, places, head, target, sem):
@@ -201,6 +182,11 @@
             ],
         ),
         out_shape=jax.ShapeDtypeStruct(queries.shape, jnp.bfloat16),
+        cost_estimate=pl.CostEstimate(
+            flops=4 * rows * heads * KEY_SET * BLK * HEAD_DIMENSION,
+            bytes_accessed=4 * (span + rows) * heads * HEAD_DIMENSION,
+            transcendentals=rows * heads * KEY_SET * BLK,
+        ),
         compiler_params=pltpu.CompilerParams(vmem_limit_bytes=VMEM),
     )(at, queries, *sources, *after)
 
@@ -264,7 +250,7 @@
 def lead(first, queries, sources, places, span, given, last):
     rows, width = queries.shape
     heads = width // HEAD_DIMENSION
-    step = min(span, 1024)
+    step = math.gcd(span, 1024)
     assert span % step == 0
     block = pl.BlockSpec((rows, HEAD_DIMENSION), lambda i, s: (0, i))
     state = [jax.ShapeDtypeStruct(queries.shape, jnp.float32)] * 3
@@ -283,6 +269,11 @@
             ],
         ),
         out_shape=jax.ShapeDtypeStruct(queries.shape, jnp.bfloat16) if last else state,
+        cost_estimate=pl.CostEstimate(
+            flops=4 * rows * width * span,
+            bytes_accessed=4 * span * width,
+            transcendentals=rows * heads * span,
+        ),
         compiler_params=pltpu.CompilerParams(vmem_limit_bytes=VMEM),
     )(first, queries, *sources, *given)
 
@@ -319,11 +310,6 @@
     return held, near, far
 
 
-def awaited(parts):
-    near = parts[-1][1] if parts else []
-    return near + ([cells for run, _, cells in parts[-2][0] if run] if len(parts) > 1 else [])
-
-
 def after(cells, *others):
     in_hbm = pl.BlockSpec(memory_space=pl.ANY)
     return pl.pallas_call(
@@ -335,21 +321,33 @@
     )(cells, *others)
 
 
+def cut_kernel(start, x_ref, *refs):
+    o_ref, sem = refs[-2:]
+    copy = pltpu.make_async_copy(x_ref.at[pl.ds(start, o_ref.shape[0]), :], o_ref, sem)
+    copy.start()
+    copy.wait()
+
+
+def cut(cells, start, size, after):
+    anywhere = pl.BlockSpec(memory_space=pl.ANY)
+    return pl.pallas_call(
+        functools.partial(cut_kernel, start),
+        grid=(1,),
+        in_specs=[anywhere] * (1 + len(after)),
+        out_specs=pl.BlockSpec((size, cells.shape[1]), lambda i: (0, 0)),
+        out_shape=jax.ShapeDtypeStruct((size, cells.shape[1]), cells.dtype),
+        scratch_shapes=[pltpu.SemaphoreType.DMA(())],
+    )(cells, *after)
+
+
 def gather_features(tokens, weight, sizes):
-    found, start, two = [], 0, None
-    for part, size in enumerate(sizes):
-        own = lax.slice_in_dim(tokens, start, start + size)
-        if PERMUTED[part] and lax.axis_size("head") == 4:
-            two = lax.ppermute(own, "head", [(2, 0), (3, 1), (0, 2), (1, 3)])
-            above = lax.ppermute(own, "head", [(1, 0), (2, 1), (3, 2)])
-            below = lax.ppermute(own, "head", [(0, 1), (1, 2), (2, 3)])
-            two = after(two, weight)
-            far = lax.ppermute(two, "head", [(1, 0), (2, 3)])
-            found.append((own, below, above, two, far))
-        else:
-            own = own if two is None else after(own, two)
-            found.append((lax.all_gather(own, "head", axis=1, tiled=True),))
-        start += size
+    found, start = [], 0
+    for group in range(GROUPS[-1] + 1):
+        members = [size for size, own in zip(sizes, GROUPS) if own == group]
+        own = cut(tokens, start, sum(members), [weight] if start else [])
+        full = lax.all_gather(own, "head", axis=1, tiled=True)
+        found += [(full, sum(members[:i])) for i in range(len(members))]
+        start += sum(members)
     return found
 
 
@@ -398,15 +396,20 @@
         return sources, places, span
 
     at = at.reshape(-1)
-    for part, pieces in enumerate(gather_features(tokens, weight, sizes)):
-        queries, keyval = project(pieces, weight, queries, start, rows, awaited(parts))
-        before = []
+    for part, (x, begin) in enumerate(gather_features(tokens, weight, sizes)):
+        fresh = part == 0 or GROUPS[part] > GROUPS[part - 1]
+        near, far = parts[-1][1:] if parts else ([], [])
+        settled = [cells for run, _, cells in parts[-2][0] if run] if part > 1 else []
+        queries, keyval = project(
+            x, begin, sizes[part], weight, queries, start, rows, settled + (near if fresh else [])
+        )
+        ready, before = (far, []) if fresh else (near, far)
         if part == len(sizes) - 1:
             got = lax.ppermute(queries[:LEAD, half:], "ctx", [(0, 1)])
             lead_queries = jnp.where(me == 1, got, queries[:LEAD, :half])
             given = lead(first, lead_queries, *placed(range(part)), (), False)
-            before = given[:1]
-        parts.append(spread(keyval, count, parts[-1][2] if parts else [], before))
+            before = [given[0]] + before
+        parts.append(spread(keyval, count, ready, before))
         start += sizes[part]
 
     lead_own = lead(first, lead_queries, *placed([len(sizes) - 1]), given, True)

time: 303 us -> 295 us (0.974)
  waiting for transfers between devices: 107 us -> 98.1 us
  starting transfers between devices: 33.3 us -> 38 us
  local copies, waits for them, and re-layouts: 43.4 us -> 39.9 us
    ppermute x36, waiting for transfers between devices: 78.7 us -> 71.4 us  [crossed(): return lax.ppermute(cells, 'ctx', [(i, i ^ bit) for i in range(count)])]
    ppermute x36, starting transfers between devices: 29.6 us -> 34.3 us  [crossed(): return lax.ppermute(cells, 'ctx', [(i, i ^ bit) for i in range(count)])]
    unnamed x50 -> x48, local copies, waits for them, and re-layouts: 30.3 us -> 29.7 us
    pallas_call x4 -> x8, Pallas kernels: 63.1 us -> 63.4 us  [the longest x4 56 us: project(): pl.pallas_call(functools.partial(project_kernel, start), grid=(heads // p...]
where the time goes in v3:
time: 295 us; the launch traced here: 293 us
  Pallas kernels  98.9 us (34%)
  waiting for transfers between devices  98.1 us (33%)
  local copies, waits for them, and re-layouts  39.9 us (14%)
  starting transfers between devices  38 us (13%)
  between operations  13.5 us (5%)
  other arithmetic  5.03 us (2%)
    ppermute x36, waiting for transfers between devices, crossed(): return lax.ppermute(cells, 'ctx', [(i, i ^ bit) for i in range(count)])  71.4 us
    pallas_call x4, Pallas kernels, project(): pl.pallas_call(functools.partial(project_kernel, start), grid=(heads // p...  56 us
    ppermute x36, starting transfers between devices, crossed(): return lax.ppermute(cells, 'ctx', [(i, i ^ bit) for i in range(count)])  34.3 us
    unnamed x48, local copies, waits for them, and re-layouts  29.7 us
    all_gather x4, waiting for transfers between devices, gather_features(): full = lax.all_gather(own, 'head', axis=1, tiled=True)  24.7 us
    pallas_call x1, Pallas kernels, sparse(): pl.pallas_call(functools.partial(sparse_kernel, places, heads, rows // BL...  18.5 us
    pallas_call x2, Pallas kernels, lead(): pl.pallas_call(functools.partial(lead_kernel, places, step, heads, not gi...  17 us
    slice x8, local copies, waits for them, and re-layouts, halves(): return (cells[:half], cells[half:])  9.08 us
  transfers between devices with their start and end apart: 42, of which 12 were waited for; matrix products, arithmetic and copies ran while one was open for 13% of the time, Pallas kernels for 31%

profile of v3, /device:TPU:1, one launch (start us, length us, event | category | flops | bytes accessed | tf_op | source)
XLA Modules:
  0.0 293.4 jit_solution(5205395393627186093)
XLA Ops:
  6.5 1.8 shard_map.58
  8.5 23.5 %copy.16 = bf16[512,8,8,384]{3,1,2,0:T(8,128)(2,1)} copy(bf16[512,8,8,384]{3,2,1,0:T(8,128)(2,1)} %bitcast.16) | data formatting | bytes 50331648
  31.9 1.9 shard_map.57
  33.9 1.9 shard_map.56
  35.8 21.1 %all-gather.11.cloned.1.call-done.x_ref = bf16[256,4096]{1,0:T(8,128)(2,1)} async-done(((bf16[256,1024]{1,0:T(8,128)(2,1)}), bf16[256,4096]{1,0:T(8,128)(2,1)}) %all-gather.11.cloned.1.call-update) | async-done | bytes 2097168 | tf_op jit(solution)/shard_map/all_gather | solution.py:348
  56.9 14.1 %shard_map.59 = (bf16[1024,1024]{1,0:T(8,128)(2,1)}, bf16[256,2048]{1,0:T(8,128)(2,1)}) custom-call(bf16[256,4096]{1,0:T(8,128)(2,1)} %all-gather.11.cloned.1.call-done.x_ref, bf16[4096,3072]{1,0:T(8,128)(2,1)} %bitcast.11), custom_call_target="tpu_custom_call" | custom-call | flops 6442450944 | bytes 28835840 | tf_op jit(solution)/shard_map/pallas_call | solution.py:63
  71.1 1.3 collective-permute-start
  72.3 1.2 collective-permute-start.1
  73.5 1.3 collective-permute-start.4
  74.8 20.7 %collective-permute-done.refs_1_ = bf16[256,2048]{1,0:T(8,128)(2,1)S(1)} collective-permute-done((bf16[256,2048]{1,0:T(8,128)(2,1)}, bf16[256,2048]{1,0:T(8,128)(2,1)S(1)}, u32[]{:S(2)}, u32[]{:S(2)}) %collective-permute-start) | collective-permute-done | bytes 1048608 | tf_op jit(solution)/shard_map/ppermute | solution.py:282
  95.4 0.9 slice.53
  96.3 1.2 collective-permute-start.2
  97.5 0.9 slice.54
  98.4 1.2 collective-permute-start.3
  99.6 3.6 %all-gather.9.cloned.1.call-done.x_ref = bf16[256,4096]{1,0:T(8,128)(2,1)} async-done(((bf16[256,1024]{1,0:T(8,128)(2,1)}), bf16[256,4096]{1,0:T(8,128)(2,1)}) %all-gather.9.cloned.1.call-update) | async-done | bytes 2097168 | tf_op jit(solution)/shard_map/all_gather | solution.py:348
  103.2 14.1 %shard_map.60 = (bf16[1024,1024]{1,0:T(8,128)(2,1)}, bf16[256,2048]{1,0:T(8,128)(2,1)}) custom-call(bf16[256,4096]{1,0:T(8,128)(2,1)} %all-gather.9.cloned.1.call-done.x_ref, bf16[4096,3072]{1,0:T(8,128)(2,1)} %bitcast.12, bf16[1024,1024]{1,0:T(8,128)(2,1)} %get-tuple-element.16.refs_0_, bf16[256,2048]{1,0:T(8,128)(2,1)} %copy-done, ...), custom_call_target="tpu_custom_call", output_to_operand_aliasing={{0}: (2, {})} | custom-call | flops 6442450944 | bytes 28835840 | tf_op jit(solution)/shard_map/pallas_call | solution.py:63
  117.4 0.8 copy-done.11
  118.3 1.2 collective-permute-start.10
  119.5 1.2 collective-permute-start.9
  120.7 1.8 shard_map.55
  122.6 1.3 collective-permute-start.5
  124.5 18.2 %collective-permute-done.10.refs_11_.refs_2_.refs_12_ = bf16[256,2048]{1,0:T(8,128)(2,1)S(1)} collective-permute-done((bf16[256,2048]{1,0:T(8,128)(2,1)}, bf16[256,2048]{1,0:T(8,128)(2,1)S(1)}, u32[]{:S(2)}, u32[]{:S(2)}) %collective-permute-start.10) | collective-permute-done | bytes 1048608 | tf_op jit(solution)/shard_map/ppermute | solution.py:282
  142.7 1.5 collective-permute-start.8
  144.1 1.3 collective-permute-start.13
  145.4 1.9 slice.55
  147.4 0.8 slice.56
  148.5 1.2 collective-permute-start.12
  149.6 14.1 %shard_map.62 = (bf16[1024,1024]{1,0:T(8,128)(2,1)}, bf16[256,2048]{1,0:T(8,128)(2,1)}) custom-call(bf16[256,4096]{1,0:T(8,128)(2,1)} %all-gather.7.cloned.1.call-done.x_ref, bf16[4096,3072]{1,0:T(8,128)(2,1)} %bitcast.14, bf16[1024,1024]{1,0:T(8,128)(2,1)} %get-tuple-element.18.refs_0_, bf16[256,2048]{1,0:T(8,128)(2,1)} %copy-done, ...), custom_call_target="tpu_custom_call", output_to_operand_aliasing={{0}: (2, {})} | custom-call | flops 6442450944 | bytes 28835840 | tf_op jit(solution)/shard_map/pallas_call | solution.py:63
  163.8 1.1 collective-permute-start.18
  164.9 1.2 collective-permute-start.19
  166.1 1.3 collective-permute-start.16
  167.9 1.2 collective-permute-done.16.refs_8_.refs_18_
  169.5 18.7 %collective-permute-done.18.refs_10_.refs_21_ = bf16[256,2048]{1,0:T(8,128)(2,1)S(1)} collective-permute-done((bf16[256,2048]{1,0:T(8,128)(2,1)}, bf16[256,2048]{1,0:T(8,128)(2,1)S(1)}, u32[]{:S(2)}, u32[]{:S(2)}) %collective-permute-start.18) | collective-permute-done | bytes 1048608 | tf_op jit(solution)/shard_map/ppermute | solution.py:282
  188.2 1.5 collective-permute-start.25
  189.7 1.0 collective-permute-start.26
  190.7 0.9 slice.57
  191.6 0.8 slice.58
  192.4 1.2 collective-permute-start.21
  194.6 1.0 copy-done.9
  196.0 13.6 %shard_map.64 = (bf16[1024,1024]{1,0:T(8,128)(2,1)}, bf16[256,2048]{1,0:T(8,128)(2,1)}) custom-call(bf16[256,4096]{1,0:T(8,128)(2,1)} %all-gather.5.cloned.1.call-done.x_ref, bf16[4096,3072]{1,0:T(8,128)(2,1)} %bitcast.15, bf16[1024,1024]{1,0:T(8,128)(2,1)} %get-tuple-element.20.refs_0_, ...), custom_call_target="tpu_custom_call", output_to_operand_aliasing={{0}: (2, {})} | custom-call | flops 6442450944 | bytes 28835840 | tf_op jit(solution)/shard_map/pallas_call | solution.py:63
  209.6 0.9 collective-permute-start.24
  210.5 1.2 collective-permute-start.23
  211.7 0.9 slice.44
  212.6 1.5 collective-permute-start.20
  214.1 1.9 collective-permute-done.20
  216.5 1.6 slice_select_fusion.1.q_ref
  218.2 0.6 collective-permute-done.29.refs_29_
  218.8 0.8 copy-done.17
  219.7 10.3 %shard_map.66 = (f32[128,512]{1,0:T(8,128)}, f32[128,512]{1,0:T(8,128)}, f32[128,512]{1,0:T(8,128)}) custom-call(s32[1]{0:T(128)} %bitcast.first_ref, bf16[128,512]{1,0:T(8,128)(2,1)} %slice_select_fusion.1.q_ref, bf16[256,2048]{1,0:T(8,128)(2,1)} %get-tuple-element.17.refs_0_, bf16[256,2048]{1,0:T(8,128)(2,1)} %copy-done, bf16[256,2048]{1,0:T(8,128)(2,1)} %copy-done.2, ...), custom_call_target="tpu_custom_call" | custom-call | flops 1610612736 | bytes 12582912 | tf_op jit(solution)/shard_map/pallas_call | solution.py:257
  230.0 4.4 %collective-permute-done.24.refs_2_.refs_32_ = bf16[256,2048]{1,0:T(8,128)(2,1)S(1)} collective-permute-done((bf16[256,2048]{1,0:T(8,128)(2,1)}, bf16[256,2048]{1,0:T(8,128)(2,1)S(1)}, u32[]{:S(2)}, u32[]{:S(2)}) %collective-permute-start.24) | collective-permute-done | bytes 1048608 | tf_op jit(solution)/shard_map/ppermute | solution.py:282
  234.4 0.9 slice.60.refs_0_
  235.8 1.9 slice.59.refs_0_
  237.7 1.2 collective-permute-start.30
  238.9 2.0 collective-permute-start.32
  241.5 6.6 %collective-permute-done.31.refs_4_.refs_34_ = bf16[128,2048]{1,0:T(8,128)(2,1)} collective-permute-done((bf16[128,2048]{1,0:T(8,128)(2,1)}, bf16[128,2048]{1,0:T(8,128)(2,1)}, u32[]{:S(2)}, u32[]{:S(2)}) %collective-permute-start.31) | collective-permute-done | bytes 524320 | tf_op jit(solution)/shard_map/ppermute | solution.py:282
  248.1 2.0 collective-permute-start.36
  250.1 2.2 collective-permute-start.35
  253.4 0.8 collective-permute-done.35.refs_8_.refs_38_
  254.4 6.7 %shard_map.69.refs_40_ = bf16[128,512]{1,0:T(8,128)(2,1)} custom-call(s32[1]{0:T(128)} %bitcast.first_ref, bf16[128,512]{1,0:T(8,128)(2,1)} %slice_select_fusion.1.q_ref, bf16[256,2048]{1,0:T(8,128)(2,1)} %shard_map.65.refs_0_.refs_30_, bf16[256,2048]{1,0:T(8,128)(2,1)} %collective-permute-done.23.refs_1_.refs_31_, bf16[256,2048]{1,0:T(8,128)(2,1)} %copy-done.13, ...), custom_call_target="tpu_custom_call" | custom-call | flops 536870912 | bytes 4194304 | tf_op jit(solution)/shard_map/pallas_call | solution.py:257
  261.1 2.1 collective-permute-start.37
  263.2 18.5 %shard_map.70 = bf16[1024,1024]{1,0:T(8,128)(2,1)} custom-call(s32[1024]{0:T(1024)} %fusion.4.at_ref, bf16[1024,1024]{1,0:T(8,128)(2,1)} %get-tuple-element.22.q_ref, bf16[256,2048]{1,0:T(8,128)(2,1)} %get-tuple-element.17.refs_0_, bf16[256,2048]{1,0:T(8,128)(2,1)} %copy-done, bf16[256,2048]{1,0:T(8,128)(2,1)} %copy-done.2, bf16[128,2048]{1,0:T(8,128)(2,1)} %copy-done.11, ...), custom_call_target="tpu_custom_call" | custom-call | flops 2147483648 | bytes 37748736 | tf_op jit(solution)/shard_map/pallas_call | solution.py:171
  281.7 1.6 slice_bitcast_fusion
  284.3 1.0 fusion
  285.4 1.5 pad_maximum_fusion
  (110 shorter events, 7.4 us)
Async XLA Ops:
  6.5 50.4 %all-gather.11.cloned.1.call-start = ((), (), s32[]{:S(2)}) async-start(), calls=%async_computation.3 | async-start | bytes 2621440 | tf_op jit(solution)/shard_map/all_gather | solution.py:348
  8.4 94.8 %all-gather.9.cloned.1.call-start = ((), (), s32[]{:S(2)}) async-start(), calls=%async_computation.2 | async-start | bytes 2621440 | tf_op jit(solution)/shard_map/all_gather | solution.py:348
  33.9 115.8 %all-gather.7.cloned.1.call-start = ((), (), s32[]{:S(2)}) async-start(), calls=%async_computation.1 | async-start | bytes 2621440 | tf_op jit(solution)/shard_map/all_gather | solution.py:348
  35.8 160.2 %all-gather.5.cloned.1.call-start = ((), (), s32[]{:S(2)}) async-start(), calls=%async_computation | async-start | bytes 2621440 | tf_op jit(solution)/shard_map/all_gather | solution.py:348
  71.1 24.4 %collective-permute-start = (bf16[256,2048]{1,0:T(8,128)(2,1)}, bf16[256,2048]{1,0:T(8,128)(2,1)S(1)}, u32[]{:S(2)}, u32[]{:S(2)}) collective-permute-start(bf16[256,2048]{1,0:T(8,128)(2,1)} %get-tuple-element.17.refs_0_), channel_id=1, source_target_pairs={{0,8},{4,12},{8,0},{12,4},{16,24},{20,28},{24,16},{28,20},{1,9},{5... | collective-permute-start | bytes 3145736 | tf_op jit(solution)/shard_map/ppermute | solution.py:282
  72.3 25.2 %collective-permute-start.1 = (bf16[256,2048]{1,0:T(8,128)(2,1)}, bf16[256,2048]{1,0:T(8,128)(2,1)S(1)}, u32[]{:S(2)}, u32[]{:S(2)}) collective-permute-start(bf16[256,2048]{1,0:T(8,128)(2,1)} %get-tuple-element.17.refs_0_), channel_id=1, source_target_pairs={{0,16},{4,20},{8,24},{12,28},{16,0},{20,4},{24,8},{28,12},{1,17},{... | collective-permute-start | bytes 3145736 | tf_op jit(solution)/shard_map/ppermute | solution.py:282
  73.5 50.6 %collective-permute-start.4 = (bf16[256,2048]{1,0:T(8,128)(2,1)}, bf16[256,2048]{1,0:T(8,128)(2,1)}, u32[]{:S(2)}, u32[]{:S(2)}) collective-permute-start(bf16[256,2048]{1,0:T(8,128)(2,1)} %get-tuple-element.17.refs_0_), channel_id=1, source_target_pairs={{0,4},{4,0},{8,12},{12,8},{16,20},{20,16},{24,28},{28,24},{1,5},{5... | collective-permute-start | bytes 3145736 | tf_op jit(solution)/shard_map/ppermute | solution.py:282
  95.4 7.8 %copy-start = (bf16[256,2048]{1,0:T(8,128)(2,1)}, bf16[256,2048]{1,0:T(8,128)(2,1)S(1)}, u32[]{:S(2)}) copy-start(bf16[256,2048]{1,0:T(8,128)(2,1)S(1)} %collective-permute-done.refs_1_) | copy-start | bytes 3145732
  96.3 21.0 %collective-permute-start.2 = (bf16[128,2048]{1,0:T(8,128)(2,1)}, bf16[128,2048]{1,0:T(8,128)(2,1)S(1)}, u32[]{:S(2)}, u32[]{:S(2)}) collective-permute-start(bf16[128,2048]{1,0:T(8,128)(2,1)} %slice.53), channel_id=1, source_target_pairs={{0,16},{4,20},{8,24},{12,28},{16,0},{20,4},{24,8},{28,12},{1,17},{... | collective-permute-start | bytes 1572872 | tf_op jit(solution)/shard_map/ppermute | solution.py:282
  97.5 5.7 %copy-start.2 = (bf16[256,2048]{1,0:T(8,128)(2,1)}, bf16[256,2048]{1,0:T(8,128)(2,1)S(1)}, u32[]{:S(2)}) copy-start(bf16[256,2048]{1,0:T(8,128)(2,1)S(1)} %collective-permute-done.1.refs_2_) | copy-start | bytes 3145732
  98.4 18.9 %collective-permute-start.3 = (bf16[128,2048]{1,0:T(8,128)(2,1)}, bf16[128,2048]{1,0:T(8,128)(2,1)S(1)}, u32[]{:S(2)}, u32[]{:S(2)}) collective-permute-start(bf16[128,2048]{1,0:T(8,128)(2,1)} %slice.54), channel_id=1, source_target_pairs={{0,8},{4,12},{8,0},{12,4},{16,24},{20,28},{24,16},{28,20},{1,9},{5... | collective-permute-start | bytes 1572872 | tf_op jit(solution)/shard_map/ppermute | solution.py:282
  117.3 0.8 copy-start.11
  117.4 1.0 copy-start.12
  118.3 4.3 %copy-start.1 = (bf16[256,2048]{1,0:T(8,128)(2,1)S(1)}, bf16[256,2048]{1,0:T(8,128)(2,1)}, u32[]{:S(2)}) copy-start(bf16[256,2048]{1,0:T(8,128)(2,1)} %copy-done) | copy-start | bytes 3145732
  118.3 5.6 %copy-start.3 = (bf16[256,2048]{1,0:T(8,128)(2,1)S(1)}, bf16[256,2048]{1,0:T(8,128)(2,1)}, u32[]{:S(2)}) copy-start(bf16[256,2048]{1,0:T(8,128)(2,1)} %copy-done.2) | copy-start | bytes 3145732
  118.3 24.3 %collective-permute-start.10 = (bf16[256,2048]{1,0:T(8,128)(2,1)}, bf16[256,2048]{1,0:T(8,128)(2,1)S(1)}, u32[]{:S(2)}, u32[]{:S(2)}) collective-permute-start(bf16[256,2048]{1,0:T(8,128)(2,1)} %shard_map.61.refs_10_), channel_id=1, source_target_pairs={{0,16},{4,20},{8,24},{12,28},{16,0},{20,4},{24,8},{28,12},{1,17},{... | collective-permute-start | bytes 3145736 | tf_op jit(solution)/shard_map/ppermute | solution.py:282
  119.5 24.6 %collective-permute-start.9 = (bf16[256,2048]{1,0:T(8,128)(2,1)}, bf16[256,2048]{1,0:T(8,128)(2,1)}, u32[]{:S(2)}, u32[]{:S(2)}) collective-permute-start(bf16[256,2048]{1,0:T(8,128)(2,1)} %shard_map.61.refs_10_), channel_id=1, source_target_pairs={{0,8},{4,12},{8,0},{12,4},{16,24},{20,28},{24,16},{28,20},{1,9},{5... | collective-permute-start | bytes 3145736 | tf_op jit(solution)/shard_map/ppermute | solution.py:282
  122.6 27.0 %collective-permute-start.5 = (bf16[256,2048]{1,0:T(8,128)(2,1)S(1)}, bf16[256,2048]{1,0:T(8,128)(2,1)}, u32[]{:S(2)}, u32[]{:S(2)}) collective-permute-start(bf16[256,2048]{1,0:T(8,128)(2,1)S(1)} %copy-done.1), channel_id=1, source_target_pairs={{0,4},{4,0},{8,12},{12,8},{16,20},{20,16},{24,28},{28,24},{1,5},{5... | collective-permute-start | bytes 3145736 | tf_op jit(solution)/shard_map/ppermute | solution.py:282
  124.0 25.7 %collective-permute-start.6 = (bf16[256,2048]{1,0:T(8,128)(2,1)S(1)}, bf16[256,2048]{1,0:T(8,128)(2,1)}, u32[]{:S(2)}, u32[]{:S(2)}) collective-permute-start(bf16[256,2048]{1,0:T(8,128)(2,1)S(1)} %copy-done.3), channel_id=1, source_target_pairs={{0,4},{4,0},{8,12},{12,8},{16,20},{20,16},{24,28},{28,24},{1,5},{5... | collective-permute-start | bytes 3145736 | tf_op jit(solution)/shard_map/ppermute | solution.py:282
  124.0 24.1 %collective-permute-start.7 = (bf16[128,2048]{1,0:T(8,128)(2,1)}, bf16[128,2048]{1,0:T(8,128)(2,1)}, u32[]{:S(2)}, u32[]{:S(2)}) collective-permute-start(bf16[128,2048]{1,0:T(8,128)(2,1)} %copy-done.11), channel_id=1, source_target_pairs={{0,4},{4,0},{8,12},{12,8},{16,20},{20,16},{24,28},{28,24},{1,5},{5... | collective-permute-start | bytes 1572872 | tf_op jit(solution)/shard_map/ppermute | solution.py:282
  142.6 7.0 %copy-start.4 = (bf16[256,2048]{1,0:T(8,128)(2,1)}, bf16[256,2048]{1,0:T(8,128)(2,1)S(1)}, u32[]{:S(2)}) copy-start(bf16[256,2048]{1,0:T(8,128)(2,1)S(1)} %collective-permute-done.10.refs_11_.refs_2_.refs_12_) | copy-start | bytes 3145732
  142.7 5.8 %collective-permute-start.8 = (bf16[128,2048]{1,0:T(8,128)(2,1)}, bf16[128,2048]{1,0:T(8,128)(2,1)}, u32[]{:S(2)}, u32[]{:S(2)}) collective-permute-start(bf16[128,2048]{1,0:T(8,128)(2,1)} %copy-done.12), channel_id=1, source_target_pairs={{0,4},{4,0},{8,12},{12,8},{16,20},{20,16},{24,28},{28,24},{1,5},{5... | collective-permute-start | bytes 1572872 | tf_op jit(solution)/shard_map/ppermute | solution.py:282
  144.1 23.2 %collective-permute-start.13 = (bf16[256,2048]{1,0:T(8,128)(2,1)}, bf16[256,2048]{1,0:T(8,128)(2,1)}, u32[]{:S(2)}, u32[]{:S(2)}) collective-permute-start(bf16[256,2048]{1,0:T(8,128)(2,1)} %shard_map.61.refs_10_), channel_id=1, source_target_pairs={{0,4},{4,0},{8,12},{12,8},{16,20},{20,16},{24,28},{28,24},{1,5},{5... | collective-permute-start | bytes 3145736 | tf_op jit(solution)/shard_map/ppermute | solution.py:282
  148.2 15.6 %collective-permute-start.11 = (bf16[128,2048]{1,0:T(8,128)(2,1)}, bf16[128,2048]{1,0:T(8,128)(2,1)}, u32[]{:S(2)}, u32[]{:S(2)}) collective-permute-start(bf16[128,2048]{1,0:T(8,128)(2,1)} %slice.55), channel_id=1, source_target_pairs={{0,16},{4,20},{8,24},{12,28},{16,0},{20,4},{24,8},{28,12},{1,17},{... | collective-permute-start | bytes 1572872 | tf_op jit(solution)/shard_map/ppermute | solution.py:282
  148.5 15.3 %collective-permute-start.12 = (bf16[128,2048]{1,0:T(8,128)(2,1)}, bf16[128,2048]{1,0:T(8,128)(2,1)}, u32[]{:S(2)}, u32[]{:S(2)}) collective-permute-start(bf16[128,2048]{1,0:T(8,128)(2,1)} %slice.56), channel_id=1, source_target_pairs={{0,8},{4,12},{8,0},{12,4},{16,24},{20,28},{24,16},{28,20},{1,9},{5... | collective-permute-start | bytes 1572872 | tf_op jit(solution)/shard_map/ppermute | solution.py:282
  163.8 3.6 %copy-start.5 = (bf16[256,2048]{1,0:T(8,128)(2,1)S(1)}, bf16[256,2048]{1,0:T(8,128)(2,1)}, u32[]{:S(2)}) copy-start(bf16[256,2048]{1,0:T(8,128)(2,1)} %copy-done.4) | copy-start | bytes 3145732
  163.8 24.4 %collective-permute-start.18 = (bf16[256,2048]{1,0:T(8,128)(2,1)}, bf16[256,2048]{1,0:T(8,128)(2,1)S(1)}, u32[]{:S(2)}, u32[]{:S(2)}) collective-permute-start(bf16[256,2048]{1,0:T(8,128)(2,1)} %shard_map.63.refs_20_), channel_id=1, source_target_pairs={{0,8},{4,12},{8,0},{12,4},{16,24},{20,28},{24,16},{28,20},{1,9},{5... | collective-permute-start | bytes 3145736 | tf_op jit(solution)/shard_map/ppermute | solution.py:282
  164.9 24.8 %collective-permute-start.19 = (bf16[256,2048]{1,0:T(8,128)(2,1)}, bf16[256,2048]{1,0:T(8,128)(2,1)S(1)}, u32[]{:S(2)}, u32[]{:S(2)}) collective-permute-start(bf16[256,2048]{1,0:T(8,128)(2,1)} %shard_map.63.refs_20_), channel_id=1, source_target_pairs={{0,16},{4,20},{8,24},{12,28},{16,0},{20,4},{24,8},{28,12},{1,17},{... | collective-permute-start | bytes 3145736 | tf_op jit(solution)/shard_map/ppermute | solution.py:282
  166.1 3.0 %collective-permute-start.16 = (bf16[128,2048]{1,0:T(8,128)(2,1)}, bf16[128,2048]{1,0:T(8,128)(2,1)S(1)}, u32[]{:S(2)}, u32[]{:S(2)}) collective-permute-start(bf16[128,2048]{1,0:T(8,128)(2,1)} %collective-permute-done.11.refs_1_.refs_3_.refs_13_), channel_id=1, source_target_pairs={{0,4},{4,0},{8,12},{12,8},{16,20},{20,16},{24,28},{28,24},{1,5},{5... | collective-permute-start | bytes 1572872 | tf_op jit(solution)/shard_map/ppermute | solution.py:282
  167.3 26.2 %collective-permute-start.14 = (bf16[256,2048]{1,0:T(8,128)(2,1)}, bf16[256,2048]{1,0:T(8,128)(2,1)S(1)}, u32[]{:S(2)}, u32[]{:S(2)}) collective-permute-start(bf16[256,2048]{1,0:T(8,128)(2,1)} %collective-permute-done.9.refs_10_.refs_1_.refs_11_), channel_id=1, source_target_pairs={{0,4},{4,0},{8,12},{12,8},{16,20},{20,16},{24,28},{28,24},{1,5},{5... | collective-permute-start | bytes 3145736 | tf_op jit(solution)/shard_map/ppermute | solution.py:282
  167.4 26.7 %collective-permute-start.15 = (bf16[256,2048]{1,0:T(8,128)(2,1)S(1)}, bf16[256,2048]{1,0:T(8,128)(2,1)S(1)}, u32[]{:S(2)}, u32[]{:S(2)}) collective-permute-start(bf16[256,2048]{1,0:T(8,128)(2,1)S(1)} %copy-done.5), channel_id=1, source_target_pairs={{0,4},{4,0},{8,12},{12,8},{16,20},{20,16},{24,28},{28,24},{1,5},{5... | collective-permute-start | bytes 3145736 | tf_op jit(solution)/shard_map/ppermute | solution.py:282
  169.1 20.6 %copy-start.14 = (bf16[128,2048]{1,0:T(8,128)(2,1)}, bf16[128,2048]{1,0:T(8,128)(2,1)S(1)}, u32[]{:S(2)}) copy-start(bf16[128,2048]{1,0:T(8,128)(2,1)S(1)} %collective-permute-done.16.refs_8_.refs_18_) | copy-start | bytes 1572868
  169.1 23.3 %collective-permute-start.17 = (bf16[128,2048]{1,0:T(8,128)(2,1)}, bf16[128,2048]{1,0:T(8,128)(2,1)S(1)}, u32[]{:S(2)}, u32[]{:S(2)}) collective-permute-start(bf16[128,2048]{1,0:T(8,128)(2,1)} %collective-permute-done.12.refs_2_.refs_4_.refs_14_), channel_id=1, source_target_pairs={{0,4},{4,0},{8,12},{12,8},{16,20},{20,16},{24,28},{28,24},{1,5},{5... | collective-permute-start | bytes 1572872 | tf_op jit(solution)/shard_map/ppermute | solution.py:282
  188.2 7.8 %copy-start.6 = (bf16[256,2048]{1,0:T(8,128)(2,1)}, bf16[256,2048]{1,0:T(8,128)(2,1)S(1)}, u32[]{:S(2)}) copy-start(bf16[256,2048]{1,0:T(8,128)(2,1)S(1)} %collective-permute-done.18.refs_10_.refs_21_) | copy-start | bytes 3145732
  188.2 24.4 %collective-permute-start.25 = (bf16[256,2048]{1,0:T(8,128)(2,1)}, bf16[256,2048]{1,0:T(8,128)(2,1)}, u32[]{:S(2)}, u32[]{:S(2)}) collective-permute-start(bf16[256,2048]{1,0:T(8,128)(2,1)} %shard_map.63.refs_20_), channel_id=1, source_target_pairs={{0,4},{4,0},{8,12},{12,8},{16,20},{20,16},{24,28},{28,24},{1,5},{5... | collective-permute-start | bytes 3145736 | tf_op jit(solution)/shard_map/ppermute | solution.py:282
  189.7 6.3 %copy-start.7 = (bf16[256,2048]{1,0:T(8,128)(2,1)}, bf16[256,2048]{1,0:T(8,128)(2,1)S(1)}, u32[]{:S(2)}) copy-start(bf16[256,2048]{1,0:T(8,128)(2,1)S(1)} %collective-permute-done.19.refs_11_.refs_22_) | copy-start | bytes 3145732
  189.7 26.5 %collective-permute-start.26 = (bf16[256,2048]{1,0:T(8,128)(2,1)S(1)}, bf16[256,2048]{1,0:T(8,128)(2,1)}, u32[]{:S(2)}, u32[]{:S(2)}) collective-permute-start(bf16[256,2048]{1,0:T(8,128)(2,1)S(1)} %collective-permute-done.18.refs_10_.refs_21_), channel_id=1, source_target_pairs={{0,4},{4,0},{8,12},{12,8},{16,20},{20,16},{24,28},{28,24},{1,5},{5... | collective-permute-start | bytes 3145736 | tf_op jit(solution)/shard_map/ppermute | solution.py:282
  192.4 1.7 copy-start.15
  192.4 17.2 %collective-permute-start.21 = (bf16[128,2048]{1,0:T(8,128)(2,1)}, bf16[128,2048]{1,0:T(8,128)(2,1)}, u32[]{:S(2)}, u32[]{:S(2)}) collective-permute-start(bf16[128,2048]{1,0:T(8,128)(2,1)} %slice.57), channel_id=1, source_target_pairs={{0,16},{4,20},{8,24},{12,28},{16,0},{20,4},{24,8},{28,12},{1,17},{... | collective-permute-start | bytes 1572872 | tf_op jit(solution)/shard_map/ppermute | solution.py:282
  193.6 1.0 copy-start.8
  193.6 16.0 %collective-permute-start.22 = (bf16[128,2048]{1,0:T(8,128)(2,1)}, bf16[128,2048]{1,0:T(8,128)(2,1)}, u32[]{:S(2)}, u32[]{:S(2)}) collective-permute-start(bf16[128,2048]{1,0:T(8,128)(2,1)} %slice.58), channel_id=1, source_target_pairs={{0,8},{4,12},{8,0},{12,4},{16,24},{20,28},{24,16},{28,20},{1,9},{5... | collective-permute-start | bytes 1572872 | tf_op jit(solution)/shard_map/ppermute | solution.py:282
  194.6 1.1 copy-start.9
  195.6 22.5 %collective-permute-start.27 = (bf16[256,2048]{1,0:T(8,128)(2,1)S(1)}, bf16[256,2048]{1,0:T(8,128)(2,1)}, u32[]{:S(2)}, u32[]{:S(2)}) collective-permute-start(bf16[256,2048]{1,0:T(8,128)(2,1)S(1)} %collective-permute-done.19.refs_11_.refs_22_), channel_id=1, source_target_pairs={{0,4},{4,0},{8,12},{12,8},{16,20},{20,16},{24,28},{28,24},{1,5},{5... | collective-permute-start | bytes 3145736 | tf_op jit(solution)/shard_map/ppermute | solution.py:282
  209.6 24.8 %collective-permute-start.24 = (bf16[256,2048]{1,0:T(8,128)(2,1)}, bf16[256,2048]{1,0:T(8,128)(2,1)S(1)}, u32[]{:S(2)}, u32[]{:S(2)}) collective-permute-start(bf16[256,2048]{1,0:T(8,128)(2,1)} %shard_map.65.refs_0_.refs_30_), channel_id=1, source_target_pairs={{0,16},{4,20},{8,24},{12,28},{16,0},{20,4},{24,8},{28,12},{1,17},{... | collective-permute-start | bytes 3145736 | tf_op jit(solution)/shard_map/ppermute | solution.py:282
  210.5 25.3 %collective-permute-start.23 = (bf16[256,2048]{1,0:T(8,128)(2,1)}, bf16[256,2048]{1,0:T(8,128)(2,1)}, u32[]{:S(2)}, u32[]{:S(2)}) collective-permute-start(bf16[256,2048]{1,0:T(8,128)(2,1)} %shard_map.65.refs_0_.refs_30_), channel_id=1, source_target_pairs={{0,8},{4,12},{8,0},{12,4},{16,24},{20,28},{24,16},{28,20},{1,9},{5... | collective-permute-start | bytes 3145736 | tf_op jit(solution)/shard_map/ppermute | solution.py:282
  212.6 3.4 %collective-permute-start.20 = (bf16[128,512]{1,0:T(8,128)(2,1)S(1)}, bf16[128,512]{1,0:T(8,128)(2,1)S(1)}, u32[]{:S(2)}, u32[]{:S(2)}) collective-permute-start(bf16[128,512]{1,0:T(8,128)(2,1)S(1)} %slice.44), channel_id=1, source_target_pairs={{0,4},{1,5},{2,6},{3,7}} | collective-permute-start | bytes 393224 | tf_op jit(solution)/shard_map/ppermute | solution.py:408
  216.0 2.3 collective-permute-start.28
  216.1 2.7 collective-permute-start.29
  218.8 0.8 copy-start.17
  234.4 6.5 %copy-start.13 = (bf16[256,2048]{1,0:T(8,128)(2,1)}, bf16[256,2048]{1,0:T(8,128)(2,1)S(1)}, u32[]{:S(2)}) copy-start(bf16[256,2048]{1,0:T(8,128)(2,1)S(1)} %collective-permute-done.24.refs_2_.refs_32_) | copy-start | bytes 3145732
  235.3 3.5 %copy-start.10 = (bf16[256,2048]{1,0:T(8,128)(2,1)S(1)}, bf16[256,2048]{1,0:T(8,128)(2,1)}, u32[]{:S(2)}) copy-start(bf16[256,2048]{1,0:T(8,128)(2,1)} %shard_map.65.refs_0_.refs_30_) | copy-start | bytes 3145732
  235.3 6.1 %copy-start.21 = (s32[3]{0:T(128)S(1)}, s32[3]{0:T(128)}, u32[]{:S(2)}) copy-start(s32[3]{0:T(128)} %constant.58.clone) | copy-start | bytes 40
  235.3 17.0 %copy-start.19 = (s32[8,128,3]{1,0,2:T(8,128)S(1)}, s32[8,128,3]{1,0,2:T(8,128)}, u32[]{:S(2)}) copy-start(s32[8,128,3]{1,0,2:T(8,128)} %param.8) | copy-start | bytes 36868
  235.3 17.0 %copy-start.20 = (s32[8,128,3]{1,0,2:T(8,128)S(1)}, s32[8,128,3]{1,0,2:T(8,128)}, u32[]{:S(2)}) copy-start(s32[8,128,3]{1,0,2:T(8,128)} %param.7) | copy-start | bytes 36868
  235.4 12.7 %collective-permute-start.31 = (bf16[128,2048]{1,0:T(8,128)(2,1)}, bf16[128,2048]{1,0:T(8,128)(2,1)}, u32[]{:S(2)}, u32[]{:S(2)}) collective-permute-start(bf16[128,2048]{1,0:T(8,128)(2,1)} %shard_map.68), channel_id=1, source_target_pairs={{0,8},{4,12},{8,0},{12,4},{16,24},{20,28},{24,16},{28,20},{1,9},{5... | collective-permute-start | bytes 1572872 | tf_op jit(solution)/shard_map/ppermute | solution.py:282
  237.7 12.4 %collective-permute-start.30 = (bf16[128,2048]{1,0:T(8,128)(2,1)}, bf16[128,2048]{1,0:T(8,128)(2,1)}, u32[]{:S(2)}, u32[]{:S(2)}) collective-permute-start(bf16[128,2048]{1,0:T(8,128)(2,1)} %shard_map.67), channel_id=1, source_target_pairs={{0,16},{4,20},{8,24},{12,28},{16,0},{20,4},{24,8},{28,12},{1,17},{... | collective-permute-start | bytes 1572872 | tf_op jit(solution)/shard_map/ppermute | solution.py:282
  238.9 14.5 %collective-permute-start.32 = (bf16[256,2048]{1,0:T(8,128)(2,1)S(1)}, bf16[256,2048]{1,0:T(8,128)(2,1)S(1)}, u32[]{:S(2)}, u32[]{:S(2)}) collective-permute-start(bf16[256,2048]{1,0:T(8,128)(2,1)S(1)} %copy-done.10), channel_id=1, source_target_pairs={{0,4},{4,0},{8,12},{12,8},{16,20},{20,16},{24,28},{28,24},{1,5},{5... | collective-permute-start | bytes 3145736 | tf_op jit(solution)/shard_map/ppermute | solution.py:282
  240.9 12.5 %collective-permute-start.33 = (bf16[256,2048]{1,0:T(8,128)(2,1)}, bf16[256,2048]{1,0:T(8,128)(2,1)}, u32[]{:S(2)}, u32[]{:S(2)}) collective-permute-start(bf16[256,2048]{1,0:T(8,128)(2,1)} %collective-permute-done.23.refs_1_.refs_31_), channel_id=1, source_target_pairs={{0,4},{4,0},{8,12},{12,8},{16,20},{20,16},{24,28},{28,24},{1,5},{5... | collective-permute-start | bytes 3145736 | tf_op jit(solution)/shard_map/ppermute | solution.py:282
  240.9 12.5 %collective-permute-start.34 = (bf16[256,2048]{1,0:T(8,128)(2,1)S(1)}, bf16[256,2048]{1,0:T(8,128)(2,1)}, u32[]{:S(2)}, u32[]{:S(2)}) collective-permute-start(bf16[256,2048]{1,0:T(8,128)(2,1)S(1)} %collective-permute-done.24.refs_2_.refs_32_), channel_id=1, source_target_pairs={{0,4},{4,0},{8,12},{12,8},{16,20},{20,16},{24,28},{28,24},{1,5},{5... | collective-permute-start | bytes 3145736 | tf_op jit(solution)/shard_map/ppermute | solution.py:282
  248.1 5.3 %collective-permute-start.36 = (bf16[128,2048]{1,0:T(8,128)(2,1)}, bf16[128,2048]{1,0:T(8,128)(2,1)}, u32[]{:S(2)}, u32[]{:S(2)}) collective-permute-start(bf16[128,2048]{1,0:T(8,128)(2,1)} %collective-permute-done.31.refs_4_.refs_34_), channel_id=1, source_target_pairs={{0,4},{4,0},{8,12},{12,8},{16,20},{20,16},{24,28},{28,24},{1,5},{5... | collective-permute-start | bytes 1572872 | tf_op jit(solution)/shard_map/ppermute | solution.py:282
  250.1 4.1 %collective-permute-start.35 = (bf16[128,2048]{1,0:T(8,128)(2,1)}, bf16[128,2048]{1,0:T(8,128)(2,1)}, u32[]{:S(2)}, u32[]{:S(2)}) collective-permute-start(bf16[128,2048]{1,0:T(8,128)(2,1)} %collective-permute-done.30.refs_3_.refs_33_), channel_id=1, source_target_pairs={{0,4},{4,0},{8,12},{12,8},{16,20},{20,16},{24,28},{28,24},{1,5},{5... | collective-permute-start | bytes 1572872 | tf_op jit(solution)/shard_map/ppermute | solution.py:282
  253.4 1.0 copy-start.16
  261.1 22.8 %collective-permute-start.37 = (bf16[128,512]{1,0:T(8,128)(2,1)}, bf16[128,512]{1,0:T(8,128)(2,1)S(1)}, u32[]{:S(2)}, u32[]{:S(2)}) collective-permute-start(bf16[128,512]{1,0:T(8,128)(2,1)} %shard_map.69.refs_40_), channel_id=1, source_target_pairs={{4,0},{5,1},{6,2},{7,3}} | collective-permute-start | bytes 393224 | tf_op jit(solution)/shard_map/ppermute | solution.py:416
  283.4 0.9 copy-start.18
Sparse Core Ops, SparseCore 0:
  8.9 47.9 all-gather.10
  58.5 44.6 all-gather.8
  104.8 44.6 all-gather.6
  150.9 44.6 all-gather.4

commit v4 on v3

--- a/solution.py
+++ b/solution.py
@@ -18,69 +18,38 @@
 PARTS = (4, 4, 4, 4)
 GROUPS = (0, 1, 2, 3)
 TOGETHER = 16
-PER = 2
+COLUMNS = 512
 VMEM = 60 << 20
 TRANSPOSED = (((1,), (1,)), ((), ()))
 
 
-def project_kernel(start, x_ref, w_ref, *refs):
-    q_ref, kv_ref, hold_ref, sem = refs[-4:]
-    step = pl.program_id(0)
-    rows = x_ref.shape[0]
-    out = jnp.dot(x_ref[...], w_ref[...], preferred_element_type=jnp.float32).astype(jnp.bfloat16)
-    per = out.shape[1] // (3 * HEAD_DIMENSION)
-    for i in range(per):
-        at = i * 3 * HEAD_DIMENSION
-        hold_ref[step, :, i * HEAD_DIMENSION : (i + 1) * HEAD_DIMENSION] = out[
-            :, at : at + HEAD_DIMENSION
-        ]
-        kv_ref[:, 2 * i * HEAD_DIMENSION : 2 * (i + 1) * HEAD_DIMENSION] = out[
-            :, at + HEAD_DIMENSION : at + 3 * HEAD_DIMENSION
-        ]
-    width = per * HEAD_DIMENSION
-    copies = [
-        pltpu.make_async_copy(
-            hold_ref.at[i], q_ref.at[pl.ds(start, rows), pl.ds(i * width, width)], sem
-        )
-        for i in range(hold_ref.shape[0])
-    ]
-    for i, copy in enumerate(copies):
-        pl.when(step == i)(copy.start)
-
-    @pl.when(step == len(copies) - 1)
-    def _():
-        for copy in copies:
-            copy.wait()
-
-
-def project(x, begin, rows, weight, queries, start, total, after):
-    depth = x.shape[1]
-    assert begin % rows == 0
-    heads = weight.shape[1] // (3 * HEAD_DIMENSION)
-    per = PER
-    given = () if queries is None else (queries,)
+def project_kernel(x_ref, w_ref, *refs):
+    o_ref = refs[-1]
+    out = jnp.dot(x_ref[...], w_ref[...], preferred_element_type=jnp.float32)
+    o_ref[...] = out.astype(jnp.bfloat16)
+
+
+def project(x, weight, into, start, total, after):
+    rows, depth = x.shape
+    columns = weight.shape[1]
+    wide = min(COLUMNS, columns)
+    assert start % rows == 0
+    given = () if into is None else (into,)
     anywhere = pl.BlockSpec(memory_space=pl.ANY)
     return pl.pallas_call(
-        functools.partial(project_kernel, start),
-        grid=(heads // per,),
+        project_kernel,
+        grid=(columns // wide,),
         in_specs=[
-            pl.BlockSpec((rows, depth), lambda i: (begin // rows, 0)),
-            pl.BlockSpec((depth, per * 3 * HEAD_DIMENSION), lambda i: (0, i)),
+            pl.BlockSpec((rows, depth), lambda i: (0, 0)),
+            pl.BlockSpec((depth, wide), lambda i: (0, i)),
         ]
         + [anywhere] * (len(given) + len(after)),
-        out_specs=[anywhere, pl.BlockSpec((rows, per * 2 * HEAD_DIMENSION), lambda i: (0, i))],
-        out_shape=[
-            jax.ShapeDtypeStruct((total, heads * HEAD_DIMENSION), jnp.bfloat16),
-            jax.ShapeDtypeStruct((rows, heads * 2 * HEAD_DIMENSION), jnp.bfloat16),
-        ],
-        scratch_shapes=[
-            pltpu.VMEM((heads // per, rows, per * HEAD_DIMENSION), jnp.bfloat16),
-            pltpu.SemaphoreType.DMA(()),
-        ],
+        out_specs=pl.BlockSpec((rows, wide), lambda i: (start // rows, i)),
+        out_shape=jax.ShapeDtypeStruct((total, columns), jnp.bfloat16),
         input_output_aliases={2: 0} if given else {},
         cost_estimate=pl.CostEstimate(
-            flops=2 * rows * depth * weight.shape[1],
-            bytes_accessed=2 * (rows * depth + (depth + rows) * weight.shape[1]),
+            flops=2 * rows * depth * columns,
+            bytes_accessed=2 * (rows * depth + (depth + rows) * columns),
             transcendentals=0,
         ),
         compiler_params=pltpu.CompilerParams(vmem_limit_bytes=VMEM),
@@ -358,7 +327,8 @@
     count = lax.axis_size("ctx")
     me = lax.axis_index("ctx")
     span = rows * count
-    weight = proj_weight.reshape(depth, heads * 3 * HEAD_DIMENSION)
+    weight_q = proj_weight[..., :HEAD_DIMENSION].reshape(depth, heads * HEAD_DIMENSION)
+    weight_kv = proj_weight[..., HEAD_DIMENSION:].reshape(depth, heads * 2 * HEAD_DIMENSION)
 
     mine = me * blocks + jnp.arange(blocks)
     near = (mine[:, None] + jnp.array([-1, 0, 1])) % (count * blocks)
@@ -396,20 +366,29 @@
         return sources, places, span
 
     at = at.reshape(-1)
-    for part, (x, begin) in enumerate(gather_features(tokens, weight, sizes)):
+    for part, (x, begin) in enumerate(gather_features(tokens, weight_kv, sizes)):
         fresh = part == 0 or GROUPS[part] > GROUPS[part - 1]
         near, far = parts[-1][1:] if parts else ([], [])
         settled = [cells for run, _, cells in parts[-2][0] if run] if part > 1 else []
-        queries, keyval = project(
-            x, begin, sizes[part], weight, queries, start, rows, settled + (near if fresh else [])
+        settled = settled + [lead_queries] * (part == 2)
+        keyval = project(
+            x,
+            weight_kv,
+            None,
+            0,
+            sizes[part],
+            settled + (near if fresh else []) + ([] if queries is None or part == len(sizes) - 1 else [queries]),
         )
         ready, before = (far, []) if fresh else (near, far)
-        if part == len(sizes) - 1:
+        keyval = after(keyval, *ready) if ready else keyval
+        queries = project(x, weight_q, queries, start, rows, [keyval])
+        if part == 0:
             got = lax.ppermute(queries[:LEAD, half:], "ctx", [(0, 1)])
             lead_queries = jnp.where(me == 1, got, queries[:LEAD, :half])
+        if part == len(sizes) - 1:
             given = lead(first, lead_queries, *placed(range(part)), (), False)
             before = [given[0]] + before
-        parts.append(spread(keyval, count, ready, before))
+        parts.append(spread(keyval, count, (), before))
         start += sizes[part]
 
     lead_own = lead(first, lead_queries, *placed([len(sizes) - 1]), given, True)

time: 295 us -> 304 us (1.031)
  Pallas kernels: 98.9 us -> 108 us
  local copies, waits for them, and re-layouts: 39.9 us -> 48.3 us
  waiting for transfers between devices: 98.1 us -> 89.7 us
    ppermute x36, waiting for transfers between devices: 71.4 us -> 57.9 us  [crossed(): return lax.ppermute(cells, 'ctx', [(i, i ^ bit) for i in range(count)])]
    slice x0 -> x3, local copies, waits for them, and re-layouts: none -> 12.9 us  [the longest x1 7.1 us: per_device(): proj_weight[..., :HEAD_DIMENSION].reshape(depth, heads * HEAD_DIMENSION)]
    pallas_call x4 -> x8, Pallas kernels: 56 us -> 64.9 us  [project(): pl.pallas_call(project_kernel, grid=(columns // wide,), in_specs=[pl.Bloc...]
    all_gather x4, waiting for transfers between devices: 24.7 us -> 31.2 us  [gather_features(): full = lax.all_gather(own, 'head', axis=1, tiled=True)]
    unnamed x48 -> x49, local copies, waits for them, and re-layouts: 29.7 us -> 25.3 us
  transfers between devices with their start and end apart: 42 -> 42, of which waited for: 12 -> 12; matrix products, arithmetic and copies ran while one was open for 13% -> 13% of each run, Pallas kernels for 31% -> 33%
where the time goes in v4:
time: 304 us; the launch traced here: 302 us
  Pallas kernels  108 us (36%)
  waiting for transfers between devices  89.7 us (30%)
  local copies, waits for them, and re-layouts  48.3 us (16%)
  starting transfers between devices  38.3 us (13%)
  between operations  13.4 us (4%)
  other arithmetic  5.02 us (2%)
    pallas_call x8, Pallas kernels, project(): pl.pallas_call(project_kernel, grid=(columns // wide,), in_specs=[pl.Bloc...  64.9 us
    ppermute x36, waiting for transfers between devices, crossed(): return lax.ppermute(cells, 'ctx', [(i, i ^ bit) for i in range(count)])  57.9 us
    ppermute x36, starting transfers between devices, crossed(): return lax.ppermute(cells, 'ctx', [(i, i ^ bit) for i in range(count)])  34.8 us
    all_gather x4, waiting for transfers between devices, gather_features(): full = lax.all_gather(own, 'head', axis=1, tiled=True)  31.2 us
    unnamed x49, local copies, waits for them, and re-layouts  25.3 us
    pallas_call x1, Pallas kernels, sparse(): pl.pallas_call(functools.partial(sparse_kernel, places, heads, rows // BL...  18.5 us
    pallas_call x2, Pallas kernels, lead(): pl.pallas_call(functools.partial(lead_kernel, places, step, heads, not gi...  16.9 us
    slice x8, local copies, waits for them, and re-layouts, halves(): return (cells[:half], cells[half:])  8.94 us
  transfers between devices with their start and end apart: 42, of which 12 were waited for; matrix products, arithmetic and copies ran while one was open for 13% of the time, Pallas kernels for 33%

profile of v4, /device:TPU:1, one launch (start us, length us, event | category | flops | bytes accessed | tf_op | source)
XLA Modules:
  0.0 302.5 jit_solution(10236409760017074725)
XLA Ops:
  6.5 1.8 shard_map.55
  8.5 5.8 %slice-done = bf16[4096,8,256]{2,1,0:T(8,128)(2,1)S(1)} async-done(((bf16[4096,8,384]{2,1,0:T(8,128)(2,1)}), bf16[4096,8,256]{2,1,0:T(8,128)(2,1)S(1)}, s32[]{:S(2)}) %slice-start) | async-done | bytes 16777240 | tf_op jit(solution)/shard_map/slice | solution.py:331
  14.3 9.8 %copy.17 = bf16[512,8,8,256]{3,1,2,0:T(8,128)(2,1)} copy(bf16[512,8,8,256]{3,2,1,0:T(8,128)(2,1)S(1)} %bitcast.24) | data formatting | bytes 33554432
  24.1 1.9 shard_map.59
  26.0 1.9 shard_map.62
  28.0 29.0 %all-gather.5.cloned.1.call-done.x_ref = bf16[256,4096]{1,0:T(8,128)(2,1)} async-done(((bf16[256,1024]{1,0:T(8,128)(2,1)}), bf16[256,4096]{1,0:T(8,128)(2,1)}) %all-gather.5.cloned.1.call-update) | async-done | bytes 2097168 | tf_op jit(solution)/shard_map/all_gather | solution.py:317
  56.9 10.1 %shard_map.56.refs_0_ = bf16[256,2048]{1,0:T(8,128)(2,1)} custom-call(bf16[256,4096]{1,0:T(8,128)(2,1)} %all-gather.5.cloned.1.call-done.x_ref, bf16[4096,2048]{1,0:T(8,128)(2,1)} %bitcast.15), custom_call_target="tpu_custom_call" | custom-call | flops 4294967296 | bytes 19922944 | tf_op jit(solution)/shard_map/pallas_call | solution.py:39
  67.1 1.1 collective-permute-start.1
  68.2 1.2 collective-permute-start.2
  69.4 7.1 %slice.46 = bf16[4096,8,128]{2,1,0:T(8,128)(2,1)} slice(bf16[4096,8,384]{2,1,0:T(8,128)(2,1)} %param.6), slice={[0:4096], [0:8], [0:128]} | slice | bytes 16777216 | tf_op jit(solution)/shard_map/slice | solution.py:330
  76.5 8.9 %copy.21 = bf16[512,8,8,128]{3,1,2,0:T(8,128)(2,1)} copy(bf16[512,8,8,128]{3,2,1,0:T(8,128)(2,1)} %bitcast.25) | data formatting | bytes 16777216
  85.4 5.8 %collective-permute-done.1.refs_0_.refs_1_ = bf16[256,2048]{1,0:T(8,128)(2,1)S(1)} collective-permute-done((bf16[256,2048]{1,0:T(8,128)(2,1)}, bf16[256,2048]{1,0:T(8,128)(2,1)S(1)}, u32[]{:S(2)}, u32[]{:S(2)}) %collective-permute-start.1) | collective-permute-done | bytes 1048608 | tf_op jit(solution)/shard_map/ppermute | solution.py:251
  91.2 0.9 slice.63
  92.1 1.2 collective-permute-start.3
  93.3 0.9 slice.64
  94.2 1.2 collective-permute-start.4
  95.4 6.1 %shard_map.57.refs_2_.refs_0_ = bf16[1024,1024]{1,0:T(8,128)(2,1)} custom-call(bf16[256,4096]{1,0:T(8,128)(2,1)} %all-gather.5.cloned.1.call-done.x_ref, bf16[4096,1024]{1,0:T(8,128)(2,1)} %bitcast.20, bf16[256,2048]{1,0:T(8,128)(2,1)} %shard_map.56.refs_0_), custom_call_target="tpu_custom_call" | custom-call | flops 2147483648 | bytes 11010048 | tf_op jit(solution)/shard_map/pallas_call | solution.py:39
  101.4 1.8 all-gather.9.cloned.1.call-done.x_ref
  103.2 10.1 %shard_map.60.refs_0_ = bf16[256,2048]{1,0:T(8,128)(2,1)} custom-call(bf16[256,4096]{1,0:T(8,128)(2,1)} %all-gather.9.cloned.1.call-done.x_ref, bf16[4096,2048]{1,0:T(8,128)(2,1)} %bitcast.16, bf16[256,2048]{1,0:T(8,128)(2,1)} %copy-done.2, bf16[256,2048]{1,0:T(8,128)(2,1)} %copy-done.4, bf16[1024,1024]{1,0:T(8,128)(2,1)} %shard_map.57.refs_2_.refs_0_), custom_call_target="tpu_custom_call" | custom-call | flops 4294967296 | bytes 19922944 | tf_op jit(solution)/shard_map/pallas_call | solution.py:39
  115.0 1.1 collective-permute-start.5
  116.1 1.2 collective-permute-start.6
  117.3 1.9 shard_map.58
  119.2 1.4 collective-permute-start.14
  120.6 0.9 slice.61
  121.5 1.5 collective-permute-start
  123.0 1.2 collective-permute-start.15
  124.9 14.3 %collective-permute-done.5.refs_10_.refs_0_.refs_11_ = bf16[256,2048]{1,0:T(8,128)(2,1)S(1)} collective-permute-done((bf16[256,2048]{1,0:T(8,128)(2,1)}, bf16[256,2048]{1,0:T(8,128)(2,1)S(1)}, u32[]{:S(2)}, u32[]{:S(2)}) %collective-permute-start.5) | collective-permute-done | bytes 1048608 | tf_op jit(solution)/shard_map/ppermute | solution.py:251
  139.2 1.6 collective-permute-start.17
  140.8 1.2 collective-permute-start.18
  142.0 1.6 slice_select_fusion.1.refs_9_.q_ref
  143.6 0.8 slice.65
  144.4 1.9 slice.66
  146.3 1.2 collective-permute-start.7
  147.8 6.1 %shard_map.63.refs_12_.refs_0_ = bf16[1024,1024]{1,0:T(8,128)(2,1)} custom-call(bf16[256,4096]{1,0:T(8,128)(2,1)} %all-gather.9.cloned.1.call-done.x_ref, bf16[4096,1024]{1,0:T(8,128)(2,1)} %bitcast.21, bf16[1024,1024]{1,0:T(8,128)(2,1)} %shard_map.57.refs_2_.refs_0_, bf16[256,2048]{1,0:T(8,128)(2,1)} %shard_map.61.refs_1_.refs_10_), custom_call_target="tpu_custom_call", output_to_operand_aliasing={{}: (2, {})} | custom-call | flops 2147483648 | bytes 11010048 | tf_op jit(solution)/shard_map/pallas_call | solution.py:39
  154.7 10.3 %shard_map.64.refs_0_ = bf16[256,2048]{1,0:T(8,128)(2,1)} custom-call(bf16[256,4096]{1,0:T(8,128)(2,1)} %all-gather.11.cloned.1.call-done.x_ref, bf16[4096,2048]{1,0:T(8,128)(2,1)} %bitcast.18, bf16[256,2048]{1,0:T(8,128)(2,1)} %copy-done.2, bf16[256,2048]{1,0:T(8,128)(2,1)} %copy-done.4, bf16[128,2048]{1,0:T(8,128)(2,1)} %copy-done.10, ...), custom_call_target="tpu_custom_call" | custom-call | flops 4294967296 | bytes 19922944 | tf_op jit(solution)/shard_map/pallas_call | solution.py:39
  165.0 1.0 collective-permute-start.19
  166.3 1.0 collective-permute-start.11
  167.8 21.8 %collective-permute-done.19.refs_9_.refs_21_ = bf16[256,2048]{1,0:T(8,128)(2,1)S(1)} collective-permute-done((bf16[256,2048]{1,0:T(8,128)(2,1)}, bf16[256,2048]{1,0:T(8,128)(2,1)S(1)}, u32[]{:S(2)}, u32[]{:S(2)}) %collective-permute-start.19) | collective-permute-done | bytes 1048608 | tf_op jit(solution)/shard_map/ppermute | solution.py:251
  189.6 1.2 collective-permute-start.25
  190.9 1.0 collective-permute-start.26
  195.5 10.0 %shard_map.66.refs_0_ = bf16[256,2048]{1,0:T(8,128)(2,1)} custom-call(bf16[256,4096]{1,0:T(8,128)(2,1)} %all-gather.7.cloned.1.call-done.x_ref, bf16[4096,2048]{1,0:T(8,128)(2,1)} %bitcast.19, bf16[256,2048]{1,0:T(8,128)(2,1)} %copy-done.6, bf16[256,2048]{1,0:T(8,128)(2,1)} %collective-permute-done.6.refs_11_.refs_1_.refs_12_, ...), custom_call_target="tpu_custom_call" | custom-call | flops 4294967296 | bytes 19922944 | tf_op jit(solution)/shard_map/pallas_call | solution.py:39
  205.5 1.8 collective-permute-done.21.refs_1_.refs_23_
  207.7 1.1 collective-permute-start.24
  208.8 1.8 collective-permute-start.28
  211.0 1.6 collective-permute-done.28.refs_28_
  213.2 0.9 copy-done.16
  214.0 10.3 %shard_map.68 = (f32[128,512]{1,0:T(8,128)}, f32[128,512]{1,0:T(8,128)}, f32[128,512]{1,0:T(8,128)}) custom-call(s32[1]{0:T(128)} %bitcast.first_ref, bf16[128,512]{1,0:T(8,128)(2,1)} %slice_select_fusion.1.refs_9_.q_ref, bf16[256,2048]{1,0:T(8,128)(2,1)} %shard_map.56.refs_0_, bf16[256,2048]{1,0:T(8,128)(2,1)} %copy-done.2, bf16[256,2048]{1,0:T(8,128)(2,1)} %copy-done.4, ...), custom_call_target="tpu_custom_call" | custom-call | flops 1610612736 | bytes 12582912 | tf_op jit(solution)/shard_map/pallas_call | solution.py:226
  224.3 6.8 %collective-permute-done.23.refs_1_.refs_31_ = bf16[256,2048]{1,0:T(8,128)(2,1)S(1)} collective-permute-done((bf16[256,2048]{1,0:T(8,128)(2,1)}, bf16[256,2048]{1,0:T(8,128)(2,1)S(1)}, u32[]{:S(2)}, u32[]{:S(2)}) %collective-permute-start.23) | collective-permute-done | bytes 1048608 | tf_op jit(solution)/shard_map/ppermute | solution.py:251
  231.2 0.9 slice.69.refs_0_
  232.1 1.1 collective-permute-start.30
  233.2 1.9 slice.70.refs_0_
  235.4 2.6 collective-permute-start.32
  238.9 5.0 %collective-permute-done.30.refs_3_.refs_33_ = bf16[128,2048]{1,0:T(8,128)(2,1)} collective-permute-done((bf16[128,2048]{1,0:T(8,128)(2,1)}, bf16[128,2048]{1,0:T(8,128)(2,1)}, u32[]{:S(2)}, u32[]{:S(2)}) %collective-permute-start.30) | collective-permute-done | bytes 524320 | tf_op jit(solution)/shard_map/ppermute | solution.py:251
  243.9 2.8 collective-permute-start.35
  246.8 3.0 collective-permute-start.36
  250.3 6.1 %shard_map.72.refs_0_ = bf16[1024,1024]{1,0:T(8,128)(2,1)} custom-call(bf16[256,4096]{1,0:T(8,128)(2,1)} %all-gather.11.cloned.1.call-done.x_ref, bf16[4096,1024]{1,0:T(8,128)(2,1)} %bitcast.22, bf16[1024,1024]{1,0:T(8,128)(2,1)} %shard_map.63.refs_12_.refs_0_, bf16[256,2048]{1,0:T(8,128)(2,1)} %shard_map.65.refs_20_.refs_1_), custom_call_target="tpu_custom_call", output_to_operand_aliasing={{}: (2, {})} | custom-call | flops 2147483648 | bytes 11010048 | tf_op jit(solution)/shard_map/pallas_call | solution.py:39
  256.4 6.1 %shard_map.73.q_ref = bf16[1024,1024]{1,0:T(8,128)(2,1)} custom-call(bf16[256,4096]{1,0:T(8,128)(2,1)} %all-gather.7.cloned.1.call-done.x_ref, bf16[4096,1024]{1,0:T(8,128)(2,1)} %bitcast.23, bf16[1024,1024]{1,0:T(8,128)(2,1)} %shard_map.72.refs_0_, bf16[256,2048]{1,0:T(8,128)(2,1)} %shard_map.67.refs_0_.refs_1_.refs_30_), custom_call_target="tpu_custom_call", output_to_operand_aliasing={{}: (2, {})} | custom-call | flops 2147483648 | bytes 11010048 | tf_op jit(solution)/shard_map/pallas_call | solution.py:39
  262.5 1.0 copy-done.15
  263.7 6.7 %shard_map.71.refs_40_ = bf16[128,512]{1,0:T(8,128)(2,1)} custom-call(s32[1]{0:T(128)} %bitcast.first_ref, bf16[128,512]{1,0:T(8,128)(2,1)} %slice_select_fusion.1.refs_9_.q_ref, bf16[256,2048]{1,0:T(8,128)(2,1)} %shard_map.67.refs_0_.refs_1_.refs_30_, bf16[256,2048]{1,0:T(8,128)(2,1)} %copy-done.12, ...), custom_call_target="tpu_custom_call" | custom-call | flops 536870912 | bytes 4194304 | tf_op jit(solution)/shard_map/pallas_call | solution.py:226
  270.3 1.9 collective-permute-start.37
  272.3 18.5 %shard_map.74 = bf16[1024,1024]{1,0:T(8,128)(2,1)} custom-call(s32[1024]{0:T(1024)} %fusion.4.at_ref, bf16[1024,1024]{1,0:T(8,128)(2,1)} %shard_map.73.q_ref, bf16[256,2048]{1,0:T(8,128)(2,1)} %shard_map.56.refs_0_, bf16[256,2048]{1,0:T(8,128)(2,1)} %copy-done.2, bf16[256,2048]{1,0:T(8,128)(2,1)} %copy-done.4, bf16[128,2048]{1,0:T(8,128)(2,1)} %copy-done.10, ...), custom_call_target="tpu_custom_call" | custom-call | flops 2147483648 | bytes 37748736 | tf_op jit(solution)/shard_map/pallas_call | solution.py:140
  290.8 1.6 slice_bitcast_fusion
  293.3 1.0 fusion
  294.4 1.5 pad_maximum_fusion
  (118 shorter events, 12.3 us)
Async XLA Ops:
  6.5 50.4 %all-gather.5.cloned.1.call-start = ((), (), s32[]{:S(2)}) async-start(), calls=%async_computation | async-start | bytes 2621440 | tf_op jit(solution)/shard_map/all_gather | solution.py:317
  8.4 94.8 %all-gather.9.cloned.1.call-start = ((), (), s32[]{:S(2)}) async-start(), calls=%async_computation.2 | async-start | bytes 2621440 | tf_op jit(solution)/shard_map/all_gather | solution.py:317
  8.5 5.8 %slice-start = ((bf16[4096,8,384]{2,1,0:T(8,128)(2,1)}), bf16[4096,8,256]{2,1,0:T(8,128)(2,1)S(1)}, s32[]{:S(2)}) async-start(bf16[4096,8,384]{2,1,0:T(8,128)(2,1)} %param.6), calls=%async_computation.4 | async-start | bytes 33554432 | tf_op jit(solution)/shard_map/slice | solution.py:331
  26.0 128.7 %all-gather.11.cloned.1.call-start = ((), (), s32[]{:S(2)}) async-start(), calls=%async_computation.3 | async-start | bytes 2621440 | tf_op jit(solution)/shard_map/all_gather | solution.py:317
  27.9 167.6 %all-gather.7.cloned.1.call-start = ((), (), s32[]{:S(2)}) async-start(), calls=%async_computation.1 | async-start | bytes 2621440 | tf_op jit(solution)/shard_map/all_gather | solution.py:317
  67.1 24.2 %collective-permute-start.1 = (bf16[256,2048]{1,0:T(8,128)(2,1)}, bf16[256,2048]{1,0:T(8,128)(2,1)S(1)}, u32[]{:S(2)}, u32[]{:S(2)}) collective-permute-start(bf16[256,2048]{1,0:T(8,128)(2,1)} %shard_map.56.refs_0_), channel_id=1, source_target_pairs={{0,8},{4,12},{8,0},{12,4},{16,24},{20,28},{24,16},{28,20},{1,9},{5... | collective-permute-start | bytes 3145736 | tf_op jit(solution)/shard_map/ppermute | solution.py:251
  68.2 25.1 %collective-permute-start.2 = (bf16[256,2048]{1,0:T(8,128)(2,1)}, bf16[256,2048]{1,0:T(8,128)(2,1)S(1)}, u32[]{:S(2)}, u32[]{:S(2)}) collective-permute-start(bf16[256,2048]{1,0:T(8,128)(2,1)} %shard_map.56.refs_0_), channel_id=1, source_target_pairs={{0,16},{4,20},{8,24},{12,28},{16,0},{20,4},{24,8},{28,12},{1,17},{... | collective-permute-start | bytes 3145736 | tf_op jit(solution)/shard_map/ppermute | solution.py:251
  91.2 10.2 %copy-start.2 = (bf16[256,2048]{1,0:T(8,128)(2,1)}, bf16[256,2048]{1,0:T(8,128)(2,1)S(1)}, u32[]{:S(2)}) copy-start(bf16[256,2048]{1,0:T(8,128)(2,1)S(1)} %collective-permute-done.1.refs_0_.refs_1_) | copy-start | bytes 3145732
  92.1 21.2 %collective-permute-start.3 = (bf16[128,2048]{1,0:T(8,128)(2,1)}, bf16[128,2048]{1,0:T(8,128)(2,1)S(1)}, u32[]{:S(2)}, u32[]{:S(2)}) collective-permute-start(bf16[128,2048]{1,0:T(8,128)(2,1)} %slice.63), channel_id=1, source_target_pairs={{0,16},{4,20},{8,24},{12,28},{16,0},{20,4},{24,8},{28,12},{1,17},{... | collective-permute-start | bytes 1572872 | tf_op jit(solution)/shard_map/ppermute | solution.py:251
  93.3 8.1 %copy-start.4 = (bf16[256,2048]{1,0:T(8,128)(2,1)}, bf16[256,2048]{1,0:T(8,128)(2,1)S(1)}, u32[]{:S(2)}) copy-start(bf16[256,2048]{1,0:T(8,128)(2,1)S(1)} %collective-permute-done.2.refs_1_.refs_2_) | copy-start | bytes 3145732
  94.2 19.1 %collective-permute-start.4 = (bf16[128,2048]{1,0:T(8,128)(2,1)}, bf16[128,2048]{1,0:T(8,128)(2,1)S(1)}, u32[]{:S(2)}, u32[]{:S(2)}) collective-permute-start(bf16[128,2048]{1,0:T(8,128)(2,1)} %slice.64), channel_id=1, source_target_pairs={{0,8},{4,12},{8,0},{12,4},{16,24},{20,28},{24,16},{28,20},{1,9},{5... | collective-permute-start | bytes 1572872 | tf_op jit(solution)/shard_map/ppermute | solution.py:251
  114.1 0.8 copy-start.11
  115.0 8.0 %copy-start.3 = (bf16[256,2048]{1,0:T(8,128)(2,1)S(1)}, bf16[256,2048]{1,0:T(8,128)(2,1)}, u32[]{:S(2)}) copy-start(bf16[256,2048]{1,0:T(8,128)(2,1)} %copy-done.2) | copy-start | bytes 3145732
  115.0 9.8 %copy-start.5 = (bf16[256,2048]{1,0:T(8,128)(2,1)S(1)}, bf16[256,2048]{1,0:T(8,128)(2,1)}, u32[]{:S(2)}) copy-start(bf16[256,2048]{1,0:T(8,128)(2,1)} %copy-done.4) | copy-start | bytes 3145732
  115.0 24.2 %collective-permute-start.5 = (bf16[256,2048]{1,0:T(8,128)(2,1)}, bf16[256,2048]{1,0:T(8,128)(2,1)S(1)}, u32[]{:S(2)}, u32[]{:S(2)}) collective-permute-start(bf16[256,2048]{1,0:T(8,128)(2,1)} %shard_map.61.refs_1_.refs_10_), channel_id=1, source_target_pairs={{0,8},{4,12},{8,0},{12,4},{16,24},{20,28},{24,16},{28,20},{1,9},{5... | collective-permute-start | bytes 3145736 | tf_op jit(solution)/shard_map/ppermute | solution.py:251
  116.1 24.6 %collective-permute-start.6 = (bf16[256,2048]{1,0:T(8,128)(2,1)}, bf16[256,2048]{1,0:T(8,128)(2,1)}, u32[]{:S(2)}, u32[]{:S(2)}) collective-permute-start(bf16[256,2048]{1,0:T(8,128)(2,1)} %shard_map.61.refs_1_.refs_10_), channel_id=1, source_target_pairs={{0,16},{4,20},{8,24},{12,28},{16,0},{20,4},{24,8},{28,12},{1,17},{... | collective-permute-start | bytes 3145736 | tf_op jit(solution)/shard_map/ppermute | solution.py:251
  119.2 27.1 %collective-permute-start.14 = (bf16[256,2048]{1,0:T(8,128)(2,1)}, bf16[256,2048]{1,0:T(8,128)(2,1)}, u32[]{:S(2)}, u32[]{:S(2)}) collective-permute-start(bf16[256,2048]{1,0:T(8,128)(2,1)} %shard_map.56.refs_0_), channel_id=1, source_target_pairs={{0,4},{4,0},{8,12},{12,8},{16,20},{20,16},{24,28},{28,24},{1,5},{5... | collective-permute-start | bytes 3145736 | tf_op jit(solution)/shard_map/ppermute | solution.py:251
  121.5 3.2 %collective-permute-start = (bf16[128,512]{1,0:T(8,128)(2,1)S(1)}, bf16[128,512]{1,0:T(8,128)(2,1)S(1)}, u32[]{:S(2)}, u32[]{:S(2)}) collective-permute-start(bf16[128,512]{1,0:T(8,128)(2,1)S(1)} %slice.61), channel_id=1, source_target_pairs={{0,4},{1,5},{2,6},{3,7}} | collective-permute-start | bytes 393224 | tf_op jit(solution)/shard_map/ppermute | solution.py:386
  123.0 31.6 %collective-permute-start.15 = (bf16[256,2048]{1,0:T(8,128)(2,1)S(1)}, bf16[256,2048]{1,0:T(8,128)(2,1)}, u32[]{:S(2)}, u32[]{:S(2)}) collective-permute-start(bf16[256,2048]{1,0:T(8,128)(2,1)S(1)} %copy-done.3), channel_id=1, source_target_pairs={{0,4},{4,0},{8,12},{12,8},{16,20},{20,16},{24,28},{28,24},{1,5},{5... | collective-permute-start | bytes 3145736 | tf_op jit(solution)/shard_map/ppermute | solution.py:251
  124.8 30.0 %collective-permute-start.16 = (bf16[256,2048]{1,0:T(8,128)(2,1)S(1)}, bf16[256,2048]{1,0:T(8,128)(2,1)}, u32[]{:S(2)}, u32[]{:S(2)}) collective-permute-start(bf16[256,2048]{1,0:T(8,128)(2,1)S(1)} %copy-done.5), channel_id=1, source_target_pairs={{0,4},{4,0},{8,12},{12,8},{16,20},{20,16},{24,28},{28,24},{1,5},{5... | collective-permute-start | bytes 3145736 | tf_op jit(solution)/shard_map/ppermute | solution.py:251
  139.2 5.3 %copy-start.6 = (bf16[256,2048]{1,0:T(8,128)(2,1)}, bf16[256,2048]{1,0:T(8,128)(2,1)S(1)}, u32[]{:S(2)}) copy-start(bf16[256,2048]{1,0:T(8,128)(2,1)S(1)} %collective-permute-done.5.refs_10_.refs_0_.refs_11_) | copy-start | bytes 3145732
  139.2 8.3 %collective-permute-start.17 = (bf16[128,2048]{1,0:T(8,128)(2,1)}, bf16[128,2048]{1,0:T(8,128)(2,1)}, u32[]{:S(2)}, u32[]{:S(2)}) collective-permute-start(bf16[128,2048]{1,0:T(8,128)(2,1)} %copy-done.10), channel_id=1, source_target_pairs={{0,4},{4,0},{8,12},{12,8},{16,20},{20,16},{24,28},{28,24},{1,5},{5... | collective-permute-start | bytes 1572872 | tf_op jit(solution)/shard_map/ppermute | solution.py:251
  140.8 13.1 %collective-permute-start.18 = (bf16[128,2048]{1,0:T(8,128)(2,1)}, bf16[128,2048]{1,0:T(8,128)(2,1)}, u32[]{:S(2)}, u32[]{:S(2)}) collective-permute-start(bf16[128,2048]{1,0:T(8,128)(2,1)} %copy-done.11), channel_id=1, source_target_pairs={{0,4},{4,0},{8,12},{12,8},{16,20},{20,16},{24,28},{28,24},{1,5},{5... | collective-permute-start | bytes 1572872 | tf_op jit(solution)/shard_map/ppermute | solution.py:251
  146.3 7.6 %copy-start.1 = (bf16[256,2048]{1,0:T(8,128)(2,1)S(1)}, bf16[256,2048]{1,0:T(8,128)(2,1)}, u32[]{:S(2)}) copy-start(bf16[256,2048]{1,0:T(8,128)(2,1)} %shard_map.61.refs_1_.refs_10_) | copy-start | bytes 3145732
  146.3 18.7 %collective-permute-start.7 = (bf16[128,2048]{1,0:T(8,128)(2,1)}, bf16[128,2048]{1,0:T(8,128)(2,1)}, u32[]{:S(2)}, u32[]{:S(2)}) collective-permute-start(bf16[128,2048]{1,0:T(8,128)(2,1)} %slice.65), channel_id=1, source_target_pairs={{0,16},{4,20},{8,24},{12,28},{16,0},{20,4},{24,8},{28,12},{1,17},{... | collective-permute-start | bytes 1572872 | tf_op jit(solution)/shard_map/ppermute | solution.py:251
  147.5 17.5 %collective-permute-start.8 = (bf16[128,2048]{1,0:T(8,128)(2,1)}, bf16[128,2048]{1,0:T(8,128)(2,1)}, u32[]{:S(2)}, u32[]{:S(2)}) collective-permute-start(bf16[128,2048]{1,0:T(8,128)(2,1)} %slice.66), channel_id=1, source_target_pairs={{0,8},{4,12},{8,0},{12,4},{16,24},{20,28},{24,16},{28,20},{1,9},{5... | collective-permute-start | bytes 1572872 | tf_op jit(solution)/shard_map/ppermute | solution.py:251
  153.9 13.4 %collective-permute-start.9 = (bf16[256,2048]{1,0:T(8,128)(2,1)S(1)}, bf16[256,2048]{1,0:T(8,128)(2,1)}, u32[]{:S(2)}, u32[]{:S(2)}) collective-permute-start(bf16[256,2048]{1,0:T(8,128)(2,1)S(1)} %copy-done.1), channel_id=1, source_target_pairs={{0,4},{4,0},{8,12},{12,8},{16,20},{20,16},{24,28},{28,24},{1,5},{5... | collective-permute-start | bytes 3145736 | tf_op jit(solution)/shard_map/ppermute | solution.py:251
  154.6 12.7 %collective-permute-start.10 = (bf16[256,2048]{1,0:T(8,128)(2,1)}, bf16[256,2048]{1,0:T(8,128)(2,1)}, u32[]{:S(2)}, u32[]{:S(2)}) collective-permute-start(bf16[256,2048]{1,0:T(8,128)(2,1)} %copy-done.6), channel_id=1, source_target_pairs={{0,4},{4,0},{8,12},{12,8},{16,20},{20,16},{24,28},{28,24},{1,5},{5... | collective-permute-start | bytes 3145736 | tf_op jit(solution)/shard_map/ppermute | solution.py:251
  165.0 24.6 %collective-permute-start.19 = (bf16[256,2048]{1,0:T(8,128)(2,1)}, bf16[256,2048]{1,0:T(8,128)(2,1)S(1)}, u32[]{:S(2)}, u32[]{:S(2)}) collective-permute-start(bf16[256,2048]{1,0:T(8,128)(2,1)} %shard_map.65.refs_20_.refs_1_), channel_id=1, source_target_pairs={{0,8},{4,12},{8,0},{12,4},{16,24},{20,28},{24,16},{28,20},{1,9},{5... | collective-permute-start | bytes 3145736 | tf_op jit(solution)/shard_map/ppermute | solution.py:251
  166.1 24.8 %collective-permute-start.20 = (bf16[256,2048]{1,0:T(8,128)(2,1)}, bf16[256,2048]{1,0:T(8,128)(2,1)S(1)}, u32[]{:S(2)}, u32[]{:S(2)}) collective-permute-start(bf16[256,2048]{1,0:T(8,128)(2,1)} %shard_map.65.refs_20_.refs_1_), channel_id=1, source_target_pairs={{0,16},{4,20},{8,24},{12,28},{16,0},{20,4},{24,8},{28,12},{1,17},{... | collective-permute-start | bytes 3145736 | tf_op jit(solution)/shard_map/ppermute | solution.py:251
  166.3 27.2 %collective-permute-start.11 = (bf16[256,2048]{1,0:T(8,128)(2,1)}, bf16[256,2048]{1,0:T(8,128)(2,1)S(1)}, u32[]{:S(2)}, u32[]{:S(2)}) collective-permute-start(bf16[256,2048]{1,0:T(8,128)(2,1)} %collective-permute-done.6.refs_11_.refs_1_.refs_12_), channel_id=1, source_target_pairs={{0,4},{4,0},{8,12},{12,8},{16,20},{20,16},{24,28},{28,24},{1,5},{5... | collective-permute-start | bytes 3145736 | tf_op jit(solution)/shard_map/ppermute | solution.py:251
  167.3 26.5 %collective-permute-start.12 = (bf16[128,2048]{1,0:T(8,128)(2,1)}, bf16[128,2048]{1,0:T(8,128)(2,1)S(1)}, u32[]{:S(2)}, u32[]{:S(2)}) collective-permute-start(bf16[128,2048]{1,0:T(8,128)(2,1)} %collective-permute-done.7.refs_1_.refs_2_.refs_13_), channel_id=1, source_target_pairs={{0,4},{4,0},{8,12},{12,8},{16,20},{20,16},{24,28},{28,24},{1,5},{5... | collective-permute-start | bytes 1572872 | tf_op jit(solution)/shard_map/ppermute | solution.py:251
  167.3 27.2 %collective-permute-start.13 = (bf16[128,2048]{1,0:T(8,128)(2,1)}, bf16[128,2048]{1,0:T(8,128)(2,1)S(1)}, u32[]{:S(2)}, u32[]{:S(2)}) collective-permute-start(bf16[128,2048]{1,0:T(8,128)(2,1)} %collective-permute-done.8.refs_2_.refs_3_.refs_14_), channel_id=1, source_target_pairs={{0,4},{4,0},{8,12},{12,8},{16,20},{20,16},{24,28},{28,24},{1,5},{5... | collective-permute-start | bytes 1572872 | tf_op jit(solution)/shard_map/ppermute | solution.py:251
  189.6 5.9 %copy-start.7 = (bf16[256,2048]{1,0:T(8,128)(2,1)}, bf16[256,2048]{1,0:T(8,128)(2,1)S(1)}, u32[]{:S(2)}) copy-start(bf16[256,2048]{1,0:T(8,128)(2,1)S(1)} %collective-permute-done.19.refs_9_.refs_21_) | copy-start | bytes 3145732
  189.6 19.2 %collective-permute-start.25 = (bf16[256,2048]{1,0:T(8,128)(2,1)}, bf16[256,2048]{1,0:T(8,128)(2,1)}, u32[]{:S(2)}, u32[]{:S(2)}) collective-permute-start(bf16[256,2048]{1,0:T(8,128)(2,1)} %shard_map.65.refs_20_.refs_1_), channel_id=1, source_target_pairs={{0,4},{4,0},{8,12},{12,8},{16,20},{20,16},{24,28},{28,24},{1,5},{5... | collective-permute-start | bytes 3145736 | tf_op jit(solution)/shard_map/ppermute | solution.py:251
  190.9 4.6 %copy-start.8 = (bf16[256,2048]{1,0:T(8,128)(2,1)}, bf16[256,2048]{1,0:T(8,128)(2,1)S(1)}, u32[]{:S(2)}) copy-start(bf16[256,2048]{1,0:T(8,128)(2,1)S(1)} %collective-permute-done.20.refs_10_.refs_22_) | copy-start | bytes 3145732
  190.9 19.8 %collective-permute-start.26 = (bf16[256,2048]{1,0:T(8,128)(2,1)S(1)}, bf16[256,2048]{1,0:T(8,128)(2,1)}, u32[]{:S(2)}, u32[]{:S(2)}) collective-permute-start(bf16[256,2048]{1,0:T(8,128)(2,1)S(1)} %collective-permute-done.19.refs_9_.refs_21_), channel_id=1, source_target_pairs={{0,4},{4,0},{8,12},{12,8},{16,20},{20,16},{24,28},{28,24},{1,5},{5... | collective-permute-start | bytes 3145736 | tf_op jit(solution)/shard_map/ppermute | solution.py:251
  193.5 1.0 copy-start.9
  193.5 13.8 %collective-permute-start.21 = (bf16[128,2048]{1,0:T(8,128)(2,1)}, bf16[128,2048]{1,0:T(8,128)(2,1)}, u32[]{:S(2)}, u32[]{:S(2)}) collective-permute-start(bf16[128,2048]{1,0:T(8,128)(2,1)} %slice.67), channel_id=1, source_target_pairs={{0,16},{4,20},{8,24},{12,28},{16,0},{20,4},{24,8},{28,12},{1,17},{... | collective-permute-start | bytes 1572872 | tf_op jit(solution)/shard_map/ppermute | solution.py:251
  193.7 1.8 copy-start.13
  193.8 13.6 %collective-permute-start.22 = (bf16[128,2048]{1,0:T(8,128)(2,1)}, bf16[128,2048]{1,0:T(8,128)(2,1)}, u32[]{:S(2)}, u32[]{:S(2)}) collective-permute-start(bf16[128,2048]{1,0:T(8,128)(2,1)} %slice.68), channel_id=1, source_target_pairs={{0,8},{4,12},{8,0},{12,4},{16,24},{20,28},{24,16},{28,20},{1,9},{5... | collective-permute-start | bytes 1572872 | tf_op jit(solution)/shard_map/ppermute | solution.py:251
  194.5 1.0 copy-start.14
  194.5 16.5 %collective-permute-start.27 = (bf16[256,2048]{1,0:T(8,128)(2,1)S(1)}, bf16[256,2048]{1,0:T(8,128)(2,1)}, u32[]{:S(2)}, u32[]{:S(2)}) collective-permute-start(bf16[256,2048]{1,0:T(8,128)(2,1)S(1)} %collective-permute-done.20.refs_10_.refs_22_), channel_id=1, source_target_pairs={{0,4},{4,0},{8,12},{12,8},{16,20},{20,16},{24,28},{28,24},{1,5},{5... | collective-permute-start | bytes 3145736 | tf_op jit(solution)/shard_map/ppermute | solution.py:251
  205.5 5.2 %copy-start.19 = (s32[8,128,3]{1,0,2:T(8,128)S(1)}, s32[8,128,3]{1,0,2:T(8,128)}, u32[]{:S(2)}) copy-start(s32[8,128,3]{1,0,2:T(8,128)} %param.8) | copy-start | bytes 36868
  205.5 5.2 %copy-start.20 = (s32[8,128,3]{1,0,2:T(8,128)S(1)}, s32[8,128,3]{1,0,2:T(8,128)}, u32[]{:S(2)}) copy-start(s32[8,128,3]{1,0,2:T(8,128)} %param.7) | copy-start | bytes 36868
  207.3 23.9 %collective-permute-start.23 = (bf16[256,2048]{1,0:T(8,128)(2,1)}, bf16[256,2048]{1,0:T(8,128)(2,1)S(1)}, u32[]{:S(2)}, u32[]{:S(2)}) collective-permute-start(bf16[256,2048]{1,0:T(8,128)(2,1)} %shard_map.67.refs_0_.refs_1_.refs_30_), channel_id=1, source_target_pairs={{0,8},{4,12},{8,0},{12,4},{16,24},{20,28},{24,16},{28,20},{1,9},{5... | collective-permute-start | bytes 3145736 | tf_op jit(solution)/shard_map/ppermute | solution.py:251
  207.7 25.5 %collective-permute-start.24 = (bf16[256,2048]{1,0:T(8,128)(2,1)}, bf16[256,2048]{1,0:T(8,128)(2,1)}, u32[]{:S(2)}, u32[]{:S(2)}) collective-permute-start(bf16[256,2048]{1,0:T(8,128)(2,1)} %shard_map.67.refs_0_.refs_1_.refs_30_), channel_id=1, source_target_pairs={{0,16},{4,20},{8,24},{12,28},{16,0},{20,4},{24,8},{28,12},{1,17},{... | collective-permute-start | bytes 3145736 | tf_op jit(solution)/shard_map/ppermute | solution.py:251
  208.8 3.7 %collective-permute-start.28 = (bf16[128,2048]{1,0:T(8,128)(2,1)}, bf16[128,2048]{1,0:T(8,128)(2,1)}, u32[]{:S(2)}, u32[]{:S(2)}) collective-permute-start(bf16[128,2048]{1,0:T(8,128)(2,1)} %collective-permute-done.21.refs_1_.refs_23_), channel_id=1, source_target_pairs={{0,4},{4,0},{8,12},{12,8},{16,20},{20,16},{24,28},{28,24},{1,5},{5... | collective-permute-start | bytes 1572872 | tf_op jit(solution)/shard_map/ppermute | solution.py:251
  210.7 2.5 collective-permute-start.29
  213.2 0.9 copy-start.16
  231.2 6.8 %copy-start.12 = (bf16[256,2048]{1,0:T(8,128)(2,1)}, bf16[256,2048]{1,0:T(8,128)(2,1)S(1)}, u32[]{:S(2)}) copy-start(bf16[256,2048]{1,0:T(8,128)(2,1)S(1)} %collective-permute-done.23.refs_1_.refs_31_) | copy-start | bytes 3145732
  232.1 3.3 %copy-start = (bf16[256,2048]{1,0:T(8,128)(2,1)S(1)}, bf16[256,2048]{1,0:T(8,128)(2,1)}, u32[]{:S(2)}) copy-start(bf16[256,2048]{1,0:T(8,128)(2,1)} %shard_map.67.refs_0_.refs_1_.refs_30_) | copy-start | bytes 3145732
  232.1 6.4 %copy-start.21 = (s32[3]{0:T(128)S(1)}, s32[3]{0:T(128)}, u32[]{:S(2)}) copy-start(s32[3]{0:T(128)} %constant.58.clone) | copy-start | bytes 40
  232.1 11.8 %collective-permute-start.30 = (bf16[128,2048]{1,0:T(8,128)(2,1)}, bf16[128,2048]{1,0:T(8,128)(2,1)}, u32[]{:S(2)}, u32[]{:S(2)}) collective-permute-start(bf16[128,2048]{1,0:T(8,128)(2,1)} %shard_map.69), channel_id=1, source_target_pairs={{0,16},{4,20},{8,24},{12,28},{16,0},{20,4},{24,8},{28,12},{1,17},{... | collective-permute-start | bytes 1572872 | tf_op jit(solution)/shard_map/ppermute | solution.py:251
  235.1 11.7 %collective-permute-start.31 = (bf16[128,2048]{1,0:T(8,128)(2,1)}, bf16[128,2048]{1,0:T(8,128)(2,1)}, u32[]{:S(2)}, u32[]{:S(2)}) collective-permute-start(bf16[128,2048]{1,0:T(8,128)(2,1)} %shard_map.70), channel_id=1, source_target_pairs={{0,8},{4,12},{8,0},{12,4},{16,24},{20,28},{24,16},{28,20},{1,9},{5... | collective-permute-start | bytes 1572872 | tf_op jit(solution)/shard_map/ppermute | solution.py:251
  235.4 27.1 %collective-permute-start.32 = (bf16[256,2048]{1,0:T(8,128)(2,1)S(1)}, bf16[256,2048]{1,0:T(8,128)(2,1)S(1)}, u32[]{:S(2)}, u32[]{:S(2)}) collective-permute-start(bf16[256,2048]{1,0:T(8,128)(2,1)S(1)} %copy-done), channel_id=1, source_target_pairs={{0,4},{4,0},{8,12},{12,8},{16,20},{20,16},{24,28},{28,24},{1,5},{5... | collective-permute-start | bytes 3145736 | tf_op jit(solution)/shard_map/ppermute | solution.py:251
  238.0 24.5 %collective-permute-start.33 = (bf16[256,2048]{1,0:T(8,128)(2,1)S(1)}, bf16[256,2048]{1,0:T(8,128)(2,1)}, u32[]{:S(2)}, u32[]{:S(2)}) collective-permute-start(bf16[256,2048]{1,0:T(8,128)(2,1)S(1)} %collective-permute-done.23.refs_1_.refs_31_), channel_id=1, source_target_pairs={{0,4},{4,0},{8,12},{12,8},{16,20},{20,16},{24,28},{28,24},{1,5},{5... | collective-permute-start | bytes 3145736 | tf_op jit(solution)/shard_map/ppermute | solution.py:251
  238.1 24.4 %collective-permute-start.34 = (bf16[256,2048]{1,0:T(8,128)(2,1)}, bf16[256,2048]{1,0:T(8,128)(2,1)}, u32[]{:S(2)}, u32[]{:S(2)}) collective-permute-start(bf16[256,2048]{1,0:T(8,128)(2,1)} %collective-permute-done.24.refs_2_.refs_32_), channel_id=1, source_target_pairs={{0,4},{4,0},{8,12},{12,8},{16,20},{20,16},{24,28},{28,24},{1,5},{5... | collective-permute-start | bytes 3145736 | tf_op jit(solution)/shard_map/ppermute | solution.py:251
  243.9 18.6 %collective-permute-start.35 = (bf16[128,2048]{1,0:T(8,128)(2,1)}, bf16[128,2048]{1,0:T(8,128)(2,1)S(1)}, u32[]{:S(2)}, u32[]{:S(2)}) collective-permute-start(bf16[128,2048]{1,0:T(8,128)(2,1)} %collective-permute-done.30.refs_3_.refs_33_), channel_id=1, source_target_pairs={{0,4},{4,0},{8,12},{12,8},{16,20},{20,16},{24,28},{28,24},{1,5},{5... | collective-permute-start | bytes 1572872 | tf_op jit(solution)/shard_map/ppermute | solution.py:251
  246.8 15.8 %collective-permute-start.36 = (bf16[128,2048]{1,0:T(8,128)(2,1)}, bf16[128,2048]{1,0:T(8,128)(2,1)}, u32[]{:S(2)}, u32[]{:S(2)}) collective-permute-start(bf16[128,2048]{1,0:T(8,128)(2,1)} %collective-permute-done.31.refs_4_.refs_34_), channel_id=1, source_target_pairs={{0,4},{4,0},{8,12},{12,8},{16,20},{20,16},{24,28},{28,24},{1,5},{5... | collective-permute-start | bytes 1572872 | tf_op jit(solution)/shard_map/ppermute | solution.py:251
  262.5 1.0 copy-start.15
  262.5 1.1 copy-start.17
  270.3 22.7 %collective-permute-start.37 = (bf16[128,512]{1,0:T(8,128)(2,1)}, bf16[128,512]{1,0:T(8,128)(2,1)S(1)}, u32[]{:S(2)}, u32[]{:S(2)}) collective-permute-start(bf16[128,512]{1,0:T(8,128)(2,1)} %shard_map.71.refs_40_), channel_id=1, source_target_pairs={{4,0},{5,1},{6,2},{7,3}} | collective-permute-start | bytes 393224 | tf_op jit(solution)/shard_map/ppermute | solution.py:395
  292.4 0.9 copy-start.18
  (1 other events, 0.8 us)
Sparse Core Ops, SparseCore 0:
  8.9 47.9 all-gather.4
  58.5 44.6 all-gather.8
  104.8 44.6 all-gather.10
  150.9 44.5 all-gather.6
